TPU v7x, 256 devices: a whole 4x4x8 slice. The times are simulated.
256 devices in a mesh: con: 8 (over y, x_hi), var: 32 (over x_lo, z, core).
Axes of the slice: x: 4 (x_hi: 2, x_lo: 2; x = x_hi * 2 + x_lo), y: 4, z: 8, core: 2. Of those that a mesh axis runs over, the one named last changes fastest.
Arguments:
- tiles: float32 [8, 32, 72, 128, 128], P('con', 'var'), may hold values from -0.25 to 0.25
- row_tile: int32 [8, 32, 72], P('con', 'var'), may hold values from 0 to 511, as said below
- col_tile: int32 [8, 32, 72], P('con', 'var'), may hold values from 0 to 31
- diag_cost: float32 [131072], P('var'), may hold values from 0.1 to 2
- linear_cost: float32 [8, 131072], P(None, 'var'), may hold values from -6 to 6
- bound_center: float32 [8, 524288], P(None, ('con', 'var')), may hold values from -6 to 6
- bound_width: float32 [8, 524288], P(None, ('con', 'var')), may hold values from 0.05 to 1
- rho_level: int32 [524288], P(('con', 'var')), may hold values from 0 to 3
- sigma_level: int32 [8], replicated, may hold values from 0 to 3
- state_x: float32 [8, 131072], P(None, 'var'), may hold values from -6 to 6
- state_w: float32 [8, 524288], P(None, ('con', 'var')), may hold values from -6 to 6
- prev_x: float32 [8, 131072], P(None, 'var'), may hold values from -6 to 6
- prev_w: float32 [8, 524288], P(None, ('con', 'var')), may hold values from -6 to 6
- prev_gx: float32 [8, 131072], P(None, 'var'), may hold values from -6 to 6
- prev_gw: float32 [8, 524288], P(None, ('con', 'var')), may hold values from -6 to 6
- hist_sx: float32 [8, 8, 131072], P(None, None, 'var'), may hold values from -6 to 6
- hist_sw: float32 [8, 8, 524288], P(None, None, ('con', 'var')), may hold values from -6 to 6
- hist_gx: float32 [8, 8, 131072], P(None, None, 'var'), may hold values from -6 to 6
- hist_gw: float32 [8, 8, 524288], P(None, None, ('con', 'var')), may hold values from -6 to 6
- slot_order: int32 [8], replicated, may hold values from 0 to 7, each once
Outputs:
- next_x: float32 [8, 131072], P(None, 'var')
- next_w: float32 [8, 524288], P(None, ('con', 'var'))
Inputs may be any that keep to these rules, and one draw needn't show every extreme that they name: `row_tile`: split each constraint block's block rows into 32 runs of 524288 / (128 * 8 * 32) consecutive block rows. Among the 72 blocks (c, v, t) of one pair (c, v), at most ceil(72 / 32) lie in the block rows of one run, and some run holds exactly that many. `slot_order`: a permutation of the 8 slots.
All inputs are finite; a program needn't handle non-finite values.
Results may differ from a plain program's by a relative error of at most 0.0003.
Values sent between devices are 32-bit elements; how exact they have to be, the bound alone decides.
No kernel may reach another device: no remote copies, remote signals or barrier semaphores. Data moves between devices by JAX's collectives and lax.ppermute only.
A program may use at most 64 MiB of HBM per device.

v0:
```python
import jax
import jax.numpy as jnp
from jax import lax
from jax.sharding import PartitionSpec as P

STEPS = 2


highest = lax.Precision.HIGHEST
relax = 1.6
ridge = 0.01


def solve_small(system, rhs):
    lower = jnp.linalg.cholesky(system)
    first = jax.scipy.linalg.solve_triangular(lower, rhs[:, :, None], lower=True)
    return jax.scipy.linalg.solve_triangular(lower, first, trans=1, lower=True)[:, :, 0]


def per_device(
    tiles,
    row_tile,
    col_tile,
    diag_cost,
    linear_cost,
    bound_center,
    bound_width,
    rho_level,
    sigma_level,
    state_x,
    state_w,
    prev_x,
    prev_w,
    prev_gx,
    prev_gw,
    hist_sx,
    hist_sw,
    hist_gx,
    hist_gw,
    slot_order,
):
    problems = state_x.shape[0]
    tile_size = tiles.shape[-1]
    var_cols = state_x.shape[1]
    memory = hist_sx.shape[0]
    var_count = lax.axis_size("var")
    col_count = var_cols // tile_size
    run_length = state_w.shape[1] // tile_size
    row_count = run_length * var_count
    blocks = tiles.reshape(-1, tile_size, tile_size)
    rows_here = row_tile.reshape(-1)
    cols_here = col_tile.reshape(-1)
    col_onehot = (jnp.arange(col_count, dtype=jnp.int32)[:, None] == cols_here[None, :]).astype(
        jnp.float32
    )
    leader = (lax.axis_index("con") == 0).astype(jnp.float32)
    rho = 0.4 * (1.0 + rho_level.astype(jnp.float32))
    sigma = 0.2 * (1.0 + sigma_level.astype(jnp.float32))[:, None]
    lower_bound = bound_center - bound_width
    upper_bound = bound_center + bound_width
    row_onehot = (jnp.arange(row_count, dtype=jnp.int32)[:, None] == rows_here[None, :]).astype(
        jnp.float32
    )

    def forward(vector):
        pieces = jnp.take(vector.reshape(problems, col_count, tile_size), cols_here, axis=1)
        contrib = jnp.einsum("ktj,tij->kti", pieces, blocks, precision=highest)
        panel = jnp.einsum("rt,kti->kri", row_onehot, contrib, precision=highest).reshape(
            problems, row_count * tile_size
        )
        return lax.psum_scatter(panel, "var", scatter_dimension=1, tiled=True)

    def backward(vector):
        panel = lax.all_gather(vector, "var", axis=1, tiled=True)
        pieces = jnp.take(panel.reshape(problems, row_count, tile_size), rows_here, axis=1)
        contrib = jnp.einsum("kti,tij->ktj", pieces, blocks, precision=highest)
        partial_sum = jnp.einsum("ct,ktj->kcj", col_onehot, contrib, precision=highest).reshape(
            problems, var_cols
        )
        return lax.psum(partial_sum, "con")

    identity = jnp.eye(memory, dtype=jnp.float32)
    state_a, state_b = (state_x, state_w)
    for step_index in range(STEPS):
        slack = jnp.clip(state_b, lower_bound, upper_bound)
        dual = rho * (state_b - slack)
        image_start = forward(state_a)
        resid = -linear_cost - diag_cost * state_a + backward(rho * (slack - image_start) - dual)
        res_norm = lax.psum(jnp.sum(resid * resid, axis=1), "var")
        trial = state_a
        tracked = image_start
        image = forward(resid)
        curved = (diag_cost + sigma) * resid + backward(rho * image)
        curve_total = lax.psum(jnp.sum(resid * curved, axis=1), "var")
        step_len = res_norm / curve_total
        trial = trial + step_len[:, None] * resid
        tracked = tracked + step_len[:, None] * image
        trial_image = forward(trial)
        primal_next = relax * trial + (1.0 - relax) * state_a
        shifted_next = relax * trial_image + (1.0 - relax) * slack + (state_b - slack)
        resid_a = primal_next - state_a
        resid_b = shifted_next - state_b
        chosen = (jnp.arange(memory, dtype=jnp.int32) == slot_order[step_index])[:, None, None]
        hist_sx = jnp.where(chosen, (state_a - prev_x)[None], hist_sx)
        hist_sw = jnp.where(chosen, (state_b - prev_w)[None], hist_sw)
        hist_gx = jnp.where(chosen, (resid_a - prev_gx)[None], hist_gx)
        hist_gw = jnp.where(chosen, (resid_b - prev_gw)[None], hist_gw)
        gram_part = leader * jnp.einsum(
            "mkn,pkn->kmp", hist_gx, hist_gx, precision=highest
        ) + jnp.einsum("mkn,pkn->kmp", hist_gw, hist_gw, precision=highest)
        rhs_part = leader * jnp.einsum(
            "mkn,kn->km", hist_gx, resid_a, precision=highest
        ) + jnp.einsum("mkn,kn->km", hist_gw, resid_b, precision=highest)
        frob_part = (
            leader
            * (jnp.sum(hist_sx * hist_sx, axis=(0, 2)) + jnp.sum(hist_gx * hist_gx, axis=(0, 2)))
            + jnp.sum(hist_sw * hist_sw, axis=(0, 2))
            + jnp.sum(hist_gw * hist_gw, axis=(0, 2))
        )
        gram, rhs, frob = lax.psum((gram_part, rhs_part, frob_part), ("con", "var"))
        coef = solve_small(gram + (ridge * frob)[:, None, None] * identity, rhs)
        prev_x, prev_w, prev_gx, prev_gw = (state_a, state_b, resid_a, resid_b)
        state_a = (
            state_a + resid_a - jnp.einsum("km,mkn->kn", coef, hist_sx + hist_gx, precision=highest)
        )
        state_b = (
            state_b + resid_b - jnp.einsum("km,mkn->kn", coef, hist_sw + hist_gw, precision=highest)
        )
    return (state_a, state_b)


def solution(mesh):
    in_specs = (
        P("con", "var", None, None, None),
        P("con", "var", None),
        P("con", "var", None),
        P("var"),
        P(None, "var"),
        P(None, ("con", "var")),
        P(None, ("con", "var")),
        P(("con", "var")),
        P(),
        P(None, "var"),
        P(None, ("con", "var")),
        P(None, "var"),
        P(None, ("con", "var")),
        P(None, "var"),
        P(None, ("con", "var")),
        P(None, None, "var"),
        P(None, None, ("con", "var")),
        P(None, None, "var"),
        P(None, None, ("con", "var")),
        P(),
    )
    out_specs = (P(None, "var"), P(None, ("con", "var")))
    return jax.shard_map(
        per_device, mesh=mesh, in_specs=in_specs, out_specs=out_specs, check_vma=False
    )
```

profile of v0, /device:TPU:1, one launch (start us, length us, event | category | flops | bytes accessed | tf_op | source)
XLA Modules:
  0.0 1774.2 jit_solution(15769028892441200494)
XLA Ops:
  10.1 9.3 fusion.20
  27.1 117.6 %reduce-scatter.7.cloned.1.call-done = f32[8,2048]{1,0:T(8,128)} async-done(((f32[8,65536]{1,0:T(8,128)}), f32[8,2048]{1,0:T(8,128)}) %reduce-scatter.7.cloned.1.call-update) | async-done | bytes 65552 | tf_op jit(solution)/shard_map/reduce_scatter | solution.py:71
  146.3 66.1 %all-gather.5.cloned.1.call-done = f32[8,65536]{1,0:T(8,128)} async-done(((f32[8,2048]{1,0:T(8,128)}), f32[8,65536]{1,0:T(8,128)}) %all-gather.5.cloned.1.call-update) | async-done | bytes 2097168 | tf_op jit(solution)/shard_map/all_gather | solution.py:74
  214.6 5.9 fusion.23
  221.9 82.7 %all-reduce.9.cloned.1.call-done = f32[8,4096]{1,0:T(8,128)} async-done(((f32[8,4096]{1,0:T(8,128)}), f32[8,4096]{1,0:T(8,128)}) %all-reduce.9.cloned.1.call-update) | async-done | bytes 131088 | tf_op jit(solution)/shard_map/psum | solution.py:80
  306.2 9.3 fusion.26
  322.6 117.7 %reduce-scatter.9.cloned.1.call-done = f32[8,2048]{1,0:T(8,128)} async-done(((f32[8,65536]{1,0:T(8,128)}), f32[8,2048]{1,0:T(8,128)}) %reduce-scatter.9.cloned.1.call-update) | async-done | bytes 65552 | tf_op jit(solution)/shard_map/reduce_scatter | solution.py:71
  441.9 65.4 %all-gather.7.cloned.1.call-done = f32[8,65536]{1,0:T(8,128)} async-done(((f32[8,2048]{1,0:T(8,128)}), f32[8,65536]{1,0:T(8,128)}) %all-gather.7.cloned.1.call-update) | async-done | bytes 2097168 | tf_op jit(solution)/shard_map/all_gather | solution.py:74
  509.5 5.9 fusion.29
  516.5 82.9 %all-reduce.11.cloned.1.call-done = f32[8,4096]{1,0:T(8,128)} async-done(((f32[8,4096]{1,0:T(8,128)}), f32[8,4096]{1,0:T(8,128)}) %all-reduce.11.cloned.1.call-update) | async-done | bytes 131088 | tf_op jit(solution)/shard_map/psum | solution.py:80
  600.6 58.6 %all-reduce.3 = (f32[8]{0:T(128)S(1)}, f32[8]{0:T(128)S(1)}) all-reduce(f32[8]{0:T(128)S(1)} %get-tuple-element.10, f32[8]{0:T(128)S(1)} %get-tuple-element.8), channel_id=1, replica_groups=mesh['con'=8,'var'=32] {'var'}, use_global_device_ids=true, to_apply=%region_3.6 | all-reduce | flops 16 | bytes 128 | tf_op jit(solution)/shard_map/psum | solution.py:89
  660.6 9.3 fusion.32
  690.5 94.0 %reduce-scatter.11.cloned.1.call-done = f32[8,2048]{1,0:T(8,128)} async-done(((f32[8,65536]{1,0:T(8,128)}), f32[8,2048]{1,0:T(8,128)}) %reduce-scatter.11.cloned.1.call-update) | async-done | bytes 65552 | tf_op jit(solution)/shard_map/reduce_scatter | solution.py:71
  791.8 78.5 %all-reduce.1 = (f32[8,8,1]{1,0,2:T(8,128)}, f32[8,8,8]{1,2,0:T(8,128)}, f32[8]{0:T(128)}) all-reduce(f32[8,8,1]{1,0,2:T(8,128)} %add_bitcast_fusion.1, f32[8,8,8]{1,2,0:T(8,128)} %convolution_add_fusion.1, f32[8]{0:T(128)} %add_add_fusion.1), channel_id=1, replica_groups=mesh['con'=8,'var'=32] {'con','var'}, use_global_device_ids=true, to_apply=%region_17.21 | all-reduce | flops 584 | bytes 4672 | tf_op jit(solution)/shard_map/psum | solution.py:120
  875.8 7.2 custom-call.12
  885.9 6.5 custom-call.14
  897.3 9.3 fusion.35
  918.2 107.8 %reduce-scatter.13.cloned.1.call-done = f32[8,2048]{1,0:T(8,128)} async-done(((f32[8,65536]{1,0:T(8,128)}), f32[8,2048]{1,0:T(8,128)}) %reduce-scatter.13.cloned.1.call-update) | async-done | bytes 65552 | tf_op jit(solution)/shard_map/reduce_scatter | solution.py:71
  1027.5 64.8 %all-gather.9.cloned.1.call-done = f32[8,65536]{1,0:T(8,128)} async-done(((f32[8,2048]{1,0:T(8,128)}), f32[8,65536]{1,0:T(8,128)}) %all-gather.9.cloned.1.call-update) | async-done | bytes 2097168 | tf_op jit(solution)/shard_map/all_gather | solution.py:74
  1094.7 5.9 fusion.38
  1101.9 82.8 %all-reduce.13.cloned.1.call-done = f32[8,4096]{1,0:T(8,128)} async-done(((f32[8,4096]{1,0:T(8,128)}), f32[8,4096]{1,0:T(8,128)}) %all-reduce.13.cloned.1.call-update) | async-done | bytes 131088 | tf_op jit(solution)/shard_map/psum | solution.py:80
  1186.3 9.3 fusion.41
  1205.1 117.7 %reduce-scatter.15.cloned.1.call-done = f32[8,2048]{1,0:T(8,128)} async-done(((f32[8,65536]{1,0:T(8,128)}), f32[8,2048]{1,0:T(8,128)}) %reduce-scatter.15.cloned.1.call-update) | async-done | bytes 65552 | tf_op jit(solution)/shard_map/reduce_scatter | solution.py:71
  1324.4 64.9 %all-gather.11.cloned.1.call-done = f32[8,65536]{1,0:T(8,128)} async-done(((f32[8,2048]{1,0:T(8,128)}), f32[8,65536]{1,0:T(8,128)}) %all-gather.11.cloned.1.call-update) | async-done | bytes 2097168 | tf_op jit(solution)/shard_map/all_gather | solution.py:74
  1391.6 5.9 fusion.44
  1398.6 83.0 %all-reduce.15.cloned.1.call-done = f32[8,4096]{1,0:T(8,128)} async-done(((f32[8,4096]{1,0:T(8,128)}), f32[8,4096]{1,0:T(8,128)}) %all-reduce.15.cloned.1.call-update) | async-done | bytes 131088 | tf_op jit(solution)/shard_map/psum | solution.py:80
  1482.7 58.2 %all-reduce.2 = (f32[8]{0:T(128)S(1)}, f32[8]{0:T(128)S(1)}) all-reduce(f32[8]{0:T(128)S(1)} %get-tuple-element.6, f32[8]{0:T(128)S(1)} %get-tuple-element.4), channel_id=1, replica_groups=mesh['con'=8,'var'=32] {'var'}, use_global_device_ids=true, to_apply=%region_21.27 | all-reduce | flops 16 | bytes 128 | tf_op jit(solution)/shard_map/psum | solution.py:89
  1542.5 9.3 fusion.47
  1570.3 98.7 %reduce-scatter.17.cloned.1.call-done = f32[8,2048]{1,0:T(8,128)} async-done(((f32[8,65536]{1,0:T(8,128)}), f32[8,2048]{1,0:T(8,128)}) %reduce-scatter.17.cloned.1.call-update) | async-done | bytes 65552 | tf_op jit(solution)/shard_map/reduce_scatter | solution.py:71
  1673.5 78.4 %all-reduce = (f32[8,8,1]{1,0,2:T(8,128)S(1)}, f32[8,8,8]{1,2,0:T(8,128)S(1)}, f32[8]{0:T(128)S(1)}) all-reduce(f32[8,8,1]{1,0,2:T(8,128)S(1)} %add_bitcast_fusion, f32[8,8,8]{1,2,0:T(8,128)S(1)} %convolution_add_fusion, f32[8]{0:T(128)S(1)} %add_add_fusion), channel_id=1, replica_groups=mesh['con'=8,'var'=32] {'con','var'}, use_global_device_ids=true, to_apply=%region_33.39 | all-reduce | flops 584 | bytes 4672 | tf_op jit(solution)/shard_map/psum | solution.py:120
  1752.1 5.8 custom-call.15
  1758.3 5.0 custom-call.17
  (257 shorter events, 135.9 us)
Async XLA Ops:
  7.2 137.5 %reduce-scatter.7.cloned.1.call-start = ((), (), s32[]{:S(2)}) async-start(), calls=%async_computation.6 | async-start | bytes 2162688 | tf_op jit(solution)/shard_map/reduce_scatter | solution.py:71
  7.9 652.7 %copy-start.36 = (pred[72]{0:T(512)(128)(4,1)}, pred[72]{0:T(512)(128)(4,1)S(1)}, u32[]{:S(2)}) copy-start(pred[72]{0:T(512)(128)(4,1)S(1)} %compare_and_fusion.1) | copy-start | bytes 220
  8.5 651.4 %copy-start.41 = (s32[1024]{0:T(1024)}, s32[1024]{0:T(1024)S(1)}, u32[]{:S(2)}) copy-start(s32[1024]{0:T(1024)S(1)} %pad_clamp_fusion.1) | copy-start | bytes 12292
  26.4 118.3 %copy-start.13 = (f32[8,2048]{1,0:T(8,128)S(1)}, f32[8,2048]{1,0:T(8,128)}, u32[]{:S(2)}) copy-start(f32[8,2048]{1,0:T(8,128)} %param.39) | copy-start | bytes 196612
  26.4 118.3 %copy-start.30 = (f32[8,2048]{1,0:T(8,128)S(1)}, f32[8,2048]{1,0:T(8,128)}, u32[]{:S(2)}) copy-start(f32[8,2048]{1,0:T(8,128)} %param.34) | copy-start | bytes 196612
  26.4 118.3 %copy-start.31 = (f32[8,2048]{1,0:T(8,128)S(1)}, f32[8,2048]{1,0:T(8,128)}, u32[]{:S(2)}) copy-start(f32[8,2048]{1,0:T(8,128)} %param.35) | copy-start | bytes 196612
  26.4 186.0 %all-gather.5.cloned.1.call-start = ((), (), s32[]{:S(2)}) async-start(), calls=%async_computation.7 | async-start | bytes 2162688 | tf_op jit(solution)/shard_map/all_gather | solution.py:74
  27.1 413.2 %copy-start.24 = (f32[2048]{0:T(1024)}, f32[2048]{0:T(1024)S(1)}, u32[]{:S(2)}) copy-start(f32[2048]{0:T(1024)S(1)} %add_multiply_fusion.2) | copy-start | bytes 24580
  146.2 638.3 %copy-start.7 = (f32[8,2048]{1,0:T(8,128)}, f32[8,2048]{1,0:T(8,128)S(1)}, u32[]{:S(2)}) copy-start(f32[8,2048]{1,0:T(8,128)S(1)} %get-tuple-element.40) | copy-start | bytes 196612
  146.2 638.3 %copy-start.10 = (f32[8,2048]{1,0:T(8,128)}, f32[8,2048]{1,0:T(8,128)S(1)}, u32[]{:S(2)}) copy-start(f32[8,2048]{1,0:T(8,128)S(1)} %get-tuple-element.41) | copy-start | bytes 196612
  146.2 158.4 %all-reduce.9.cloned.1.call-start = ((), (), s32[]{:S(2)}) async-start(), calls=%async_computation.8 | async-start | bytes 262144 | tf_op jit(solution)/shard_map/psum | solution.py:80
  146.3 361.0 %copy-start.44 = (s32[1024]{0:T(1024)}, s32[1024]{0:T(1024)S(1)}, u32[]{:S(2)}) copy-start(s32[1024]{0:T(1024)S(1)} %pad_clamp_fusion) | copy-start | bytes 12292
  146.3 363.1 %copy-start.47 = (pred[72]{0:T(512)(128)(4,1)}, pred[72]{0:T(512)(128)(4,1)S(1)}, u32[]{:S(2)}) copy-start(pred[72]{0:T(512)(128)(4,1)S(1)} %compare_and_fusion) | copy-start | bytes 220
  221.6 218.7 %reduce-scatter.9.cloned.1.call-start = ((), (), s32[]{:S(2)}) async-start(), calls=%async_computation.9 | async-start | bytes 2162688 | tf_op jit(solution)/shard_map/reduce_scatter | solution.py:71
  322.5 184.7 %all-gather.7.cloned.1.call-start = ((), (), s32[]{:S(2)}) async-start(), calls=%async_computation.10 | async-start | bytes 2162688 | tf_op jit(solution)/shard_map/all_gather | solution.py:74
  441.8 157.6 %all-reduce.11.cloned.1.call-start = ((), (), s32[]{:S(2)}) async-start(), calls=%async_computation.11 | async-start | bytes 262144 | tf_op jit(solution)/shard_map/psum | solution.py:80
  509.5 149.7 %copy-start.27 = (f32[8,4096]{1,0:T(8,128)S(1)}, f32[8,4096]{1,0:T(8,128)}, u32[]{:S(2)}) copy-start(f32[8,4096]{1,0:T(8,128)} %param.42) | copy-start | bytes 393220
  509.5 149.7 %copy-start.28 = (f32[8,4096]{1,0:T(8,128)S(1)}, f32[8,4096]{1,0:T(8,128)}, u32[]{:S(2)}) copy-start(f32[8,4096]{1,0:T(8,128)} %param.40) | copy-start | bytes 393220
  516.5 268.0 %reduce-scatter.11.cloned.1.call-start = ((), (), s32[]{:S(2)}) async-start(), calls=%async_computation.12 | async-start | bytes 2162688 | tf_op jit(solution)/shard_map/reduce_scatter | solution.py:71
  516.5 143.4 %copy-start.53 = (f32[8]{0:T(128)}, f32[8]{0:T(128)S(1)}, u32[]{:S(2)}) copy-start(f32[8]{0:T(128)S(1)} %add_multiply_fusion.3) | copy-start | bytes 100
  677.0 349.0 %reduce-scatter.13.cloned.1.call-start = ((), (), s32[]{:S(2)}) async-start(), calls=%async_computation.13 | async-start | bytes 2162688 | tf_op jit(solution)/shard_map/reduce_scatter | solution.py:71
  916.1 109.9 %copy-start.8 = (f32[8,2048]{1,0:T(8,128)S(1)}, f32[8,2048]{1,0:T(8,128)}, u32[]{:S(2)}) copy-start(f32[8,2048]{1,0:T(8,128)} %copy-done.7) | copy-start | bytes 196612
  916.1 109.9 %copy-start.11 = (f32[8,2048]{1,0:T(8,128)S(1)}, f32[8,2048]{1,0:T(8,128)}, u32[]{:S(2)}) copy-start(f32[8,2048]{1,0:T(8,128)} %copy-done.10) | copy-start | bytes 196612
  916.1 109.9 %copy-start.25 = (f32[2048]{0:T(1024)S(1)}, f32[2048]{0:T(1024)}, u32[]{:S(2)}) copy-start(f32[2048]{0:T(1024)} %copy-done.24) | copy-start | bytes 24580
  916.1 178.6 %copy-start.48 = (pred[72]{0:T(512)(128)(4,1)S(1)}, pred[72]{0:T(512)(128)(4,1)}, u32[]{:S(2)}) copy-start(pred[72]{0:T(512)(128)(4,1)} %copy-done.47) | copy-start | bytes 220
  916.1 176.2 %all-gather.9.cloned.1.call-start = ((), (), s32[]{:S(2)}) async-start(), calls=%async_computation.14 | async-start | bytes 2162688 | tf_op jit(solution)/shard_map/all_gather | solution.py:74
  1027.5 157.1 %all-reduce.13.cloned.1.call-start = ((), (), s32[]{:S(2)}) async-start(), calls=%async_computation.15 | async-start | bytes 262144 | tf_op jit(solution)/shard_map/psum | solution.py:80
  1101.6 221.2 %reduce-scatter.15.cloned.1.call-start = ((), (), s32[]{:S(2)}) async-start(), calls=%async_computation.16 | async-start | bytes 2162688 | tf_op jit(solution)/shard_map/reduce_scatter | solution.py:71
  1205.1 184.3 %all-gather.11.cloned.1.call-start = ((), (), s32[]{:S(2)}) async-start(), calls=%async_computation.17 | async-start | bytes 2162688 | tf_op jit(solution)/shard_map/all_gather | solution.py:74
  1324.3 157.2 %all-reduce.15.cloned.1.call-start = ((), (), s32[]{:S(2)}) async-start(), calls=%async_computation.18 | async-start | bytes 262144 | tf_op jit(solution)/shard_map/psum | solution.py:80
  1398.5 270.5 %reduce-scatter.17.cloned.1.call-start = ((), (), s32[]{:S(2)}) async-start(), calls=%async_computation.19 | async-start | bytes 2162688 | tf_op jit(solution)/shard_map/reduce_scatter | solution.py:71
  1564.3 105.6 %copy-start.3 = (f32[8,8,2048]{2,1,0:T(8,128)S(1)}, f32[8,8,2048]{2,1,0:T(8,128)}, u32[]{:S(2)}) copy-start(f32[8,8,2048]{2,1,0:T(8,128)} %param.45) | copy-start | bytes 1572868
  (42 other events, 1707.0 us)
Sparse Core Ops, SparseCore 0:
  26.6 118.1 reduce-scatter.6
  147.3 65.0 all-gather.4
  221.7 82.8 all-reduce.8
  322.7 117.6 reduce-scatter.8
  442.8 64.4 all-gather.6
  516.6 82.8 all-reduce.10
  677.1 107.3 reduce-scatter.10
  916.2 109.6 reduce-scatter.12
  1027.8 64.4 all-gather.8
  1101.7 82.8 all-reduce.12
  1205.2 117.6 reduce-scatter.14
  1324.5 64.7 all-gather.10
  1398.6 82.8 all-reduce.14
  1561.7 107.2 reduce-scatter.16
where the time goes:
time: 1780 us; the launch traced here: 1770 us
  waiting for transfers between devices  1250 us (70%)
  blocking collectives  274 us (15%)
  matrix products  116 us (7%)
  local copies, waits for them, and re-layouts  61.5 us (3%)
  other arithmetic  59.9 us (3%)
    reduce_scatter x6, waiting for transfers between devices, forward(): return lax.psum_scatter(panel, 'var', scatter_dimension=1, tiled=True)  654 us
    psum x4, waiting for transfers between devices, backward(): return lax.psum(partial_sum, 'con')  331 us
    all_gather x4, waiting for transfers between devices, backward(): panel = lax.all_gather(vector, 'var', axis=1, tiled=True)  261 us
    psum x2, blocking collectives, per_device(): gram, rhs, frob = lax.psum((gram_part, rhs_part, frob_part), ('con', 'var'))  157 us
    psum x2, blocking collectives, per_device(): res_norm = lax.psum(jnp.sum(resid * resid, axis=1), 'var')  117 us
    dot_general x6, matrix products, forward(): contrib = jnp.einsum('ktj,tij->kti', pieces, blocks, precision=highest)  55.7 us
  transfers between devices with their start and end apart: 14, of which 14 were waited for; matrix products, arithmetic and copies ran while one was open for 1% of the time, Pallas kernels for 0%

commit v1 on v0

v1 whole, which is shorter than its diff:
```python
import functools

import jax
import jax.numpy as jnp
from jax import lax
from jax.experimental import pallas as pl
from jax.experimental.pallas import tpu as pltpu
from jax.sharding import PartitionSpec as P

STEPS = 2
LANES = 128
UNROLL = 24

relax = 1.6
ridge = 0.01

f32 = jnp.float32
bf16 = jnp.bfloat16

U_H, V_H, U_U, U_V, U_P, V_P, V_V, S_S, R_R, C_C, U_D, V_D, SCALARS = 0, 8, 16, 17, 18, 19, 20, 21, 22, 23, 24, 25, 26


def halves(value):
    high = value.astype(bf16)
    return high, (value - high.astype(f32)).astype(bf16)


def stacked(piece):
    high, low = halves(piece)
    return jnp.concatenate(
        [
            jnp.concatenate([high, high], axis=1),
            jnp.concatenate([low, jnp.zeros_like(low)], axis=1),
        ],
        axis=0,
    )


def times(left, right, contract):
    both = lax.dot_general(left, right, (((1,), (contract,)), ((), ())), preferred_element_type=f32)
    half = both.shape[0] // 2
    return both[:half] + both[half:]


def at(ref, block):
    return ref[:, pl.ds(pl.multiple_of(block * LANES, LANES), LANES)]


def tile_loop(count, body):
    step = max(d for d in range(1, UNROLL + 1) if count % d == 0)

    def some(i, _):
        for j in range(step):
            body(i * step + j)
        return 0

    lax.fori_loop(0, count // step, some, 0)


def lane_ids(shape):
    return lax.broadcasted_iota(jnp.int32, shape, len(shape) - 1)


def send_products(x_ref, cols, where, tiles, send, left):
    for block in range(x_ref.shape[1] // LANES):
        left[block] = stacked(x_ref[:, block * LANES : (block + 1) * LANES])
    send[...] = jnp.zeros_like(send)

    def one(t):
        high, low = halves(tiles[t])
        send[where(t)] = times(left[cols[t]], jnp.concatenate([high, low], axis=1), 1)

    tile_loop(tiles.shape[0], one)


def add_rows(got, index, rows, runs, sums):
    for ref in sums:
        ref[...] = jnp.zeros_like(ref)
    for s in range(rows.shape[0]):
        ref = sums[s % len(sums)]
        row = rows[s]
        ref[row] = ref[row] + got[index(s)]
    return lambda b: functools.reduce(lambda p, q: p + q, [ref[b] for ref in sums])


def block_of(ref, b):
    return ref[:, b * LANES : (b + 1) * LANES]


def rho_of(level_ref, b):
    return 0.4 * (1.0 + block_of(level_ref, b).astype(f32))


def slack_of(w, center, width):
    return jnp.minimum(jnp.maximum(w, center - width), center + width)


def total(value):
    return jnp.sum(value, axis=1, keepdims=True)


def open_kernel(
    per_run, run_length, rows, cols, con, tiles, x, px, w, pw, pgx, pgw, hsx, hsw, hgx, hgw, send, slot, left, count, asked
):
    memory = hgx.shape[0]
    problems = x.shape[0]
    runs = send.shape[0] // (per_run + 1)
    wide = per_run + 1
    share = x.shape[1] // LANES // con[1]

    def clear(i, _):
        count[i] = 0
        return 0

    lax.fori_loop(0, runs, clear, 0)

    def clear_asked(i, _):
        asked[i] = 0
        return 0

    lax.fori_loop(0, runs * per_run, clear_asked, 0)

    def assign(t, _):
        owner = rows[t] // run_length
        rank = count[owner]
        count[owner] = rank + 1
        slot[t] = owner * per_run + rank
        asked[owner * per_run + rank] = rows[t] - owner * run_length
        return 0

    lax.fori_loop(0, tiles.shape[0], assign, 0)

    def where(t):
        owner = slot[t] // per_run
        return slot[t] + owner

    send_products(x, cols, where, tiles, send, left)

    lanes = lane_ids((problems, LANES))
    first = con[0] * share
    out = jnp.zeros((problems, LANES), f32)

    def both(f):
        acc = None
        for b in range(w.shape[1] // LANES):
            v = f(False, b)
            acc = v if acc is None else acc + v
        for b in range(share):
            acc = acc + f(True, first + b)
        return total(acc)

    def hist(ref_x, ref_w, m, is_x, b):
        if is_x:
            return ref_x[m, :, pl.ds(pl.multiple_of(b * LANES, LANES), LANES)]
        return ref_w[m, :, b * LANES : (b + 1) * LANES]

    def plain(ref_x, ref_w, is_x, b):
        return at(ref_x, b) if is_x else block_of(ref_w, b)

    for m in range(memory):
        for n in range(m, memory):
            value = both(lambda q, b: hist(hgx, hgw, m, q, b) * hist(hgx, hgw, n, q, b))
            out = jnp.where((lanes == m * memory + n) | (lanes == n * memory + m), value, out)
        value = both(lambda q, b: hist(hgx, hgw, m, q, b) * plain(pgx, pgw, q, b))
        out = jnp.where(lanes == memory * memory + m, value, out)

        def square(q, b):
            h = hist(hsx, hsw, m, q, b)
            return h * h

        out = jnp.where(lanes == memory * (memory + 1) + m, both(square), out)
    for r in range(runs):
        mark = out
        for s in range(per_run):
            mark = jnp.where(lanes == LANES - per_run + s, asked[r * per_run + s].astype(f32), mark)
        send[r * wide + per_run] = mark


def penalty_kernel(first, per_run, *refs):
    if first:
        got, w, center, width, level, send, image, early, rows, marks, marks_int, sem, *sums = refs
    else:
        got, rows, w, center, width, level, send, image, *sums = refs
    slots = send.shape[0]
    runs = slots // per_run
    if first:
        wide = per_run + 1
        early_sum = None
        for r in range(runs):
            side = got[r * wide + per_run]
            early_sum = side if early_sum is None else early_sum + side
            marks_int[r : r + 1, :] = side[:1].astype(jnp.int32)
        early[...] = early_sum
        copy = pltpu.make_async_copy(marks_int, marks, sem)
        copy.start()
        copy.wait()
        for s in range(slots):
            rows[s] = marks[s // per_run, LANES - per_run + s % per_run]
        result = add_rows(got, lambda s: s // per_run * wide + s % per_run, rows, runs, sums)
    else:
        result = add_rows(got, lambda s: s, rows, runs, sums)
    blocks = w.shape[1] // LANES
    for b in range(blocks):
        start = result(b)
        image[:, b * LANES : (b + 1) * LANES] = start
        here = block_of(w, b)
        slack = slack_of(here, block_of(center, b), block_of(width, b))
        rho = rho_of(level, b)
        sums[0][b] = rho * (slack - start) - rho * (here - slack)
    for s in range(slots):
        send[s] = sums[0][rows[s]]


def transpose_kernel(first, *refs):
    if first:
        back, slot, cols, tiles, early, send, acc = refs
    else:
        back, slot, cols, tiles, send, acc = refs
    acc[...] = jnp.zeros_like(acc)

    def one(t):
        high, low = halves(tiles[t])
        term = times(stacked(back[slot[t]]), jnp.concatenate([high, low], axis=0), 0)
        col = cols[t]
        acc[col] = acc[col] + term

    tile_loop(tiles.shape[0], one)
    columns = acc.shape[0]
    for b in range(columns):
        value = acc[b]
        for c in range(send.shape[0]):
            send[c, :, b * LANES : (b + 1) * LANES] = value
    if first:
        value = early[...]
        for c in range(send.shape[0]):
            send[c, :, columns * LANES :] = value


def residual_kernel(first, got, x, linear, diag, cols, slot, tiles, send, resid, *refs):
    columns = x.shape[1] // LANES
    if first:
        early, left = refs
    else:
        (left,) = refs
    for b in range(columns):
        lo, hi = b * LANES, (b + 1) * LANES
        value = -linear[:, lo:hi] - diag[:, lo:hi] * x[:, lo:hi]
        part = got[0, :, lo:hi]
        for c in range(1, got.shape[0]):
            part = part + got[c, :, lo:hi]
        resid[:, lo:hi] = value + part
    if first:
        part = got[0, :, columns * LANES :]
        for c in range(1, got.shape[0]):
            part = part + got[c, :, columns * LANES :]
        early[...] = part
    send_products(resid, cols, lambda t: slot[t], tiles, send, left)


def scalar_kernel(
    per_run, got, rows, con, start, w, center, width, level, pw, pgw, x, px, pgx, resid, diag, hgx, hgw, qgx, qgw, send, image, *sums
):
    problems = w.shape[0]
    result = add_rows(got, lambda s: s, rows, sums[0].shape[0], sums)
    memory = hgx.shape[0]
    acc = [None] * SCALARS

    def add(i, value):
        acc[i] = value if acc[i] is None else acc[i] + value

    def terms(u, v, p, s, d, hist):
        for m in range(memory):
            h = hist(m)
            add(U_H + m, u * h)
            add(V_H + m, v * h)
        for i, value in ((U_U, u * u), (U_V, u * v), (U_P, u * p), (V_P, v * p), (V_V, v * v), (S_S, s * s), (U_D, u * d), (V_D, v * d)):
            add(i, value)

    for b in range(w.shape[1] // LANES):
        ar = result(b)
        image[:, b * LANES : (b + 1) * LANES] = ar
        here = block_of(w, b)
        slack = slack_of(here, block_of(center, b), block_of(width, b))
        p = block_of(pgw, b)
        u = relax * (block_of(start, b) - slack) - p
        add(C_C, rho_of(level, b) * ar * ar)
        terms(u, relax * ar, p, here - block_of(pw, b), p - block_of(qgw, b), lambda m: hgw[m, :, b * LANES : (b + 1) * LANES])
    share = x.shape[1] // LANES // con[1]
    for i in range(share):
        b = con[0] * share + i
        r = at(resid, b)
        p = at(pgx, b)
        add(R_R, r * r)
        add(C_C, at(diag, b) * r * r)
        terms(-p, relax * r, p, at(x, b) - at(px, b), p - at(qgx, b), lambda m: hgx[m, :, pl.ds(pl.multiple_of(b * LANES, LANES), LANES)])
    lanes = lane_ids((problems, LANES))
    lane_of = 16 * lax.broadcasted_iota(jnp.int32, (problems, LANES), 0)
    packed = []
    for row in range(2):
        tile = jnp.zeros((problems, LANES), f32)
        for i in range(16):
            if row * 16 + i < SCALARS:
                tile = jnp.where(lanes == lane_of + i, total(acc[row * 16 + i]), tile)
        packed.append(jnp.sum(tile, axis=0, keepdims=True))
    both = jnp.concatenate(packed, axis=0)
    send[...] = jnp.broadcast_to(both[None], send.shape)


def update_kernel(last, steps_before, *refs):
    (late, known, order, sigma_level, x, px, pgx, resid, hsx, hgx, w, pw, pgw, start, image, center, width, hsw, hgw) = refs[:19]
    refs = refs[19:]
    if steps_before:
        dx, dw = refs[:2]
        refs = refs[2:]
    if last:
        x_out, w_out = refs
    else:
        cols, slot, tiles, x_out, w_out, gx_out, gw_out, dx_out, dw_out, known_out, send, left = refs
    problems = x.shape[0]
    memory = hgx.shape[0]
    shape = (problems, LANES)
    lanes = lane_ids(shape)
    program = lax.broadcasted_iota(jnp.int32, shape, 0)
    rows = late[0]
    for i in range(1, late.shape[0]):
        rows = rows + late[i]

    def scalar(i):
        row = jnp.broadcast_to(rows[i // 16 : i // 16 + 1], shape)
        picked = jnp.where(lanes == program * 16 + i % 16, row, 0.0)
        return jnp.broadcast_to(total(picked), shape)

    def given(i):
        return jnp.broadcast_to(known[:, i : i + 1], shape)

    new = [jnp.where(order[steps_before] == m, 1.0, 0.0) for m in range(memory)]
    keep = [1.0 - f for f in new]
    if steps_before:
        old = [jnp.where(order[0] == m, 1.0, 0.0) for m in range(memory)]
    sigma = jnp.zeros(shape, f32)
    for k in range(problems):
        sigma = jnp.where(program == k, 0.2 * (1.0 + sigma_level[k].astype(f32)), sigma)
    norm = scalar(R_R)
    step = norm / (scalar(C_C) + sigma * norm)
    u_h = [scalar(U_H + m) for m in range(memory)]
    v_h = [scalar(V_H + m) for m in range(memory)]
    if steps_before:
        u_d, v_d = scalar(U_D), scalar(V_D)
        u_h = [h * (1.0 - f) + u_d * f for h, f in zip(u_h, old)]
        v_h = [h * (1.0 - f) + v_d * f for h, f in zip(v_h, old)]
    dot = [u + step * v for u, v in zip(u_h, v_h)]
    own = scalar(U_U) + 2.0 * step * scalar(U_V) + step * step * scalar(V_V)
    with_p = scalar(U_P) + step * scalar(V_P)
    gram = [[None] * memory for _ in range(memory)]
    for m in range(memory):
        gram[m][m] = given(m * memory + m) * keep[m] + own * new[m]
        for n in range(m + 1, memory):
            value = given(m * memory + n) * (keep[m] * keep[n]) + dot[n] * new[m] + dot[m] * new[n]
            gram[m][n] = gram[n][m] = value
    at_p, at_s = memory * memory, memory * (memory + 1)
    rhs = []
    for m in range(memory):
        value = given(at_p + m) * keep[m] + with_p * new[m]
        for n in range(memory):
            value = value + gram[m][n] * new[n]
        rhs.append(value)
    s_s = scalar(S_S)
    squares = [given(at_s + m) * keep[m] + s_s * new[m] for m in range(memory)]
    frob = functools.reduce(lambda p, q: p + q, squares + [gram[m][m] for m in range(memory)])
    damp = ridge * frob
    if not last:
        out = jnp.zeros(shape, f32)
        for m in range(memory):
            for n in range(m, memory):
                out = jnp.where((lanes == m * memory + n) | (lanes == n * memory + m), gram[m][n], out)
            out = jnp.where(lanes == at_p + m, rhs[m], out)
            out = jnp.where(lanes == at_s + m, squares[m], out)
        known_out[...] = out
    low = [[None] * memory for _ in range(memory)]
    inverse = []
    for j in range(memory):
        value = gram[j][j] + damp
        for k in range(j):
            value = value - low[j][k] * low[j][k]
        inverse.append(1.0 / jnp.sqrt(value))
        for i in range(j + 1, memory):
            value = gram[i][j]
            for k in range(j):
                value = value - low[i][k] * low[j][k]
            low[i][j] = value * inverse[j]
    half = []
    for i in range(memory):
        value = rhs[i]
        for k in range(i):
            value = value - low[i][k] * half[k]
        half.append(value * inverse[i])
    coef = [None] * memory
    for i in reversed(range(memory)):
        value = half[i]
        for k in range(i + 1, memory):
            value = value - low[k][i] * coef[k]
        coef[i] = value * inverse[i]

    newest = functools.reduce(lambda p, q: p + q, [c * f for c, f in zip(coef, new)])
    left_over = [c * f for c, f in zip(coef, keep)]
    if steps_before:
        older = functools.reduce(lambda p, q: p + q, [c * f for c, f in zip(left_over, old)])
        left_over = [c * (1.0 - f) for c, f in zip(left_over, old)]

    def advance(b, state, previous, g, previous_g, hs, hg, kept, out, g_out, d_out):
        lo, hi = b * LANES, (b + 1) * LANES
        here = state[:, lo:hi]
        fresh = (here - previous[:, lo:hi]) + (g - previous_g[:, lo:hi])
        value = here + g - newest * fresh
        for m in range(memory):
            value = value - left_over[m] * (hs[m, :, lo:hi] + hg[m, :, lo:hi])
        if steps_before:
            value = value - older * kept[:, lo:hi]
        out[:, lo:hi] = value
        if not last:
            g_out[:, lo:hi] = g
            d_out[:, lo:hi] = fresh

    scaled = relax * step
    for b in range(x.shape[1] // LANES):
        g = scaled * block_of(resid, b)
        advance(b, x, px, g, pgx, hsx, hgx, dx if steps_before else None, x_out, None if last else gx_out, None if last else dx_out)
    for b in range(w.shape[1] // LANES):
        slack = slack_of(block_of(w, b), block_of(center, b), block_of(width, b))
        g = relax * (block_of(start, b) + step * block_of(image, b) - slack)
        advance(b, w, pw, g, pgw, hsw, hgw, dw if steps_before else None, w_out, None if last else gw_out, None if last else dw_out)
    if not last:
        send_products(x_out, cols, lambda t: slot[t], tiles, send, left)


def call(kernel, name, ins, outs, scratch=()):
    spaces = {"v": pltpu.VMEM, "s": pltpu.SMEM}
    return pl.pallas_call(
        kernel,
        out_shape=[jax.ShapeDtypeStruct(shape, dtype) for shape, dtype, _ in outs],
        in_specs=[pl.BlockSpec(memory_space=spaces[space]) for _, space in ins],
        out_specs=[pl.BlockSpec(memory_space=spaces[space]) for _, _, space in outs],
        scratch_shapes=list(scratch),
        compiler_params=pltpu.CompilerParams(vmem_limit_bytes=24 * 1024 * 1024),
        name=name,
    )(*[array for array, _ in ins])


def per_device(
    tiles,
    row_tile,
    col_tile,
    diag_cost,
    linear_cost,
    bound_center,
    bound_width,
    rho_level,
    sigma_level,
    state_x,
    state_w,
    prev_x,
    prev_w,
    prev_gx,
    prev_gw,
    hist_sx,
    hist_sw,
    hist_gx,
    hist_gw,
    slot_order,
):
    problems, var_cols = state_x.shape
    con_cols = state_w.shape[1]
    tile_size = tiles.shape[-1]
    var_count, con_count = lax.axis_size("var"), lax.axis_size("con")
    col_count = var_cols // tile_size
    run_length = con_cols // tile_size
    blocks = tiles.reshape(-1, tile_size, tile_size)
    count = blocks.shape[0]
    per_run = -(-count // var_count)
    slots = var_count * per_run
    rows_here = row_tile.reshape(-1)
    cols_here = col_tile.reshape(-1)
    diag = diag_cost.reshape(1, -1)
    level = rho_level.reshape(1, -1)
    con = jnp.stack([lax.axis_index("con").astype(jnp.int32), jnp.int32(con_count)])

    x_like = ((problems, var_cols), f32, "v")
    w_like = ((problems, con_cols), f32, "v")
    panel = ((slots, problems, tile_size), f32, "v")
    wide_panel = ((slots + var_count, problems, tile_size), f32, "v")
    one_tile = ((problems, tile_size), f32, "v")
    left = pltpu.VMEM((col_count, 2 * problems, 2 * tile_size), bf16)
    sums = [pltpu.VMEM((run_length, problems, tile_size), f32)] * 4
    bounds = [(bound_center, "v"), (bound_width, "v")]
    vs = lambda *arrays: [(a, "v") for a in arrays]
    ss = lambda *arrays: [(a, "s") for a in arrays]

    def exchange(x):
        return lax.all_to_all(x, "var", 0, 0, tiled=True)

    def open_with_sizes(rows, cols, where, *refs):
        return open_kernel(per_run, run_length, rows, cols, (where[0], con_count), *refs)

    sent, slot = call(
        open_with_sizes,
        "open",
        ss(rows_here, cols_here, con)
        + vs(blocks, state_x, prev_x, state_w, prev_w, prev_gx, prev_gw, hist_sx, hist_sw, hist_gx, hist_gw),
        [wide_panel, ((count,), jnp.int32, "s")],
        [left, pltpu.SMEM((var_count,), jnp.int32), pltpu.SMEM((slots,), jnp.int32)],
    )
    got = exchange(sent)
    x, w, px, pw, pgx, pgw = state_x, state_w, prev_x, prev_w, prev_gx, prev_gw
    qgx, qgw = pgx, pgw
    kept = []
    known = None
    for step in range(STEPS):
        first, last = step == 0, step == STEPS - 1
        if first:
            sent, start, early, rows = call(
                functools.partial(penalty_kernel, True, per_run),
                "penalty_first",
                vs(got, w, bound_center, bound_width, level),
                [panel, w_like, one_tile, ((slots,), jnp.int32, "s")],
                [pltpu.SMEM((var_count, tile_size), jnp.int32), pltpu.VMEM((var_count, tile_size), jnp.int32), pltpu.SemaphoreType.DMA(())]
                + sums,
            )
        else:
            sent, start = call(
                functools.partial(penalty_kernel, False, per_run),
                "penalty",
                vs(got) + ss(rows) + vs(w, bound_center, bound_width, level),
                [panel, w_like],
                sums,
            )
        back = exchange(sent)
        width = var_cols + (tile_size if first else 0)
        (sent,) = call(
            functools.partial(transpose_kernel, first),
            "transpose",
            vs(back) + ss(slot, cols_here) + vs(blocks) + (vs(early) if first else []),
            [((con_count, problems, width), f32, "v")],
            [pltpu.VMEM((col_count, problems, tile_size), f32)],
        )
        got = lax.all_to_all(sent, "con", 0, 0, tiled=True)
        outs = call(
            functools.partial(residual_kernel, first),
            "residual",
            vs(got, x, linear_cost, diag) + ss(cols_here, slot) + vs(blocks),
            [panel, x_like] + ([one_tile] if first else []),
            [left],
        )
        sent, resid = outs[:2]
        if first:
            known = outs[2]
        got = exchange(sent)

        def scalars_with_sizes(got, rows, where, *refs):
            return scalar_kernel(per_run, got, rows, (where[0], con_count), *refs)

        sent, image = call(
            scalars_with_sizes,
            "scalars",
            vs(got)
            + ss(rows, con)
            + vs(start, w, bound_center, bound_width, level, pw, pgw, x, px, pgx, resid, diag, hist_gx, hist_gw, qgx, qgw),
            [((con_count * var_count, 2, LANES), f32, "v"), w_like],
            sums,
        )
        late = lax.all_to_all(sent, ("con", "var"), 0, 0, tiled=True)
        outs = call(
            functools.partial(update_kernel, last, step),
            "update",
            vs(late, known)
            + ss(slot_order, sigma_level)
            + vs(x, px, pgx, resid, hist_sx, hist_gx, w, pw, pgw, start, image, bound_center, bound_width, hist_sw, hist_gw)
            + vs(*kept)
            + ([] if last else ss(cols_here, slot) + vs(blocks)),
            [x_like, w_like] + ([] if last else [x_like, w_like, x_like, w_like, one_tile, panel]),
            [] if last else [left],
        )
        if last:
            return outs[0], outs[1]
        qgx, qgw = pgx, pgw
        px, pw = x, w
        x, w, pgx, pgw, dx, dw, known, sent = outs
        kept = [dx, dw]
        got = exchange(sent)


def solution(mesh):
    in_specs = (
        P("con", "var", None, None, None),
        P("con", "var", None),
        P("con", "var", None),
        P("var"),
        P(None, "var"),
        P(None, ("con", "var")),
        P(None, ("con", "var")),
        P(("con", "var")),
        P(),
        P(None, "var"),
        P(None, ("con", "var")),
        P(None, "var"),
        P(None, ("con", "var")),
        P(None, "var"),
        P(None, ("con", "var")),
        P(None, None, "var"),
        P(None, None, ("con", "var")),
        P(None, None, "var"),
        P(None, None, ("con", "var")),
        P(),
    )
    out_specs = (P(None, "var"), P(None, ("con", "var")))
    return jax.shard_map(
        per_device, mesh=mesh, in_specs=in_specs, out_specs=out_specs, check_vma=False
    )
```

time: 1780 us -> 247 us (0.14)
  waiting for transfers between devices: 1250 us -> 0 us
  matrix products: 116 us -> 0 us
  blocking collectives: 274 us -> 209 us
  other arithmetic: 59.9 us -> 0.08 us
  local copies, waits for them, and re-layouts: 61.5 us -> 13.5 us
  Pallas kernels: 0 us -> 22.6 us
    reduce_scatter x6 -> x0, waiting for transfers between devices: 654 us -> none  [forward(): return lax.psum_scatter(panel, 'var', scatter_dimension=1, tiled=True)]
    psum x4 -> x0, waiting for transfers between devices: 331 us -> none  [backward(): return lax.psum(partial_sum, 'con')]
    psum x4 -> x0, blocking collectives: 274 us -> none  [the longest x2 157 us: per_device(): gram, rhs, frob = lax.psum((gram_part, rhs_part, frob_part), ('con', 'var'))]
    all_gather x4 -> x0, waiting for transfers between devices: 261 us -> none  [backward(): panel = lax.all_gather(vector, 'var', axis=1, tiled=True)]
    all_to_all x0 -> x10, blocking collectives: none -> 209 us  [the longest x6 124 us: exchange(): return lax.all_to_all(x, 'var', 0, 0, tiled=True)]
    dot_general x32 -> x0, matrix products: 114 us -> none  [the longest x6 55.7 us: forward(): contrib = jnp.einsum('ktj,tij->kti', pieces, blocks, precision=highest)]
    another operation x11 -> x1, other arithmetic: 27.7 us -> 0.08 us  [per_device(): jnp.stack([lax.axis_index('con').astype(jnp.int32), jnp.int32(con_count)])]
    pallas_call x0 -> x11, Pallas kernels: none -> 22.6 us  [call(): pl.pallas_call(kernel, out_shape=[jax.ShapeDtypeStruct(shape, dtype) for...]
  transfers between devices with their start and end apart: 14 -> 0, of which waited for: 14 -> 0; matrix products, arithmetic and copies ran while one was open for 1% -> 0% of each run, Pallas kernels for 0% -> 0%
where the time goes in v1:
time: 247 us; the launch traced here: 246 us
  blocking collectives  209 us (85%)
  Pallas kernels  22.6 us (9%)
  local copies, waits for them, and re-layouts  13.5 us (5%)
    all_to_all x6, blocking collectives, exchange(): return lax.all_to_all(x, 'var', 0, 0, tiled=True)  124 us
    all_to_all x2, blocking collectives, per_device(): late = lax.all_to_all(sent, ('con', 'var'), 0, 0, tiled=True)  45.6 us
    all_to_all x2, blocking collectives, per_device(): got = lax.all_to_all(sent, 'con', 0, 0, tiled=True)  39.3 us
    pallas_call x11, Pallas kernels, call(): pl.pallas_call(kernel, out_shape=[jax.ShapeDtypeStruct(shape, dtype) for...  22.6 us
    unnamed x64, local copies, waits for them, and re-layouts  13.5 us

profile of v1, /device:TPU:1, one launch (start us, length us, event | category | flops | bytes accessed | tf_op | source)
XLA Modules:
  0.0 246.3 jit_solution(10786802256761966599)
XLA Ops:
  0.7 2.3 copy-done
  3.0 1.2 copy-done.2
  4.3 1.0 copy-done.4
  5.3 1.2 copy-done.6
  6.5 0.9 copy-done.8
  7.4 1.0 copy-done.10
  8.5 0.9 copy-done.12
  9.4 0.8 copy-done.14
  10.2 0.8 copy-done.18
  11.1 0.9 copy-done.20
  12.0 0.8 copy-done.22
  14.1 5.0 %open.1 = (f32[128,8,128]{2,1,0:T(8,128)S(1)}, s32[72]{0:T(128)S(1)}) custom-call(s32[72]{0:T(128)S(1)} %bitcast.26, s32[72]{0:T(128)S(1)} %bitcast.20, s32[2]{0:T(128)S(1)} %pad_add_fusion.where, f32[72,128,128]{2,1,0:T(8,128)S(1)} %bitcast.6, f32[8,4096]{1,0:T(8,128)S(1)} %copy-done.8, f32[8,4096]{1,0:T(8,128)S(1)} %copy-done.20, ...), custom_call_target="tpu_custom_call" | custom-call | tf_op jit(solution)/shard_map/open/pallas_call | solution.py:438
  19.2 27.6 %all_to_all.50.refs_0_ = f32[128,8,128]{2,1,0:T(8,128)S(1)} all-to-all(f32[128,8,128]{2,1,0:T(8,128)S(1)} %get-tuple-element.27), channel_id=1, replica_groups=mesh['con'=8,'var'=32] {'var'}, dimensions={0} | all-to-all | bytes 1048576 | tf_op jit(solution)/shard_map/all_to_all | solution.py:499
  46.7 1.7 penalty_first.1
  48.4 19.0 %all_to_all.51.refs_0_ = f32[96,8,128]{2,1,0:T(8,128)S(1)} all-to-all(f32[96,8,128]{2,1,0:T(8,128)S(1)} %get-tuple-element.28), channel_id=1, replica_groups=mesh['con'=8,'var'=32] {'var'}, dimensions={0} | all-to-all | bytes 786432 | tf_op jit(solution)/shard_map/all_to_all | solution.py:499
  67.4 1.6 transpose.2
  69.0 21.4 %all_to_all.52.got = f32[8,8,4224]{2,1,0:T(8,128)S(1)} all-to-all(f32[8,8,4224]{2,1,0:T(8,128)S(1)} %transpose.2), channel_id=1, replica_groups=mesh['con'=8,'var'=32] {'con'}, dimensions={0} | all-to-all | bytes 2162688 | tf_op jit(solution)/shard_map/all_to_all | solution.py:545
  90.5 2.3 residual.2
  92.8 21.0 %all_to_all.53.got = f32[96,8,128]{2,1,0:T(8,128)S(1)} all-to-all(f32[96,8,128]{2,1,0:T(8,128)S(1)} %get-tuple-element.31), channel_id=1, replica_groups=mesh['con'=8,'var'=32] {'var'}, dimensions={0} | all-to-all | bytes 786432 | tf_op jit(solution)/shard_map/all_to_all | solution.py:499
  113.8 1.1 scalars.2
  114.9 22.8 %all_to_all.54.refs_0_ = f32[256,2,128]{2,1,0:T(2,128)S(1)} all-to-all(f32[256,2,128]{2,1,0:T(2,128)S(1)} %get-tuple-element.35), channel_id=1, replica_groups=mesh['con'=8,'var'=32] {'con','var'}, dimensions={0} | all-to-all | bytes 524288 | tf_op jit(solution)/shard_map/all_to_all | solution.py:570
  137.7 3.2 %update.2 = (f32[8,4096]{1,0:T(8,128)S(1)}, f32[8,2048]{1,0:T(8,128)S(1)}, f32[8,4096]{1,0:T(8,128)S(1)}, f32[8,2048]{1,0:T(8,128)S(1)}, f32[8,4096]{1,0:T(8,128...) custom-call(f32[256,2,128]{2,1,0:T(2,128)S(1)} %all_to_all.54.refs_0_, ...), custom_call_target="tpu_custom_call" | custom-call | tf_op jit(solution)/shard_map/update/pallas_call | solution.py:438
  141.0 17.4 %all_to_all.55.refs_0_ = f32[96,8,128]{2,1,0:T(8,128)S(1)} all-to-all(f32[96,8,128]{2,1,0:T(8,128)S(1)} %get-tuple-element.38), channel_id=1, replica_groups=mesh['con'=8,'var'=32] {'var'}, dimensions={0} | all-to-all | bytes 786432 | tf_op jit(solution)/shard_map/all_to_all | solution.py:499
  158.3 0.8 penalty.1
  159.1 18.9 %all_to_all.56.refs_0_ = f32[96,8,128]{2,1,0:T(8,128)S(1)} all-to-all(f32[96,8,128]{2,1,0:T(8,128)S(1)} %get-tuple-element.40), channel_id=1, replica_groups=mesh['con'=8,'var'=32] {'var'}, dimensions={0} | all-to-all | bytes 786432 | tf_op jit(solution)/shard_map/all_to_all | solution.py:499
  178.0 1.6 transpose.3
  179.6 17.9 %all_to_all.57.got = f32[8,8,4096]{2,1,0:T(8,128)S(1)} all-to-all(f32[8,8,4096]{2,1,0:T(8,128)S(1)} %transpose.3), channel_id=1, replica_groups=mesh['con'=8,'var'=32] {'con'}, dimensions={0} | all-to-all | bytes 2097152 | tf_op jit(solution)/shard_map/all_to_all | solution.py:545
  197.5 2.2 residual.3
  199.8 20.6 %all_to_all.58.got = f32[96,8,128]{2,1,0:T(8,128)S(1)} all-to-all(f32[96,8,128]{2,1,0:T(8,128)S(1)} %get-tuple-element.42), channel_id=1, replica_groups=mesh['con'=8,'var'=32] {'var'}, dimensions={0} | all-to-all | bytes 786432 | tf_op jit(solution)/shard_map/all_to_all | solution.py:499
  220.4 1.0 scalars.3
  221.4 22.8 %all_to_all.59.refs_0_ = f32[256,2,128]{2,1,0:T(2,128)S(1)} all-to-all(f32[256,2,128]{2,1,0:T(2,128)S(1)} %get-tuple-element.47), channel_id=1, replica_groups=mesh['con'=8,'var'=32] {'con','var'}, dimensions={0} | all-to-all | bytes 524288 | tf_op jit(solution)/shard_map/all_to_all | solution.py:570
  244.2 2.1 update.3
  (54 shorter events, 1.5 us)
Async XLA Ops:
  0.7 2.3 copy-start
  3.0 1.2 copy-start.2
  4.3 1.0 copy-start.4
  5.3 1.2 copy-start.6
  6.5 0.9 copy-start.8
  7.4 1.0 copy-start.10
  8.5 0.9 copy-start.12
  9.4 0.8 copy-start.14
  10.2 0.8 copy-start.18
  11.1 0.9 copy-start.20
  12.0 0.8 copy-start.22
  12.8 0.7 copy-start.27
  13.5 0.7 copy-start.31
  14.1 32.6 %copy-start.26 = (s32[2048]{0:T(1024)S(1)}, s32[2048]{0:T(1024)}, u32[]{:S(2)}) copy-start(s32[2048]{0:T(1024)} %param.27) | copy-start | bytes 24580
  14.1 53.3 %copy-start.1 = (f32[1,1,72,128,128]{4,3,2,1,0:T(8,128)S(1)}, f32[1,1,72,128,128]{4,3,2,1,0:T(8,128)}, u32[]{:S(2)}) copy-start(f32[1,1,72,128,128]{4,3,2,1,0:T(8,128)} %param.20) | copy-start | bytes 14155780
  19.1 27.6 %copy-start.16 = (f32[8,2048]{1,0:T(8,128)S(1)}, f32[8,2048]{1,0:T(8,128)}, u32[]{:S(2)}) copy-start(f32[8,2048]{1,0:T(8,128)} %refs_15_.7) | copy-start | bytes 196612
  19.1 27.6 %copy-start.17 = (f32[8,2048]{1,0:T(8,128)S(1)}, f32[8,2048]{1,0:T(8,128)}, u32[]{:S(2)}) copy-start(f32[8,2048]{1,0:T(8,128)} %refs_16_.3) | copy-start | bytes 196612
  19.2 48.2 %copy-start.28 = (s32[1,1,72]{2,1,0:T(1,128)S(1)}, s32[1,1,72]{2,1,0:T(1,128)}, u32[]{:S(2)}) copy-start(s32[1,1,72]{2,1,0:T(1,128)} %param.22) | copy-start | bytes 868
  69.0 21.4 %copy-start.9 = (f32[8,4096]{1,0:T(8,128)S(1)}, f32[8,4096]{1,0:T(8,128)}, u32[]{:S(2)}) copy-start(f32[8,4096]{1,0:T(8,128)} %refs_5_.9) | copy-start | bytes 393220
  69.0 21.4 %copy-start.24 = (f32[8,4096]{1,0:T(8,128)S(1)}, f32[8,4096]{1,0:T(8,128)}, u32[]{:S(2)}) copy-start(f32[8,4096]{1,0:T(8,128)} %linear.3) | copy-start | bytes 393220
  69.0 21.4 %copy-start.25 = (f32[4096]{0:T(1024)S(1)}, f32[4096]{0:T(1024)}, u32[]{:S(2)}) copy-start(f32[4096]{0:T(1024)} %param.23) | copy-start | bytes 49156
  90.5 23.3 %copy-start.13 = (f32[8,4096]{1,0:T(8,128)S(1)}, f32[8,4096]{1,0:T(8,128)}, u32[]{:S(2)}) copy-start(f32[8,4096]{1,0:T(8,128)} %refs_14_.3) | copy-start | bytes 393220
  90.5 23.3 %copy-start.15 = (f32[8,2048]{1,0:T(8,128)S(1)}, f32[8,2048]{1,0:T(8,128)}, u32[]{:S(2)}) copy-start(f32[8,2048]{1,0:T(8,128)} %refs_11_.3) | copy-start | bytes 196612
  90.5 23.3 %copy-start.19 = (f32[8,2048]{1,0:T(8,128)S(1)}, f32[8,2048]{1,0:T(8,128)}, u32[]{:S(2)}) copy-start(f32[8,2048]{1,0:T(8,128)} %refs_15_.6) | copy-start | bytes 196612
  90.5 23.3 %copy-start.21 = (f32[8,4096]{1,0:T(8,128)S(1)}, f32[8,4096]{1,0:T(8,128)}, u32[]{:S(2)}) copy-start(f32[8,4096]{1,0:T(8,128)} %refs_5_.7) | copy-start | bytes 393220
  90.5 23.3 %copy-start.23 = (f32[8,2048]{1,0:T(8,128)S(1)}, f32[8,2048]{1,0:T(8,128)}, u32[]{:S(2)}) copy-start(f32[8,2048]{1,0:T(8,128)} %refs_11_.2) | copy-start | bytes 196612
  113.8 23.9 %copy-start.3 = (f32[8,8,4096]{2,1,0:T(8,128)S(1)}, f32[8,8,4096]{2,1,0:T(8,128)}, u32[]{:S(2)}) copy-start(f32[8,8,4096]{2,1,0:T(8,128)} %refs_9_.7) | copy-start | bytes 3145732
  113.8 23.9 %copy-start.5 = (f32[8,8,2048]{2,1,0:T(8,128)S(1)}, f32[8,8,2048]{2,1,0:T(8,128)}, u32[]{:S(2)}) copy-start(f32[8,8,2048]{2,1,0:T(8,128)} %refs_18_.3) | copy-start | bytes 1572868
  113.8 23.9 %copy-start.7 = (f32[8,8,4096]{2,1,0:T(8,128)S(1)}, f32[8,8,4096]{2,1,0:T(8,128)}, u32[]{:S(2)}) copy-start(f32[8,8,4096]{2,1,0:T(8,128)} %refs_8_.9) | copy-start | bytes 3145732
  113.8 23.9 %copy-start.11 = (f32[8,8,2048]{2,1,0:T(8,128)S(1)}, f32[8,8,2048]{2,1,0:T(8,128)}, u32[]{:S(2)}) copy-start(f32[8,8,2048]{2,1,0:T(8,128)} %refs_17_.3) | copy-start | bytes 1572868
  113.8 23.9 %copy-start.29 = (s32[8]{0:T(128)S(1)}, s32[8]{0:T(128)}, u32[]{:S(2)}) copy-start(s32[8]{0:T(128)} %refs_2_.11) | copy-start | bytes 100
  113.8 23.9 %copy-start.30 = (s32[8]{0:T(128)S(1)}, s32[8]{0:T(128)}, u32[]{:S(2)}) copy-start(s32[8]{0:T(128)} %refs_3_.13) | copy-start | bytes 100

commit v2 on v1

--- a/solution.py
+++ b/solution.py
@@ -61,7 +61,7 @@
     return lax.broadcasted_iota(jnp.int32, shape, len(shape) - 1)
 
 
-def send_products(x_ref, cols, where, tiles, send, left):
+def send_products(x_ref, cols, where, tiles, send, left, waits=(None,)):
     for block in range(x_ref.shape[1] // LANES):
         left[block] = stacked(x_ref[:, block * LANES : (block + 1) * LANES])
     send[...] = jnp.zeros_like(send)
@@ -70,7 +70,11 @@
         high, low = halves(tiles[t])
         send[where(t)] = times(left[cols[t]], jnp.concatenate([high, low], axis=1), 1)
 
-    tile_loop(tiles.shape[0], one)
+    size = tiles.shape[0] // len(waits)
+    for i, wait in enumerate(waits):
+        if wait is not None:
+            wait()
+        tile_loop(size, lambda t, i=i: one(t + i * size))
 
 
 def add_rows(got, index, rows, runs, sums):
@@ -99,14 +103,25 @@
     return jnp.sum(value, axis=1, keepdims=True)
 
 
-def open_kernel(
-    per_run, run_length, rows, cols, con, tiles, x, px, w, pw, pgx, pgw, hsx, hsw, hgx, hgw, send, slot, left, count, asked
-):
+def open_kernel(per_run, run_length, share, parts, *refs):
+    (hbm_rows, hbm_cols, hbm_x, hbm_tiles, *far), (send, slot), refs = refs[:13], refs[13:15], refs[15:]
+    rows_buf, cols_buf, x, tiles, px, w, pw, pgx, pgw, hsx, hsw, hgx, hgw, left, count, asked, sem = refs
     memory = hgx.shape[0]
     problems = x.shape[0]
     runs = send.shape[0] // (per_run + 1)
     wide = per_run + 1
-    share = x.shape[1] // LANES // con[1]
+    first = lax.axis_index("con") * share
+    mine = pl.ds(pl.multiple_of(first * LANES, LANES), share * LANES)
+    far_px, far_w, far_pw, far_pgx, far_pgw, far_hsx, far_hsw, far_hgx, far_hgw = far
+    size = tiles.shape[0] // parts
+    moves = [(hbm_rows, rows_buf), (hbm_cols, cols_buf), (hbm_x, x)]
+    moves += [(hbm_tiles.at[pl.ds(i * size, size)], tiles.at[pl.ds(i * size, size)]) for i in range(parts)]
+    moves += [(far_w, w), (far_pw, pw), (far_pgw, pgw), (far_hsw, hsw), (far_hgw, hgw)]
+    moves += [(far_px.at[:, mine], px), (far_pgx.at[:, mine], pgx), (far_hsx.at[:, :, mine], hsx), (far_hgx.at[:, :, mine], hgx)]
+    copies = [pltpu.make_async_copy(a, b, sem.at[i]) for i, (a, b) in enumerate(moves)]
+    for copy in copies:
+        copy.start()
+    rows, cols = rows_buf.at[0], cols_buf.at[0]
 
     def clear(i, _):
         count[i] = 0
@@ -119,6 +134,8 @@
         return 0
 
     lax.fori_loop(0, runs * per_run, clear_asked, 0)
+    copies[0].wait()
+    copies[1].wait()
 
     def assign(t, _):
         owner = rows[t] // run_length
@@ -134,10 +151,12 @@
         owner = slot[t] // per_run
         return slot[t] + owner
 
-    send_products(x, cols, where, tiles, send, left)
+    copies[2].wait()
+    send_products(x, cols, where, tiles, send, left, [copy.wait for copy in copies[3 : 3 + parts]])
+    for copy in copies[3 + parts :]:
+        copy.wait()
 
     lanes = lane_ids((problems, LANES))
-    first = con[0] * share
     out = jnp.zeros((problems, LANES), f32)
 
     def both(f):
@@ -146,16 +165,14 @@
             v = f(False, b)
             acc = v if acc is None else acc + v
         for b in range(share):
-            acc = acc + f(True, first + b)
+            acc = acc + f(True, b)
         return total(acc)
 
     def hist(ref_x, ref_w, m, is_x, b):
-        if is_x:
-            return ref_x[m, :, pl.ds(pl.multiple_of(b * LANES, LANES), LANES)]
-        return ref_w[m, :, b * LANES : (b + 1) * LANES]
+        return (ref_x if is_x else ref_w)[m, :, b * LANES : (b + 1) * LANES]
 
     def plain(ref_x, ref_w, is_x, b):
-        return at(ref_x, b) if is_x else block_of(ref_w, b)
+        return block_of(ref_x if is_x else ref_w, b)
 
     for m in range(memory):
         for n in range(m, memory):
@@ -227,16 +244,12 @@
     tile_loop(tiles.shape[0], one)
     columns = acc.shape[0]
     for b in range(columns):
-        value = acc[b]
-        for c in range(send.shape[0]):
-            send[c, :, b * LANES : (b + 1) * LANES] = value
+        send[:, b * LANES : (b + 1) * LANES] = acc[b]
     if first:
-        value = early[...]
-        for c in range(send.shape[0]):
-            send[c, :, columns * LANES :] = value
-
-
-def residual_kernel(first, got, x, linear, diag, cols, slot, tiles, send, resid, *refs):
+        send[:, columns * LANES :] = early[...]
+
+
+def residual_kernel(first, own, other, x, linear, diag, cols, slot, tiles, send, resid, *refs):
     columns = x.shape[1] // LANES
     if first:
         early, left = refs
@@ -245,20 +258,14 @@
     for b in range(columns):
         lo, hi = b * LANES, (b + 1) * LANES
         value = -linear[:, lo:hi] - diag[:, lo:hi] * x[:, lo:hi]
-        part = got[0, :, lo:hi]
-        for c in range(1, got.shape[0]):
-            part = part + got[c, :, lo:hi]
-        resid[:, lo:hi] = value + part
+        resid[:, lo:hi] = value + (own[:, lo:hi] + other[:, lo:hi])
     if first:
-        part = got[0, :, columns * LANES :]
-        for c in range(1, got.shape[0]):
-            part = part + got[c, :, columns * LANES :]
-        early[...] = part
+        early[...] = own[:, columns * LANES :] + other[:, columns * LANES :]
     send_products(resid, cols, lambda t: slot[t], tiles, send, left)
 
 
 def scalar_kernel(
-    per_run, got, rows, con, start, w, center, width, level, pw, pgw, x, px, pgx, resid, diag, hgx, hgw, qgx, qgw, send, image, *sums
+    share, got, rows, start, w, center, width, level, pw, pgw, x, px, pgx, resid, diag, hgx, hgw, qgx, qgw, send, image, *sums
 ):
     problems = w.shape[0]
     result = add_rows(got, lambda s: s, rows, sums[0].shape[0], sums)
@@ -285,9 +292,8 @@
         u = relax * (block_of(start, b) - slack) - p
         add(C_C, rho_of(level, b) * ar * ar)
         terms(u, relax * ar, p, here - block_of(pw, b), p - block_of(qgw, b), lambda m: hgw[m, :, b * LANES : (b + 1) * LANES])
-    share = x.shape[1] // LANES // con[1]
     for i in range(share):
-        b = con[0] * share + i
+        b = lax.axis_index("con") * share + i
         r = at(resid, b)
         p = at(pgx, b)
         add(R_R, r * r)
@@ -307,23 +313,27 @@
 
 
 def update_kernel(last, steps_before, *refs):
-    (late, known, order, sigma_level, x, px, pgx, resid, hsx, hgx, w, pw, pgw, start, image, center, width, hsw, hgw) = refs[:19]
-    refs = refs[19:]
+    (late, known, order, sigma_level, x, px, pgx, resid, hsx, hgx) = refs[:10]
+    refs = refs[10:]
+    if last:
+        (w, pw, pgw, start, image, center, width, hsw, hgw) = refs[:9]
+        refs = refs[9:]
     if steps_before:
         dx, dw = refs[:2]
         refs = refs[2:]
     if last:
         x_out, w_out = refs
     else:
-        cols, slot, tiles, x_out, w_out, gx_out, gw_out, dx_out, dw_out, known_out, send, left = refs
+        cols, slot, tiles, x_out, gx_out, dx_out, known_out, factors, send, left = refs
     problems = x.shape[0]
     memory = hgx.shape[0]
     shape = (problems, LANES)
     lanes = lane_ids(shape)
     program = lax.broadcasted_iota(jnp.int32, shape, 0)
-    rows = late[0]
-    for i in range(1, late.shape[0]):
-        rows = rows + late[i]
+    chains = [late[i] for i in range(8)]
+    for i in range(8, late.shape[0]):
+        chains[i % 8] = chains[i % 8] + late[i]
+    rows = functools.reduce(lambda p, q: p + q, chains)
 
     def scalar(i):
         row = jnp.broadcast_to(rows[i // 16 : i // 16 + 1], shape)
@@ -407,34 +417,48 @@
         older = functools.reduce(lambda p, q: p + q, [c * f for c, f in zip(left_over, old)])
         left_over = [c * (1.0 - f) for c, f in zip(left_over, old)]
 
-    def advance(b, state, previous, g, previous_g, hs, hg, kept, out, g_out, d_out):
-        lo, hi = b * LANES, (b + 1) * LANES
-        here = state[:, lo:hi]
-        fresh = (here - previous[:, lo:hi]) + (g - previous_g[:, lo:hi])
-        value = here + g - newest * fresh
-        for m in range(memory):
-            value = value - left_over[m] * (hs[m, :, lo:hi] + hg[m, :, lo:hi])
-        if steps_before:
-            value = value - older * kept[:, lo:hi]
-        out[:, lo:hi] = value
-        if not last:
-            g_out[:, lo:hi] = g
-            d_out[:, lo:hi] = fresh
-
     scaled = relax * step
+    older = older if steps_before else None
     for b in range(x.shape[1] // LANES):
         g = scaled * block_of(resid, b)
-        advance(b, x, px, g, pgx, hsx, hgx, dx if steps_before else None, x_out, None if last else gx_out, None if last else dx_out)
+        advance(b, newest, left_over, older, x, px, g, pgx, hsx, hgx, dx if steps_before else None, x_out, None if last else gx_out, None if last else dx_out)
+    if last:
+        for b in range(w.shape[1] // LANES):
+            slack = slack_of(block_of(w, b), block_of(center, b), block_of(width, b))
+            g = relax * (block_of(start, b) + step * block_of(image, b) - slack)
+            advance(b, newest, left_over, older, w, pw, g, pgw, hsw, hgw, dw if steps_before else None, w_out, None, None)
+    else:
+        for i, value in enumerate([step, newest] + left_over):
+            factors[i] = value
+        send_products(x_out, cols, lambda t: slot[t], tiles, send, left)
+
+
+def advance(b, newest, left_over, older, state, previous, g, previous_g, hs, hg, kept, out, g_out, d_out):
+    lo, hi = b * LANES, (b + 1) * LANES
+    here = state[:, lo:hi]
+    fresh = (here - previous[:, lo:hi]) + (g - previous_g[:, lo:hi])
+    value = here + g - newest * fresh
+    for m in range(len(left_over)):
+        value = value - left_over[m] * (hs[m, :, lo:hi] + hg[m, :, lo:hi])
+    if kept is not None:
+        value = value - older * kept[:, lo:hi]
+    out[:, lo:hi] = value
+    if g_out is not None:
+        g_out[:, lo:hi] = g
+        d_out[:, lo:hi] = fresh
+
+
+def constraint_kernel(factors, w, pw, pgw, start, image, center, width, hsw, hgw, w_out, gw_out, dw_out):
+    step, newest = factors[0], factors[1]
+    left_over = [factors[2 + m] for m in range(hgw.shape[0])]
     for b in range(w.shape[1] // LANES):
         slack = slack_of(block_of(w, b), block_of(center, b), block_of(width, b))
         g = relax * (block_of(start, b) + step * block_of(image, b) - slack)
-        advance(b, w, pw, g, pgw, hsw, hgw, dw if steps_before else None, w_out, None if last else gw_out, None if last else dw_out)
-    if not last:
-        send_products(x_out, cols, lambda t: slot[t], tiles, send, left)
+        advance(b, newest, left_over, None, w, pw, g, pgw, hsw, hgw, None, w_out, gw_out, dw_out)
 
 
 def call(kernel, name, ins, outs, scratch=()):
-    spaces = {"v": pltpu.VMEM, "s": pltpu.SMEM}
+    spaces = {"v": pltpu.VMEM, "s": pltpu.SMEM, "h": pltpu.HBM}
     return pl.pallas_call(
         kernel,
         out_shape=[jax.ShapeDtypeStruct(shape, dtype) for shape, dtype, _ in outs],
@@ -482,7 +506,6 @@
     cols_here = col_tile.reshape(-1)
     diag = diag_cost.reshape(1, -1)
     level = rho_level.reshape(1, -1)
-    con = jnp.stack([lax.axis_index("con").astype(jnp.int32), jnp.int32(con_count)])
 
     x_like = ((problems, var_cols), f32, "v")
     w_like = ((problems, con_cols), f32, "v")
@@ -498,16 +521,39 @@
     def exchange(x):
         return lax.all_to_all(x, "var", 0, 0, tiled=True)
 
-    def open_with_sizes(rows, cols, where, *refs):
-        return open_kernel(per_run, run_length, rows, cols, (where[0], con_count), *refs)
-
+    def over_con(x):
+        def partner(x, k):
+            return lax.ppermute(x, "con", [(i, i ^ k) for i in range(con_count)])
+
+        others = [partner(x, k) for k in range(2, con_count, 2)]
+        terms = [x] + others
+        while len(terms) > 1:
+            terms = [a + b for a, b in zip(terms[::2], terms[1::2])]
+        return terms[0], partner(terms[0], 1)
+
+    share = col_count // con_count
+    parts = max(d for d in range(1, 4) if count % d == 0)
+    far = [state_x, blocks, prev_x, state_w, prev_w, prev_gx, prev_gw, hist_sx, hist_sw, hist_gx, hist_gw]
+    x_mine, w_mine = pltpu.VMEM((problems, share * tile_size), f32), pltpu.VMEM((problems, con_cols), f32)
+    memory = hist_gx.shape[0]
+    hx_mine = pltpu.VMEM((memory, problems, share * tile_size), f32)
+    hw_mine = pltpu.VMEM((memory, problems, con_cols), f32)
     sent, slot = call(
-        open_with_sizes,
+        functools.partial(open_kernel, per_run, run_length, share, parts),
         "open",
-        ss(rows_here, cols_here, con)
-        + vs(blocks, state_x, prev_x, state_w, prev_w, prev_gx, prev_gw, hist_sx, hist_sw, hist_gx, hist_gw),
+        [(pltpu.with_memory_space_constraint(a, pltpu.HBM), "h") for a in [row_tile[0], col_tile[0]] + far],
         [wide_panel, ((count,), jnp.int32, "s")],
-        [left, pltpu.SMEM((var_count,), jnp.int32), pltpu.SMEM((slots,), jnp.int32)],
+        [
+            pltpu.SMEM((1, count), jnp.int32),
+            pltpu.SMEM((1, count), jnp.int32),
+            pltpu.VMEM((problems, var_cols), f32),
+            pltpu.VMEM(blocks.shape, f32),
+            x_mine, w_mine, w_mine, x_mine, w_mine, hx_mine, hw_mine, hx_mine, hw_mine,
+            left,
+            pltpu.SMEM((var_count,), jnp.int32),
+            pltpu.SMEM((slots,), jnp.int32),
+            pltpu.SemaphoreType.DMA((3 + parts + 9,)),
+        ],
     )
     got = exchange(sent)
     x, w, px, pw, pgx, pgw = state_x, state_w, prev_x, prev_w, prev_gx, prev_gw
@@ -539,14 +585,14 @@
             functools.partial(transpose_kernel, first),
             "transpose",
             vs(back) + ss(slot, cols_here) + vs(blocks) + (vs(early) if first else []),
-            [((con_count, problems, width), f32, "v")],
+            [((problems, width), f32, "v")],
             [pltpu.VMEM((col_count, problems, tile_size), f32)],
         )
-        got = lax.all_to_all(sent, "con", 0, 0, tiled=True)
+        own, other = over_con(sent)
         outs = call(
             functools.partial(residual_kernel, first),
             "residual",
-            vs(got, x, linear_cost, diag) + ss(cols_here, slot) + vs(blocks),
+            vs(own, other, x, linear_cost, diag) + ss(cols_here, slot) + vs(blocks),
             [panel, x_like] + ([one_tile] if first else []),
             [left],
         )
@@ -555,37 +601,38 @@
             known = outs[2]
         got = exchange(sent)
 
-        def scalars_with_sizes(got, rows, where, *refs):
-            return scalar_kernel(per_run, got, rows, (where[0], con_count), *refs)
-
         sent, image = call(
-            scalars_with_sizes,
+            functools.partial(scalar_kernel, share),
             "scalars",
             vs(got)
-            + ss(rows, con)
+            + ss(rows)
             + vs(start, w, bound_center, bound_width, level, pw, pgw, x, px, pgx, resid, diag, hist_gx, hist_gw, qgx, qgw),
             [((con_count * var_count, 2, LANES), f32, "v"), w_like],
             sums,
         )
         late = lax.all_to_all(sent, ("con", "var"), 0, 0, tiled=True)
+        con_part = vs(w, pw, pgw, start, image, bound_center, bound_width, hist_sw, hist_gw)
         outs = call(
             functools.partial(update_kernel, last, step),
             "update",
             vs(late, known)
             + ss(slot_order, sigma_level)
-            + vs(x, px, pgx, resid, hist_sx, hist_gx, w, pw, pgw, start, image, bound_center, bound_width, hist_sw, hist_gw)
+            + vs(x, px, pgx, resid, hist_sx, hist_gx)
+            + (con_part if last else [])
             + vs(*kept)
             + ([] if last else ss(cols_here, slot) + vs(blocks)),
-            [x_like, w_like] + ([] if last else [x_like, w_like, x_like, w_like, one_tile, panel]),
+            [x_like, w_like] if last else [x_like, x_like, x_like, one_tile, ((memory + 2, problems, tile_size), f32, "v"), panel],
             [] if last else [left],
         )
         if last:
             return outs[0], outs[1]
+        new_x, new_gx, dx, known, factors, sent = outs
+        got = exchange(sent)
+        new_w, new_gw, dw = call(constraint_kernel, "constraints", vs(factors) + con_part, [w_like] * 3)
         qgx, qgw = pgx, pgw
-        px, pw = x, w
-        x, w, pgx, pgw, dx, dw, known, sent = outs
+        px, pw, pgx, pgw = x, w, new_gx, new_gw
+        x, w = new_x, new_w
         kept = [dx, dw]
-        got = exchange(sent)
 
 
 def solution(mesh):

time: 247 us -> 238 us (0.964)
  blocking collectives: 209 us -> 157 us
  waiting for transfers between devices: 0 us -> 24.2 us
  starting transfers between devices: 0 us -> 14.5 us
  local copies, waits for them, and re-layouts: 13.5 us -> 18.2 us
    all_to_all x2 -> x0, blocking collectives: 39.3 us -> none  [per_device(): got = lax.all_to_all(sent, 'con', 0, 0, tiled=True)]
    ppermute x0 -> x8, waiting for transfers between devices: none -> 16.9 us  [partner(): return lax.ppermute(x, 'con', [(i, i ^ k) for i in range(con_count)])]
    all_to_all x6 -> x5, blocking collectives: 124 us -> 110 us  [exchange(): return lax.all_to_all(x, 'var', 0, 0, tiled=True)]
    ppermute x0 -> x8, starting transfers between devices: none -> 9.84 us  [partner(): return lax.ppermute(x, 'con', [(i, i ^ k) for i in range(con_count)])]
    all_to_all x0 -> x1, waiting for transfers between devices: none -> 7.31 us  [exchange(): return lax.all_to_all(x, 'var', 0, 0, tiled=True)]
    unnamed x64 -> x122, local copies, waits for them, and re-layouts: 13.5 us -> 18.2 us
    all_to_all x0 -> x1, starting transfers between devices: none -> 4.68 us  [exchange(): return lax.all_to_all(x, 'var', 0, 0, tiled=True)]
    pallas_call x11 -> x12, Pallas kernels: 22.6 us -> 21.7 us  [call(): pl.pallas_call(kernel, out_shape=[jax.ShapeDtypeStruct(shape, dtype) for...]
  transfers between devices with their start and end apart: 0 -> 9, of which waited for: 0 -> 7; matrix products, arithmetic and copies ran while one was open for 0% -> 0% of each run, Pallas kernels for 0% -> 0%
where the time goes in v2:
time: 238 us; the launch traced here: 237 us
  blocking collectives  157 us (66%)
  waiting for transfers between devices  24.2 us (10%)
  Pallas kernels  21.7 us (9%)
  local copies, waits for them, and re-layouts  18.2 us (8%)
  starting transfers between devices  14.5 us (6%)
    all_to_all x5, blocking collectives, exchange(): return lax.all_to_all(x, 'var', 0, 0, tiled=True)  110 us
    all_to_all x2, blocking collectives, per_device(): late = lax.all_to_all(sent, ('con', 'var'), 0, 0, tiled=True)  47.4 us
    pallas_call x12, Pallas kernels, call(): pl.pallas_call(kernel, out_shape=[jax.ShapeDtypeStruct(shape, dtype) for...  21.7 us
    unnamed x122, local copies, waits for them, and re-layouts  18.2 us
    ppermute x8, waiting for transfers between devices, partner(): return lax.ppermute(x, 'con', [(i, i ^ k) for i in range(con_count)])  16.9 us
    ppermute x8, starting transfers between devices, partner(): return lax.ppermute(x, 'con', [(i, i ^ k) for i in range(con_count)])  9.84 us
    all_to_all x1, waiting for transfers between devices, exchange(): return lax.all_to_all(x, 'var', 0, 0, tiled=True)  7.31 us
  transfers between devices with their start and end apart: 9, of which 7 were waited for; matrix products, arithmetic and copies ran while one was open for 0% of the time, Pallas kernels for 0%

profile of v2, /device:TPU:1, one launch (start us, length us, event | category | flops | bytes accessed | tf_op | source)
XLA Modules:
  0.0 236.9 jit_solution(17081837494488433881)
XLA Ops:
  0.7 4.3 %open.1 = (f32[128,8,128]{2,1,0:T(8,128)S(1)}, s32[72]{0:T(128)S(1)}) custom-call(s32[1,72]{1,0:T(1,128)} %bitcast.28, s32[1,72]{1,0:T(1,128)} %bitcast.22, f32[8,4096]{1,0:T(8,128)} %refs_5_.5, f32[72,128,128]{2,1,0:T(8,128)} %bitcast.6, f32[8,4096]{1,0:T(8,128)} %refs_5_.4, f32[8,2048]{1,0:T(8,128)} %refs_11_.3, f32[8,2048]{1,0:T(8,128)} %pw.4, ...), custom_call_target="tpu_custom_call" | custom-call | tf_op jit(solution)/shard_map/open/pallas_call | solution.py:462
  5.0 27.6 %all_to_all.40.refs_0_ = f32[128,8,128]{2,1,0:T(8,128)S(1)} all-to-all(f32[128,8,128]{2,1,0:T(8,128)S(1)} %get-tuple-element.28), channel_id=1, replica_groups=mesh['con'=8,'var'=32] {'var'}, dimensions={0} | all-to-all | bytes 1048576 | tf_op jit(solution)/shard_map/all_to_all | solution.py:522
  32.6 1.7 penalty_first.1
  34.3 19.0 %all_to_all.41.refs_0_ = f32[96,8,128]{2,1,0:T(8,128)S(1)} all-to-all(f32[96,8,128]{2,1,0:T(8,128)S(1)} %get-tuple-element.29), channel_id=1, replica_groups=mesh['con'=8,'var'=32] {'var'}, dimensions={0} | all-to-all | bytes 786432 | tf_op jit(solution)/shard_map/all_to_all | solution.py:522
  53.4 1.6 transpose.2
  54.9 2.8 %collective-permute-start.2 = (f32[8,4224]{1,0:T(8,128)S(1)}, f32[8,4224]{1,0:T(8,128)S(1)}, u32[]{:S(2)}, u32[]{:S(2)}) collective-permute-start(f32[8,4224]{1,0:T(8,128)S(1)} %transpose.2), channel_id=1, source_target_pairs={{0,192},{32,224},{64,128},{96,160},{128,64},{160,96},{192,0},{224,... | collective-permute-start | bytes 405512 | tf_op jit(solution)/shard_map/ppermute | solution.py:526
  58.4 2.9 %collective-permute-done.2 = f32[8,4224]{1,0:T(8,128)S(1)} collective-permute-done((f32[8,4224]{1,0:T(8,128)S(1)}, f32[8,4224]{1,0:T(8,128)S(1)}, u32[]{:S(2)}, u32[]{:S(2)}) %collective-permute-start.2) | collective-permute-done | bytes 135200 | tf_op jit(solution)/shard_map/ppermute | solution.py:526
  61.4 1.9 collective-permute-done.1
  63.3 2.5 %collective-permute-start.3 = (f32[8,4224]{1,0:T(8,128)S(1)}, f32[8,4224]{1,0:T(8,128)S(1)}, u32[]{:S(2)}, u32[]{:S(2)}) collective-permute-start(f32[8,4224]{1,0:T(8,128)S(1)} %add_add_fusion.own), channel_id=1, source_target_pairs={{0,32},{32,0},{64,96},{96,64},{128,160},{160,128},{192,224},{224,1... | collective-permute-start | bytes 405512 | tf_op jit(solution)/shard_map/ppermute | solution.py:526
  65.8 2.9 %collective-permute-done.3.other = f32[8,4224]{1,0:T(8,128)S(1)} collective-permute-done((f32[8,4224]{1,0:T(8,128)S(1)}, f32[8,4224]{1,0:T(8,128)S(1)}, u32[]{:S(2)}, u32[]{:S(2)}) %collective-permute-start.3) | collective-permute-done | bytes 135200 | tf_op jit(solution)/shard_map/ppermute | solution.py:526
  68.8 2.2 residual.2
  71.0 22.1 %all_to_all.42.got = f32[96,8,128]{2,1,0:T(8,128)S(1)} all-to-all(f32[96,8,128]{2,1,0:T(8,128)S(1)} %get-tuple-element.32), channel_id=1, replica_groups=mesh['con'=8,'var'=32] {'var'}, dimensions={0} | all-to-all | bytes 786432 | tf_op jit(solution)/shard_map/all_to_all | solution.py:522
  93.1 1.0 scalars.2
  94.8 24.6 %all_to_all.43.refs_0_ = f32[256,2,128]{2,1,0:T(2,128)S(1)} all-to-all(f32[256,2,128]{2,1,0:T(2,128)S(1)} %get-tuple-element.36), channel_id=1, replica_groups=mesh['con'=8,'var'=32] {'con','var'}, dimensions={0} | all-to-all | bytes 524288 | tf_op jit(solution)/shard_map/all_to_all | solution.py:613
  119.4 2.9 %update.2 = (f32[8,4096]{1,0:T(8,128)S(1)}, f32[8,4096]{1,0:T(8,128)S(1)}, f32[8,4096]{1,0:T(8,128)S(1)}, f32[8,128]{1,0:T(8,128)S(1)}, f32[10,8,128]{2,1,0:T(8,128)S(1)}, /*index=5*/f32[96,8,128]{2,1,0:T(8,128)S(1)}) custom-call(f32[256,2,128]{2,1,0:T(2,128)S(1)} %all_to_all.43.refs_0_, f32[8,128]{1,0:T(8,128)S(1)} %get-tuple-element.37.refs_1_, ...), custom_call_target="tpu_custom_call" | custom-call | tf_op jit(solution)/shard_map/update/pallas_call | solution.py:462
  126.2 4.7 %all-to-all-start.4 = ((f32[96,8,128]{2,1,0:T(8,128)}), f32[96,8,128]{2,1,0:T(8,128)}, u32[]{:S(2)}, u32[]{:S(2)}) async-start(f32[96,8,128]{2,1,0:T(8,128)} %copy-done.28), calls=%async_computation.4 | async-start | bytes 786432 | tf_op jit(solution)/shard_map/all_to_all | solution.py:522
  137.9 7.3 %all-to-all-done.4.refs_0_ = f32[96,8,128]{2,1,0:T(8,128)} async-done(((f32[96,8,128]{2,1,0:T(8,128)}), f32[96,8,128]{2,1,0:T(8,128)}, u32[]{:S(2)}, u32[]{:S(2)}) %all-to-all-start.4) | async-done | bytes 393248 | tf_op jit(solution)/shard_map/all_to_all | solution.py:522
  145.2 0.9 copy-done.11
  148.2 1.3 penalty.1
  149.5 18.9 %all_to_all.44.refs_0_ = f32[96,8,128]{2,1,0:T(8,128)S(1)} all-to-all(f32[96,8,128]{2,1,0:T(8,128)S(1)} %get-tuple-element.42), channel_id=1, replica_groups=mesh['con'=8,'var'=32] {'var'}, dimensions={0} | all-to-all | bytes 786432 | tf_op jit(solution)/shard_map/all_to_all | solution.py:522
  168.4 2.3 copy-done
  172.1 1.6 transpose.3
  173.6 1.1 collective-permute-start.6
  174.7 1.3 collective-permute-start.5
  176.0 1.1 collective-permute-start.4
  177.1 3.6 %collective-permute-done.6 = f32[8,4096]{1,0:T(8,128)S(1)} collective-permute-done((f32[8,4096]{1,0:T(8,128)S(1)}, f32[8,4096]{1,0:T(8,128)S(1)}, u32[]{:S(2)}, u32[]{:S(2)}) %collective-permute-start.6) | collective-permute-done | bytes 131104 | tf_op jit(solution)/shard_map/ppermute | solution.py:526
  181.5 5.1 %collective-permute-done.7.other = f32[8,4096]{1,0:T(8,128)S(1)} collective-permute-done((f32[8,4096]{1,0:T(8,128)S(1)}, f32[8,4096]{1,0:T(8,128)S(1)}, u32[]{:S(2)}, u32[]{:S(2)}) %collective-permute-start.7) | collective-permute-done | bytes 131104 | tf_op jit(solution)/shard_map/ppermute | solution.py:526
  186.7 2.2 residual.3
  188.9 22.2 %all_to_all.45.got = f32[96,8,128]{2,1,0:T(8,128)S(1)} all-to-all(f32[96,8,128]{2,1,0:T(8,128)S(1)} %get-tuple-element.44), channel_id=1, replica_groups=mesh['con'=8,'var'=32] {'var'}, dimensions={0} | all-to-all | bytes 786432 | tf_op jit(solution)/shard_map/all_to_all | solution.py:522
  211.1 1.0 scalars.3
  212.1 22.8 %all_to_all.46.refs_0_ = f32[256,2,128]{2,1,0:T(2,128)S(1)} all-to-all(f32[256,2,128]{2,1,0:T(2,128)S(1)} %get-tuple-element.49), channel_id=1, replica_groups=mesh['con'=8,'var'=32] {'con','var'}, dimensions={0} | all-to-all | bytes 524288 | tf_op jit(solution)/shard_map/all_to_all | solution.py:613
  235.0 1.9 update.3
  (130 shorter events, 16.6 us)
Async XLA Ops:
  0.6 52.6 %slice-start = ((s8[4718592]{0:T(1024)(128)(4,1)}), s8[4194304]{0:T(1024)(128)(4,1)S(1)}, s32[]{:S(2)}) async-start(s8[4718592]{0:T(1024)(128)(4,1)} %bitcast.7), calls=%async_computation.8 | async-start | bytes 8388608
  0.7 52.6 %slice-start.1 = ((s8[4718592]{0:T(1024)(128)(4,1)}), s8[524288]{0:T(1024)(128)(4,1)S(1)}, s32[]{:S(2)}) async-start(s8[4718592]{0:T(1024)(128)(4,1)} %bitcast.7), calls=%async_computation.9 | async-start | bytes 1048576
  0.7 52.6 %copy-start.45 = (s32[1,1,72]{2,1,0:T(1,128)S(1)}, s32[1,1,72]{2,1,0:T(1,128)}, u32[]{:S(2)}) copy-start(s32[1,1,72]{2,1,0:T(1,128)} %param.22) | copy-start | bytes 868
  5.0 114.4 %copy-start.48 = (s32[72]{0:T(128)}, s32[72]{0:T(128)S(1)}, u32[]{:S(2)}) copy-start(s32[72]{0:T(128)S(1)} %get-tuple-element.30.refs_1_.slot.refs_11_) | copy-start | bytes 868
  5.0 63.7 %copy-start.4 = (f32[8,4096]{1,0:T(8,128)S(1)}, f32[8,4096]{1,0:T(8,128)}, u32[]{:S(2)}) copy-start(f32[8,4096]{1,0:T(8,128)} %refs_5_.5) | copy-start | bytes 393220
  5.0 63.7 %copy-start.24 = (f32[8,4096]{1,0:T(8,128)S(1)}, f32[8,4096]{1,0:T(8,128)}, u32[]{:S(2)}) copy-start(f32[8,4096]{1,0:T(8,128)} %linear.3) | copy-start | bytes 393220
  5.0 63.7 %copy-start.29 = (f32[4096]{0:T(1024)S(1)}, f32[4096]{0:T(1024)}, u32[]{:S(2)}) copy-start(f32[4096]{0:T(1024)} %param.23) | copy-start | bytes 49156
  34.3 58.8 %copy-start.32 = (f32[8,2048]{1,0:T(8,128)}, f32[8,2048]{1,0:T(8,128)S(1)}, u32[]{:S(2)}) copy-start(f32[8,2048]{1,0:T(8,128)S(1)} %get-tuple-element.34.start) | copy-start | bytes 196612
  34.3 58.8 %copy-start.50 = (s32[96]{0:T(128)}, s32[96]{0:T(128)S(1)}, u32[]{:S(2)}) copy-start(s32[96]{0:T(128)S(1)} %get-tuple-element.33.rows.refs_1_) | copy-start | bytes 1156
  53.3 39.8 %copy-start.1 = (f32[8,8,4096]{2,1,0:T(8,128)S(1)}, f32[8,8,4096]{2,1,0:T(8,128)}, u32[]{:S(2)}) copy-start(f32[8,8,4096]{2,1,0:T(8,128)} %refs_9_.5) | copy-start | bytes 3145732
  53.3 39.8 %copy-start.2 = (f32[8,8,2048]{2,1,0:T(8,128)S(1)}, f32[8,8,2048]{2,1,0:T(8,128)}, u32[]{:S(2)}) copy-start(f32[8,8,2048]{2,1,0:T(8,128)} %refs_18_.1) | copy-start | bytes 1572868
  53.3 39.8 %copy-start.6 = (f32[8,4096]{1,0:T(8,128)S(1)}, f32[8,4096]{1,0:T(8,128)}, u32[]{:S(2)}) copy-start(f32[8,4096]{1,0:T(8,128)} %qgx.3) | copy-start | bytes 393220
  53.3 39.8 %copy-start.13 = (f32[8,2048]{1,0:T(8,128)S(1)}, f32[8,2048]{1,0:T(8,128)}, u32[]{:S(2)}) copy-start(f32[8,2048]{1,0:T(8,128)} %qgw.3) | copy-start | bytes 196612
  53.3 39.8 %copy-start.16 = (f32[8,4096]{1,0:T(8,128)S(1)}, f32[8,4096]{1,0:T(8,128)}, u32[]{:S(2)}) copy-start(f32[8,4096]{1,0:T(8,128)} %refs_5_.4) | copy-start | bytes 393220
  54.9 6.4 %collective-permute-start.2 = (f32[8,4224]{1,0:T(8,128)S(1)}, f32[8,4224]{1,0:T(8,128)S(1)}, u32[]{:S(2)}, u32[]{:S(2)}) collective-permute-start(f32[8,4224]{1,0:T(8,128)S(1)} %transpose.2), channel_id=1, source_target_pairs={{0,192},{32,224},{64,128},{96,160},{128,64},{160,96},{192,0},{224,... | collective-permute-start | bytes 405512 | tf_op jit(solution)/shard_map/ppermute | solution.py:526
  57.8 5.5 %collective-permute-start.1 = (f32[8,4224]{1,0:T(8,128)S(1)}, f32[8,4224]{1,0:T(8,128)S(1)}, u32[]{:S(2)}, u32[]{:S(2)}) collective-permute-start(f32[8,4224]{1,0:T(8,128)S(1)} %transpose.2), channel_id=1, source_target_pairs={{0,128},{32,160},{64,192},{96,224},{128,0},{160,32},{192,64},{224,... | collective-permute-start | bytes 405512 | tf_op jit(solution)/shard_map/ppermute | solution.py:526
  58.1 5.1 %collective-permute-start = (f32[8,4224]{1,0:T(8,128)S(1)}, f32[8,4224]{1,0:T(8,128)S(1)}, u32[]{:S(2)}, u32[]{:S(2)}) collective-permute-start(f32[8,4224]{1,0:T(8,128)S(1)} %transpose.2), channel_id=1, source_target_pairs={{0,64},{32,96},{64,0},{96,32},{128,192},{160,224},{192,128},{224,1... | collective-permute-start | bytes 405512 | tf_op jit(solution)/shard_map/ppermute | solution.py:526
  63.3 5.5 %collective-permute-start.3 = (f32[8,4224]{1,0:T(8,128)S(1)}, f32[8,4224]{1,0:T(8,128)S(1)}, u32[]{:S(2)}, u32[]{:S(2)}) collective-permute-start(f32[8,4224]{1,0:T(8,128)S(1)} %add_add_fusion.own), channel_id=1, source_target_pairs={{0,32},{32,0},{64,96},{96,64},{128,160},{160,128},{192,224},{224,1... | collective-permute-start | bytes 405512 | tf_op jit(solution)/shard_map/ppermute | solution.py:526
  68.7 50.6 %copy-start.3 = (f32[8,8,4096]{2,1,0:T(8,128)S(1)}, f32[8,8,4096]{2,1,0:T(8,128)}, u32[]{:S(2)}) copy-start(f32[8,8,4096]{2,1,0:T(8,128)} %refs_8_.5) | copy-start | bytes 3145732
  68.8 50.6 %copy-start.55 = (s32[8]{0:T(128)S(1)}, s32[8]{0:T(128)}, u32[]{:S(2)}) copy-start(s32[8]{0:T(128)} %refs_2_.7) | copy-start | bytes 100
  68.8 50.6 %copy-start.57 = (s32[8]{0:T(128)S(1)}, s32[8]{0:T(128)}, u32[]{:S(2)}) copy-start(s32[8]{0:T(128)} %refs_3_.7) | copy-start | bytes 100
  126.2 19.0 %all-to-all-start.4 = ((f32[96,8,128]{2,1,0:T(8,128)}), f32[96,8,128]{2,1,0:T(8,128)}, u32[]{:S(2)}, u32[]{:S(2)}) async-start(f32[96,8,128]{2,1,0:T(8,128)} %copy-done.28), calls=%async_computation.4 | async-start | bytes 786432 | tf_op jit(solution)/shard_map/all_to_all | solution.py:522
  145.2 41.4 %copy-start.47 = (s32[1,1,72]{2,1,0:T(1,128)S(1)}, s32[1,1,72]{2,1,0:T(1,128)}, u32[]{:S(2)}) copy-start(s32[1,1,72]{2,1,0:T(1,128)} %param.22) | copy-start | bytes 868
  173.6 7.1 %collective-permute-start.6 = (f32[8,4096]{1,0:T(8,128)S(1)}, f32[8,4096]{1,0:T(8,128)S(1)}, u32[]{:S(2)}, u32[]{:S(2)}) collective-permute-start(f32[8,4096]{1,0:T(8,128)S(1)} %transpose.3), channel_id=1, source_target_pairs={{0,192},{32,224},{64,128},{96,160},{128,64},{160,96},{192,0},{224,... | collective-permute-start | bytes 393224 | tf_op jit(solution)/shard_map/ppermute | solution.py:526
  174.7 6.0 %collective-permute-start.5 = (f32[8,4096]{1,0:T(8,128)S(1)}, f32[8,4096]{1,0:T(8,128)S(1)}, u32[]{:S(2)}, u32[]{:S(2)}) collective-permute-start(f32[8,4096]{1,0:T(8,128)S(1)} %transpose.3), channel_id=1, source_target_pairs={{0,128},{32,160},{64,192},{96,224},{128,0},{160,32},{192,64},{224,... | collective-permute-start | bytes 393224 | tf_op jit(solution)/shard_map/ppermute | solution.py:526
  176.0 5.2 %collective-permute-start.4 = (f32[8,4096]{1,0:T(8,128)S(1)}, f32[8,4096]{1,0:T(8,128)S(1)}, u32[]{:S(2)}, u32[]{:S(2)}) collective-permute-start(f32[8,4096]{1,0:T(8,128)S(1)} %transpose.3), channel_id=1, source_target_pairs={{0,64},{32,96},{64,0},{96,32},{128,192},{160,224},{192,128},{224,1... | collective-permute-start | bytes 393224 | tf_op jit(solution)/shard_map/ppermute | solution.py:526
  181.2 5.4 %collective-permute-start.7 = (f32[8,4096]{1,0:T(8,128)S(1)}, f32[8,4096]{1,0:T(8,128)S(1)}, u32[]{:S(2)}, u32[]{:S(2)}) collective-permute-start(f32[8,4096]{1,0:T(8,128)S(1)} %add_add_fusion.1.own), channel_id=1, source_target_pairs={{0,32},{32,0},{64,96},{96,64},{128,160},{160,128},{192,224},{224,1... | collective-permute-start | bytes 393224 | tf_op jit(solution)/shard_map/ppermute | solution.py:526
  186.6 48.3 %copy-start.38 = (f32[8,4096]{1,0:T(8,128)S(1)}, f32[8,4096]{1,0:T(8,128)}, u32[]{:S(2)}) copy-start(f32[8,4096]{1,0:T(8,128)} %copy-done.37) | copy-start | bytes 393220
  186.7 48.3 %copy-start.40 = (f32[8,2048]{1,0:T(8,128)S(1)}, f32[8,2048]{1,0:T(8,128)}, u32[]{:S(2)}) copy-start(f32[8,2048]{1,0:T(8,128)} %copy-done.39) | copy-start | bytes 196612
  186.7 48.3 %copy-start.54 = (f32[8,128]{1,0:T(8,128)S(1)}, f32[8,128]{1,0:T(8,128)}, u32[]{:S(2)}) copy-start(f32[8,128]{1,0:T(8,128)} %copy-done.53) | copy-start | bytes 12292
  186.7 48.3 %copy-start.56 = (s32[8]{0:T(128)S(1)}, s32[8]{0:T(128)}, u32[]{:S(2)}) copy-start(s32[8]{0:T(128)} %refs_2_.7) | copy-start | bytes 100
  186.7 48.3 %copy-start.58 = (s32[8]{0:T(128)S(1)}, s32[8]{0:T(128)}, u32[]{:S(2)}) copy-start(s32[8]{0:T(128)} %refs_3_.7) | copy-start | bytes 100
  (38 other events, 571.9 us)

commit v3 on v2

--- a/solution.py
+++ b/solution.py
@@ -309,22 +309,20 @@
                 tile = jnp.where(lanes == lane_of + i, total(acc[row * 16 + i]), tile)
         packed.append(jnp.sum(tile, axis=0, keepdims=True))
     both = jnp.concatenate(packed, axis=0)
-    send[...] = jnp.broadcast_to(both[None], send.shape)
+    send[...] = both
 
 
 def update_kernel(last, steps_before, *refs):
     (late, known, order, sigma_level, x, px, pgx, resid, hsx, hgx) = refs[:10]
-    refs = refs[10:]
-    if last:
-        (w, pw, pgw, start, image, center, width, hsw, hgw) = refs[:9]
-        refs = refs[9:]
+    (w, pw, pgw, start, image, center, width, hsw, hgw) = refs[10:19]
+    refs = refs[19:]
     if steps_before:
         dx, dw = refs[:2]
         refs = refs[2:]
     if last:
         x_out, w_out = refs
     else:
-        cols, slot, tiles, x_out, gx_out, dx_out, known_out, factors, send, left = refs
+        cols, slot, tiles, x_out, w_out, gx_out, gw_out, dx_out, dw_out, known_out, send, left = refs
     problems = x.shape[0]
     memory = hgx.shape[0]
     shape = (problems, LANES)
@@ -422,14 +420,11 @@
     for b in range(x.shape[1] // LANES):
         g = scaled * block_of(resid, b)
         advance(b, newest, left_over, older, x, px, g, pgx, hsx, hgx, dx if steps_before else None, x_out, None if last else gx_out, None if last else dx_out)
-    if last:
-        for b in range(w.shape[1] // LANES):
-            slack = slack_of(block_of(w, b), block_of(center, b), block_of(width, b))
-            g = relax * (block_of(start, b) + step * block_of(image, b) - slack)
-            advance(b, newest, left_over, older, w, pw, g, pgw, hsw, hgw, dw if steps_before else None, w_out, None, None)
-    else:
-        for i, value in enumerate([step, newest] + left_over):
-            factors[i] = value
+    for b in range(w.shape[1] // LANES):
+        slack = slack_of(block_of(w, b), block_of(center, b), block_of(width, b))
+        g = relax * (block_of(start, b) + step * block_of(image, b) - slack)
+        advance(b, newest, left_over, older, w, pw, g, pgw, hsw, hgw, dw if steps_before else None, w_out, None if last else gw_out, None if last else dw_out)
+    if not last:
         send_products(x_out, cols, lambda t: slot[t], tiles, send, left)
 
 
@@ -446,15 +441,6 @@
     if g_out is not None:
         g_out[:, lo:hi] = g
         d_out[:, lo:hi] = fresh
-
-
-def constraint_kernel(factors, w, pw, pgw, start, image, center, width, hsw, hgw, w_out, gw_out, dw_out):
-    step, newest = factors[0], factors[1]
-    left_over = [factors[2 + m] for m in range(hgw.shape[0])]
-    for b in range(w.shape[1] // LANES):
-        slack = slack_of(block_of(w, b), block_of(center, b), block_of(width, b))
-        g = relax * (block_of(start, b) + step * block_of(image, b) - slack)
-        advance(b, newest, left_over, None, w, pw, g, pgw, hsw, hgw, None, w_out, gw_out, dw_out)
 
 
 def call(kernel, name, ins, outs, scratch=()):
@@ -531,6 +517,7 @@
             terms = [a + b for a, b in zip(terms[::2], terms[1::2])]
         return terms[0], partner(terms[0], 1)
 
+    one_core = [list(range(k, con_count * var_count, 2)) for k in range(2)]
     share = col_count // con_count
     parts = max(d for d in range(1, 4) if count % d == 0)
     far = [state_x, blocks, prev_x, state_w, prev_w, prev_gx, prev_gw, hist_sx, hist_sw, hist_gx, hist_gw]
@@ -607,32 +594,30 @@
             vs(got)
             + ss(rows)
             + vs(start, w, bound_center, bound_width, level, pw, pgw, x, px, pgx, resid, diag, hist_gx, hist_gw, qgx, qgw),
-            [((con_count * var_count, 2, LANES), f32, "v"), w_like],
+            [((2, LANES), f32, "v"), w_like],
             sums,
         )
-        late = lax.all_to_all(sent, ("con", "var"), 0, 0, tiled=True)
-        con_part = vs(w, pw, pgw, start, image, bound_center, bound_width, hist_sw, hist_gw)
+        pair = sent + lax.ppermute(sent, "var", [(i, i ^ 1) for i in range(var_count)])
+        copies = jnp.broadcast_to(pair[None], (con_count * var_count // 2, 2, LANES))
+        late = lax.all_to_all(copies, ("con", "var"), 0, 0, tiled=True, axis_index_groups=one_core)
         outs = call(
             functools.partial(update_kernel, last, step),
             "update",
             vs(late, known)
             + ss(slot_order, sigma_level)
-            + vs(x, px, pgx, resid, hist_sx, hist_gx)
-            + (con_part if last else [])
+            + vs(x, px, pgx, resid, hist_sx, hist_gx, w, pw, pgw, start, image, bound_center, bound_width, hist_sw, hist_gw)
             + vs(*kept)
             + ([] if last else ss(cols_here, slot) + vs(blocks)),
-            [x_like, w_like] if last else [x_like, x_like, x_like, one_tile, ((memory + 2, problems, tile_size), f32, "v"), panel],
+            [x_like, w_like] + ([] if last else [x_like, w_like, x_like, w_like, one_tile, panel]),
             [] if last else [left],
         )
         if last:
             return outs[0], outs[1]
-        new_x, new_gx, dx, known, factors, sent = outs
+        qgx, qgw = pgx, pgw
+        px, pw = x, w
+        x, w, pgx, pgw, dx, dw, known, sent = outs
+        kept = [dx, dw]
         got = exchange(sent)
-        new_w, new_gw, dw = call(constraint_kernel, "constraints", vs(factors) + con_part, [w_like] * 3)
-        qgx, qgw = pgx, pgw
-        px, pw, pgx, pgw = x, w, new_gx, new_gw
-        x, w = new_x, new_w
-        kept = [dx, dw]
 
 
 def solution(mesh):

time: 238 us -> 220 us (0.924)
  local copies, waits for them, and re-layouts: 18.2 us -> 0.19 us
  blocking collectives: 157 us -> 165 us
  waiting for transfers between devices: 24.2 us -> 17.8 us
    all_to_all x5 -> x6, blocking collectives: 110 us -> 128 us  [exchange(): return lax.all_to_all(x, 'var', 0, 0, tiled=True)]
    unnamed x122 -> x40, local copies, waits for them, and re-layouts: 18.2 us -> 0.11 us
    all_to_all x2, blocking collectives: 47.4 us -> 36.7 us  [per_device(): lax.all_to_all(copies, ('con', 'var'), 0, 0, tiled=True, axis_index_group...]
    all_to_all x1 -> x0, waiting for transfers between devices: 7.31 us -> none  [exchange(): return lax.all_to_all(x, 'var', 0, 0, tiled=True)]
    all_to_all x1 -> x0, starting transfers between devices: 4.68 us -> none  [exchange(): return lax.all_to_all(x, 'var', 0, 0, tiled=True)]
    ppermute x0 -> x2, starting transfers between devices: none -> 4.23 us  [per_device(): lax.ppermute(sent, 'var', [(i, i ^ 1) for i in range(var_count)])]
    pallas_call x12 -> x11, Pallas kernels: 21.7 us -> 21.2 us  [call(): pl.pallas_call(kernel, out_shape=[jax.ShapeDtypeStruct(shape, dtype) for...]
  transfers between devices with their start and end apart: 9 -> 10, of which waited for: 7 -> 8; matrix products, arithmetic and copies ran while one was open for 0% -> 0% of each run, Pallas kernels for 0% -> 0%
where the time goes in v3:
time: 220 us
  blocking collectives  165 us (75%)
  Pallas kernels  21.2 us (10%)
  waiting for transfers between devices  17.8 us (8%)
  starting transfers between devices  14.6 us (7%)
    all_to_all x6, blocking collectives, exchange(): return lax.all_to_all(x, 'var', 0, 0, tiled=True)  128 us
    all_to_all x2, blocking collectives, per_device(): lax.all_to_all(copies, ('con', 'var'), 0, 0, tiled=True, axis_index_group...  36.7 us
    pallas_call x11, Pallas kernels, call(): pl.pallas_call(kernel, out_shape=[jax.ShapeDtypeStruct(shape, dtype) for...  21.2 us
    ppermute x8, waiting for transfers between devices, partner(): return lax.ppermute(x, 'con', [(i, i ^ k) for i in range(con_count)])  16.2 us
    ppermute x8, starting transfers between devices, partner(): return lax.ppermute(x, 'con', [(i, i ^ k) for i in range(con_count)])  10.4 us
  transfers between devices with their start and end apart: 10, of which 8 were waited for; matrix products, arithmetic and copies ran while one was open for 0% of the time, Pallas kernels for 0%

profile of v3, /device:TPU:1, one launch (start us, length us, event | category | flops | bytes accessed | tf_op | source)
XLA Modules:
  0.0 219.9 jit_solution(4389798189688914561)
XLA Ops:
  0.7 4.3 %open.1 = (f32[128,8,128]{2,1,0:T(8,128)S(1)}, s32[72]{0:T(128)S(1)}) custom-call(s32[1,72]{1,0:T(1,128)} %bitcast.28, s32[1,72]{1,0:T(1,128)} %bitcast.22, f32[8,4096]{1,0:T(8,128)} %refs_5_.5, f32[72,128,128]{2,1,0:T(8,128)} %bitcast.6, f32[8,4096]{1,0:T(8,128)} %refs_5_.4, f32[8,2048]{1,0:T(8,128)} %refs_11_.5, f32[8,2048]{1,0:T(8,128)} %refs_11_.4, ...), custom_call_target="tpu_custom_call" | custom-call | tf_op jit(solution)/shard_map/open/pallas_call | solution.py:448
  5.0 27.6 %all_to_all.40.refs_0_ = f32[128,8,128]{2,1,0:T(8,128)S(1)} all-to-all(f32[128,8,128]{2,1,0:T(8,128)S(1)} %get-tuple-element.27), channel_id=1, replica_groups=mesh['con'=8,'var'=32] {'var'}, dimensions={0} | all-to-all | bytes 1048576 | tf_op jit(solution)/shard_map/all_to_all | solution.py:508
  32.6 1.7 penalty_first.1
  34.3 19.0 %all_to_all.41.refs_0_ = f32[96,8,128]{2,1,0:T(8,128)S(1)} all-to-all(f32[96,8,128]{2,1,0:T(8,128)S(1)} %get-tuple-element.28), channel_id=1, replica_groups=mesh['con'=8,'var'=32] {'var'}, dimensions={0} | all-to-all | bytes 786432 | tf_op jit(solution)/shard_map/all_to_all | solution.py:508
  53.3 1.6 transpose.4
  54.9 2.8 %collective-permute-start.2 = (f32[8,4224]{1,0:T(8,128)S(1)}, f32[8,4224]{1,0:T(8,128)S(1)}, u32[]{:S(2)}, u32[]{:S(2)}) collective-permute-start(f32[8,4224]{1,0:T(8,128)S(1)} %transpose.4), channel_id=1, source_target_pairs={{0,192},{32,224},{64,128},{96,160},{128,64},{160,96},{192,0},{224,... | collective-permute-start | bytes 405512 | tf_op jit(solution)/shard_map/ppermute | solution.py:512
  58.4 2.9 %collective-permute-done.2 = f32[8,4224]{1,0:T(8,128)S(1)} collective-permute-done((f32[8,4224]{1,0:T(8,128)S(1)}, f32[8,4224]{1,0:T(8,128)S(1)}, u32[]{:S(2)}, u32[]{:S(2)}) %collective-permute-start.2) | collective-permute-done | bytes 135200 | tf_op jit(solution)/shard_map/ppermute | solution.py:512
  61.3 1.9 collective-permute-done.1
  63.2 2.5 %collective-permute-start.3 = (f32[8,4224]{1,0:T(8,128)S(1)}, f32[8,4224]{1,0:T(8,128)S(1)}, u32[]{:S(2)}, u32[]{:S(2)}) collective-permute-start(f32[8,4224]{1,0:T(8,128)S(1)} %add_add_fusion.own), channel_id=1, source_target_pairs={{0,32},{32,0},{64,96},{96,64},{128,160},{160,128},{192,224},{224,1... | collective-permute-start | bytes 405512 | tf_op jit(solution)/shard_map/ppermute | solution.py:512
  65.8 2.9 %collective-permute-done.3.other = f32[8,4224]{1,0:T(8,128)S(1)} collective-permute-done((f32[8,4224]{1,0:T(8,128)S(1)}, f32[8,4224]{1,0:T(8,128)S(1)}, u32[]{:S(2)}, u32[]{:S(2)}) %collective-permute-start.3) | collective-permute-done | bytes 135200 | tf_op jit(solution)/shard_map/ppermute | solution.py:512
  68.7 2.2 residual.2
  70.9 22.1 %all_to_all.42.got = f32[96,8,128]{2,1,0:T(8,128)S(1)} all-to-all(f32[96,8,128]{2,1,0:T(8,128)S(1)} %get-tuple-element.31), channel_id=1, replica_groups=mesh['con'=8,'var'=32] {'var'}, dimensions={0} | all-to-all | bytes 786432 | tf_op jit(solution)/shard_map/all_to_all | solution.py:508
  93.1 1.0 scalars.2
  94.0 2.1 collective-permute-start.4
  96.2 0.8 collective-permute-done.4
  97.0 19.5 %all_to_all.43.refs_0_ = f32[128,2,128]{2,1,0:T(2,128)S(1)} all-to-all(f32[128,2,128]{2,1,0:T(2,128)S(1)} %broadcast_in_dim.4), channel_id=1, replica_groups={{0,2,4,6,8,10,12,14,16,18,20,22,24,26,28,30,32,34,36,38,40,42,44,46,48,..., dimensions={0} | all-to-all | bytes 262144 | tf_op jit(solution)/shard_map/all_to_all | solution.py:602
  116.6 3.1 %update.2 = (f32[8,4096]{1,0:T(8,128)S(1)}, f32[8,2048]{1,0:T(8,128)S(1)}, f32[8,4096]{1,0:T(8,128)S(1)}, f32[8,2048]{1,0:T(8,128)S(1)}, f32[8,4096]{1,0:T(8,128...) custom-call(f32[128,2,128]{2,1,0:T(2,128)S(1)} %all_to_all.43.refs_0_, ...), custom_call_target="tpu_custom_call" | custom-call | tf_op jit(solution)/shard_map/update/pallas_call | solution.py:448
  119.7 18.5 %all_to_all.44.refs_0_ = f32[96,8,128]{2,1,0:T(8,128)S(1)} all-to-all(f32[96,8,128]{2,1,0:T(8,128)S(1)} %get-tuple-element.38), channel_id=1, replica_groups=mesh['con'=8,'var'=32] {'var'}, dimensions={0} | all-to-all | bytes 786432 | tf_op jit(solution)/shard_map/all_to_all | solution.py:508
  139.0 19.1 %all_to_all.45.refs_0_ = f32[96,8,128]{2,1,0:T(8,128)S(1)} all-to-all(f32[96,8,128]{2,1,0:T(8,128)S(1)} %get-tuple-element.40), channel_id=1, replica_groups=mesh['con'=8,'var'=32] {'var'}, dimensions={0} | all-to-all | bytes 786432 | tf_op jit(solution)/shard_map/all_to_all | solution.py:508
  158.1 1.6 transpose.5
  160.1 1.2 collective-permute-start.6
  161.3 1.7 collective-permute-start.5
  163.0 3.7 %collective-permute-done.7 = f32[8,4096]{1,0:T(8,128)S(1)} collective-permute-done((f32[8,4096]{1,0:T(8,128)S(1)}, f32[8,4096]{1,0:T(8,128)S(1)}, u32[]{:S(2)}, u32[]{:S(2)}) %collective-permute-start.7) | collective-permute-done | bytes 131104 | tf_op jit(solution)/shard_map/ppermute | solution.py:512
  167.1 1.0 collective-permute-start.8
  168.2 4.4 %collective-permute-done.8.other = f32[8,4096]{1,0:T(8,128)S(1)} collective-permute-done((f32[8,4096]{1,0:T(8,128)S(1)}, f32[8,4096]{1,0:T(8,128)S(1)}, u32[]{:S(2)}, u32[]{:S(2)}) %collective-permute-start.8) | collective-permute-done | bytes 131104 | tf_op jit(solution)/shard_map/ppermute | solution.py:512
  172.5 2.2 residual.3
  174.7 22.1 %all_to_all.46.got = f32[96,8,128]{2,1,0:T(8,128)S(1)} all-to-all(f32[96,8,128]{2,1,0:T(8,128)S(1)} %get-tuple-element.42), channel_id=1, replica_groups=mesh['con'=8,'var'=32] {'var'}, dimensions={0} | all-to-all | bytes 786432 | tf_op jit(solution)/shard_map/all_to_all | solution.py:508
  196.8 1.0 scalars.3
  197.8 2.1 collective-permute-start.9
  199.9 0.8 collective-permute-done.9
  200.8 17.2 %all_to_all.47.refs_0_ = f32[128,2,128]{2,1,0:T(2,128)S(1)} all-to-all(f32[128,2,128]{2,1,0:T(2,128)S(1)} %broadcast_in_dim.5), channel_id=1, replica_groups={{0,2,4,6,8,10,12,14,16,18,20,22,24,26,28,30,32,34,36,38,40,42,44,46,48,..., dimensions={0} | all-to-all | bytes 262144 | tf_op jit(solution)/shard_map/all_to_all | solution.py:602
  218.0 2.0 update.3
  (54 shorter events, 2.5 us)
Async XLA Ops:
  0.6 52.6 %slice-start = ((s8[4718592]{0:T(1024)(128)(4,1)}), s8[4194304]{0:T(1024)(128)(4,1)S(1)}, s32[]{:S(2)}) async-start(s8[4718592]{0:T(1024)(128)(4,1)} %bitcast.7), calls=%async_computation.8 | async-start | bytes 8388608
  0.6 31.9 %copy-start.6 = (f32[8,2048]{1,0:T(8,128)S(1)}, f32[8,2048]{1,0:T(8,128)}, u32[]{:S(2)}) copy-start(f32[8,2048]{1,0:T(8,128)} %refs_11_.5) | copy-start | bytes 196612
  0.7 31.9 %copy-start.7 = (f32[8,2048]{1,0:T(8,128)S(1)}, f32[8,2048]{1,0:T(8,128)}, u32[]{:S(2)}) copy-start(f32[8,2048]{1,0:T(8,128)} %refs_15_.3) | copy-start | bytes 196612
  0.7 31.9 %copy-start.8 = (f32[8,2048]{1,0:T(8,128)S(1)}, f32[8,2048]{1,0:T(8,128)}, u32[]{:S(2)}) copy-start(f32[8,2048]{1,0:T(8,128)} %refs_16_.3) | copy-start | bytes 196612
  0.7 31.9 %copy-start.14 = (s32[2048]{0:T(1024)S(1)}, s32[2048]{0:T(1024)}, u32[]{:S(2)}) copy-start(s32[2048]{0:T(1024)} %param.27) | copy-start | bytes 24580
  0.7 52.6 %slice-start.1 = ((s8[4718592]{0:T(1024)(128)(4,1)}), s8[524288]{0:T(1024)(128)(4,1)S(1)}, s32[]{:S(2)}) async-start(s8[4718592]{0:T(1024)(128)(4,1)} %bitcast.7), calls=%async_computation.9 | async-start | bytes 1048576
  0.7 52.6 %copy-start.15 = (s32[1,1,72]{2,1,0:T(1,128)S(1)}, s32[1,1,72]{2,1,0:T(1,128)}, u32[]{:S(2)}) copy-start(s32[1,1,72]{2,1,0:T(1,128)} %param.22) | copy-start | bytes 868
  5.0 63.7 %copy-start.3 = (f32[8,4096]{1,0:T(8,128)S(1)}, f32[8,4096]{1,0:T(8,128)}, u32[]{:S(2)}) copy-start(f32[8,4096]{1,0:T(8,128)} %refs_5_.5) | copy-start | bytes 393220
  5.0 63.7 %copy-start.12 = (f32[8,4096]{1,0:T(8,128)S(1)}, f32[8,4096]{1,0:T(8,128)}, u32[]{:S(2)}) copy-start(f32[8,4096]{1,0:T(8,128)} %linear.3) | copy-start | bytes 393220
  5.0 63.7 %copy-start.13 = (f32[4096]{0:T(1024)S(1)}, f32[4096]{0:T(1024)}, u32[]{:S(2)}) copy-start(f32[4096]{0:T(1024)} %param.23) | copy-start | bytes 49156
  53.3 39.8 %copy-start = (f32[8,8,4096]{2,1,0:T(8,128)S(1)}, f32[8,8,4096]{2,1,0:T(8,128)}, u32[]{:S(2)}) copy-start(f32[8,8,4096]{2,1,0:T(8,128)} %refs_9_.5) | copy-start | bytes 3145732
  53.3 39.8 %copy-start.1 = (f32[8,8,2048]{2,1,0:T(8,128)S(1)}, f32[8,8,2048]{2,1,0:T(8,128)}, u32[]{:S(2)}) copy-start(f32[8,8,2048]{2,1,0:T(8,128)} %refs_18_.3) | copy-start | bytes 1572868
  53.3 39.8 %copy-start.5 = (f32[8,4096]{1,0:T(8,128)S(1)}, f32[8,4096]{1,0:T(8,128)}, u32[]{:S(2)}) copy-start(f32[8,4096]{1,0:T(8,128)} %qgx.3) | copy-start | bytes 393220
  53.3 39.7 %copy-start.9 = (f32[8,2048]{1,0:T(8,128)S(1)}, f32[8,2048]{1,0:T(8,128)}, u32[]{:S(2)}) copy-start(f32[8,2048]{1,0:T(8,128)} %qgw.3) | copy-start | bytes 196612
  53.3 39.7 %copy-start.10 = (f32[8,4096]{1,0:T(8,128)S(1)}, f32[8,4096]{1,0:T(8,128)}, u32[]{:S(2)}) copy-start(f32[8,4096]{1,0:T(8,128)} %refs_5_.4) | copy-start | bytes 393220
  53.3 39.7 %copy-start.11 = (f32[8,2048]{1,0:T(8,128)S(1)}, f32[8,2048]{1,0:T(8,128)}, u32[]{:S(2)}) copy-start(f32[8,2048]{1,0:T(8,128)} %refs_11_.4) | copy-start | bytes 196612
  54.9 6.4 %collective-permute-start.2 = (f32[8,4224]{1,0:T(8,128)S(1)}, f32[8,4224]{1,0:T(8,128)S(1)}, u32[]{:S(2)}, u32[]{:S(2)}) collective-permute-start(f32[8,4224]{1,0:T(8,128)S(1)} %transpose.4), channel_id=1, source_target_pairs={{0,192},{32,224},{64,128},{96,160},{128,64},{160,96},{192,0},{224,... | collective-permute-start | bytes 405512 | tf_op jit(solution)/shard_map/ppermute | solution.py:512
  57.7 5.5 %collective-permute-start.1 = (f32[8,4224]{1,0:T(8,128)S(1)}, f32[8,4224]{1,0:T(8,128)S(1)}, u32[]{:S(2)}, u32[]{:S(2)}) collective-permute-start(f32[8,4224]{1,0:T(8,128)S(1)} %transpose.4), channel_id=1, source_target_pairs={{0,128},{32,160},{64,192},{96,224},{128,0},{160,32},{192,64},{224,... | collective-permute-start | bytes 405512 | tf_op jit(solution)/shard_map/ppermute | solution.py:512
  58.1 5.1 %collective-permute-start = (f32[8,4224]{1,0:T(8,128)S(1)}, f32[8,4224]{1,0:T(8,128)S(1)}, u32[]{:S(2)}, u32[]{:S(2)}) collective-permute-start(f32[8,4224]{1,0:T(8,128)S(1)} %transpose.4), channel_id=1, source_target_pairs={{0,64},{32,96},{64,0},{96,32},{128,192},{160,224},{192,128},{224,1... | collective-permute-start | bytes 405512 | tf_op jit(solution)/shard_map/ppermute | solution.py:512
  63.2 5.5 %collective-permute-start.3 = (f32[8,4224]{1,0:T(8,128)S(1)}, f32[8,4224]{1,0:T(8,128)S(1)}, u32[]{:S(2)}, u32[]{:S(2)}) collective-permute-start(f32[8,4224]{1,0:T(8,128)S(1)} %add_add_fusion.own), channel_id=1, source_target_pairs={{0,32},{32,0},{64,96},{96,64},{128,160},{160,128},{192,224},{224,1... | collective-permute-start | bytes 405512 | tf_op jit(solution)/shard_map/ppermute | solution.py:512
  68.7 47.9 %copy-start.2 = (f32[8,8,4096]{2,1,0:T(8,128)S(1)}, f32[8,8,4096]{2,1,0:T(8,128)}, u32[]{:S(2)}) copy-start(f32[8,8,4096]{2,1,0:T(8,128)} %refs_8_.5) | copy-start | bytes 3145732
  68.7 47.9 %copy-start.4 = (f32[8,8,2048]{2,1,0:T(8,128)S(1)}, f32[8,8,2048]{2,1,0:T(8,128)}, u32[]{:S(2)}) copy-start(f32[8,8,2048]{2,1,0:T(8,128)} %refs_17_.3) | copy-start | bytes 1572868
  68.7 47.9 %copy-start.16 = (s32[8]{0:T(128)S(1)}, s32[8]{0:T(128)}, u32[]{:S(2)}) copy-start(s32[8]{0:T(128)} %refs_2_.7) | copy-start | bytes 100
  68.7 47.9 %copy-start.17 = (s32[8]{0:T(128)S(1)}, s32[8]{0:T(128)}, u32[]{:S(2)}) copy-start(s32[8]{0:T(128)} %refs_3_.7) | copy-start | bytes 100
  94.0 2.9 %collective-permute-start.4 = (f32[2,128]{1,0:T(2,128)S(1)}, f32[2,128]{1,0:T(2,128)S(1)}, u32[]{:S(2)}, u32[]{:S(2)}) collective-permute-start(f32[2,128]{1,0:T(2,128)S(1)} %get-tuple-element.35), channel_id=1, source_target_pairs={{0,1},{1,0},{2,3},{3,2},{4,5},{5,4},{6,7},{7,6},{8,9},{9,8},{10,11... | collective-permute-start | bytes 3080 | tf_op jit(solution)/shard_map/ppermute | solution.py:600
  159.6 7.1 %collective-permute-start.7 = (f32[8,4096]{1,0:T(8,128)S(1)}, f32[8,4096]{1,0:T(8,128)S(1)}, u32[]{:S(2)}, u32[]{:S(2)}) collective-permute-start(f32[8,4096]{1,0:T(8,128)S(1)} %transpose.5), channel_id=1, source_target_pairs={{0,192},{32,224},{64,128},{96,160},{128,64},{160,96},{192,0},{224,... | collective-permute-start | bytes 393224 | tf_op jit(solution)/shard_map/ppermute | solution.py:512
  160.1 6.6 %collective-permute-start.6 = (f32[8,4096]{1,0:T(8,128)S(1)}, f32[8,4096]{1,0:T(8,128)S(1)}, u32[]{:S(2)}, u32[]{:S(2)}) collective-permute-start(f32[8,4096]{1,0:T(8,128)S(1)} %transpose.5), channel_id=1, source_target_pairs={{0,128},{32,160},{64,192},{96,224},{128,0},{160,32},{192,64},{224,... | collective-permute-start | bytes 393224 | tf_op jit(solution)/shard_map/ppermute | solution.py:512
  161.3 5.8 %collective-permute-start.5 = (f32[8,4096]{1,0:T(8,128)S(1)}, f32[8,4096]{1,0:T(8,128)S(1)}, u32[]{:S(2)}, u32[]{:S(2)}) collective-permute-start(f32[8,4096]{1,0:T(8,128)S(1)} %transpose.5), channel_id=1, source_target_pairs={{0,64},{32,96},{64,0},{96,32},{128,192},{160,224},{192,128},{224,1... | collective-permute-start | bytes 393224 | tf_op jit(solution)/shard_map/ppermute | solution.py:512
  167.1 5.4 %collective-permute-start.8 = (f32[8,4096]{1,0:T(8,128)S(1)}, f32[8,4096]{1,0:T(8,128)S(1)}, u32[]{:S(2)}, u32[]{:S(2)}) collective-permute-start(f32[8,4096]{1,0:T(8,128)S(1)} %add_add_fusion.1.own), channel_id=1, source_target_pairs={{0,32},{32,0},{64,96},{96,64},{128,160},{160,128},{192,224},{224,1... | collective-permute-start | bytes 393224 | tf_op jit(solution)/shard_map/ppermute | solution.py:512
  197.8 2.9 %collective-permute-start.9 = (f32[2,128]{1,0:T(2,128)S(1)}, f32[2,128]{1,0:T(2,128)S(1)}, u32[]{:S(2)}, u32[]{:S(2)}) collective-permute-start(f32[2,128]{1,0:T(2,128)S(1)} %get-tuple-element.47), channel_id=1, source_target_pairs={{0,1},{1,0},{2,3},{3,2},{4,5},{5,4},{6,7},{7,6},{8,9},{9,8},{10,11... | collective-permute-start | bytes 3080 | tf_op jit(solution)/shard_map/ppermute | solution.py:600

commit v4 on v3

--- a/solution.py
+++ b/solution.py
@@ -9,7 +9,7 @@
 
 STEPS = 2
 LANES = 128
-UNROLL = 24
+UNROLL = 72
 
 relax = 1.6
 ridge = 0.01
@@ -49,6 +49,11 @@
 def tile_loop(count, body):
     step = max(d for d in range(1, UNROLL + 1) if count % d == 0)
 
+    if step == count:
+        for j in range(count):
+            body(j)
+        return
+
     def some(i, _):
         for j in range(step):
             body(i * step + j)
@@ -105,7 +110,7 @@
 
 def open_kernel(per_run, run_length, share, parts, *refs):
     (hbm_rows, hbm_cols, hbm_x, hbm_tiles, *far), (send, slot), refs = refs[:13], refs[13:15], refs[15:]
-    rows_buf, cols_buf, x, tiles, px, w, pw, pgx, pgw, hsx, hsw, hgx, hgw, left, count, asked, sem = refs
+    rows_buf, cols_buf, x, tiles, px, w, pw, pgx, pgw, hsx, hsw, hgx, hgw, left, count, asked, spot, sem = refs
     memory = hgx.shape[0]
     problems = x.shape[0]
     runs = send.shape[0] // (per_run + 1)
@@ -123,33 +128,24 @@
         copy.start()
     rows, cols = rows_buf.at[0], cols_buf.at[0]
 
-    def clear(i, _):
+    for i in range(runs):
         count[i] = 0
-        return 0
-
-    lax.fori_loop(0, runs, clear, 0)
-
-    def clear_asked(i, _):
+    for i in range(runs * per_run):
         asked[i] = 0
-        return 0
-
-    lax.fori_loop(0, runs * per_run, clear_asked, 0)
     copies[0].wait()
     copies[1].wait()
-
-    def assign(t, _):
-        owner = rows[t] // run_length
+    for t in range(tiles.shape[0]):
+        row = rows[t]
+        owner = row >> (run_length.bit_length() - 1)
         rank = count[owner]
         count[owner] = rank + 1
-        slot[t] = owner * per_run + rank
-        asked[owner * per_run + rank] = rows[t] - owner * run_length
-        return 0
-
-    lax.fori_loop(0, tiles.shape[0], assign, 0)
+        place = owner * per_run + rank
+        slot[t] = place
+        spot[t] = place + owner
+        asked[place] = row & (run_length - 1)
 
     def where(t):
-        owner = slot[t] // per_run
-        return slot[t] + owner
+        return spot[t]
 
     copies[2].wait()
     send_products(x, cols, where, tiles, send, left, [copy.wait for copy in copies[3 : 3 + parts]])
@@ -186,11 +182,18 @@
             return h * h
 
         out = jnp.where(lanes == memory * (memory + 1) + m, both(square), out)
+    index = entry_ids(runs * per_run, problems) - lax.axis_index("var") * per_run
     for r in range(runs):
         mark = out
-        for s in range(per_run):
-            mark = jnp.where(lanes == LANES - per_run + s, asked[r * per_run + s].astype(f32), mark)
+        for i in range(per_run):
+            mark = jnp.where(index == i, asked[r * per_run + i].astype(f32), mark)
         send[r * wide + per_run] = mark
+
+
+def entry_ids(entries, problems):
+    shape = (problems, LANES)
+    base = LANES - -(-entries // problems)
+    return (lane_ids(shape) - base) * problems + lax.broadcasted_iota(jnp.int32, shape, 0)
 
 
 def penalty_kernel(first, per_run, *refs):
@@ -202,17 +205,16 @@
     runs = slots // per_run
     if first:
         wide = per_run + 1
-        early_sum = None
-        for r in range(runs):
-            side = got[r * wide + per_run]
-            early_sum = side if early_sum is None else early_sum + side
-            marks_int[r : r + 1, :] = side[:1].astype(jnp.int32)
+        early_sum = functools.reduce(lambda p, q: p + q, [got[r * wide + per_run] for r in range(runs)])
         early[...] = early_sum
+        marks_int[...] = early_sum.astype(jnp.int32)
         copy = pltpu.make_async_copy(marks_int, marks, sem)
         copy.start()
         copy.wait()
+        problems = w.shape[0]
+        base = LANES - -(-slots // problems)
         for s in range(slots):
-            rows[s] = marks[s // per_run, LANES - per_run + s % per_run]
+            rows[s] = marks[s % problems, base + s // problems]
         result = add_rows(got, lambda s: s // per_run * wide + s % per_run, rows, runs, sums)
     else:
         result = add_rows(got, lambda s: s, rows, runs, sums)
@@ -300,7 +302,7 @@
         add(C_C, at(diag, b) * r * r)
         terms(-p, relax * r, p, at(x, b) - at(px, b), p - at(qgx, b), lambda m: hgx[m, :, pl.ds(pl.multiple_of(b * LANES, LANES), LANES)])
     lanes = lane_ids((problems, LANES))
-    lane_of = 16 * lax.broadcasted_iota(jnp.int32, (problems, LANES), 0)
+    lane_of = (LANES - 16 * lax.broadcasted_iota(jnp.int32, (problems, LANES), 0)) & (LANES - 1)
     packed = []
     for row in range(2):
         tile = jnp.zeros((problems, LANES), f32)
@@ -333,10 +335,12 @@
         chains[i % 8] = chains[i % 8] + late[i]
     rows = functools.reduce(lambda p, q: p + q, chains)
 
+    aligned = [
+        pltpu.roll(jnp.broadcast_to(rows[i : i + 1], shape), 0, 1, stride=16, stride_axis=0) for i in range(2)
+    ]
+
     def scalar(i):
-        row = jnp.broadcast_to(rows[i // 16 : i // 16 + 1], shape)
-        picked = jnp.where(lanes == program * 16 + i % 16, row, 0.0)
-        return jnp.broadcast_to(total(picked), shape)
+        return jnp.broadcast_to(aligned[i // 16][:, i % 16 : i % 16 + 1], shape)
 
     def given(i):
         return jnp.broadcast_to(known[:, i : i + 1], shape)
@@ -539,6 +543,7 @@
             left,
             pltpu.SMEM((var_count,), jnp.int32),
             pltpu.SMEM((slots,), jnp.int32),
+            pltpu.SMEM((count,), jnp.int32),
             pltpu.SemaphoreType.DMA((3 + parts + 9,)),
         ],
     )
@@ -555,7 +560,7 @@
                 "penalty_first",
                 vs(got, w, bound_center, bound_width, level),
                 [panel, w_like, one_tile, ((slots,), jnp.int32, "s")],
-                [pltpu.SMEM((var_count, tile_size), jnp.int32), pltpu.VMEM((var_count, tile_size), jnp.int32), pltpu.SemaphoreType.DMA(())]
+                [pltpu.SMEM((problems, tile_size), jnp.int32), pltpu.VMEM((problems, tile_size), jnp.int32), pltpu.SemaphoreType.DMA(())]
                 + sums,
             )
         else:

time: 220 us -> 218 us (level)
  no operation moved by 1% of the time
where the time goes in v4:
time: 218 us
  blocking collectives  165 us (76%)
  Pallas kernels  19.2 us (9%)
  waiting for transfers between devices  17.9 us (8%)
  starting transfers between devices  14.6 us (7%)
    all_to_all x6, blocking collectives, exchange(): return lax.all_to_all(x, 'var', 0, 0, tiled=True)  128 us
    all_to_all x2, blocking collectives, per_device(): lax.all_to_all(copies, ('con', 'var'), 0, 0, tiled=True, axis_index_group...  36.7 us
    pallas_call x11, Pallas kernels, call(): pl.pallas_call(kernel, out_shape=[jax.ShapeDtypeStruct(shape, dtype) for...  19.2 us
    ppermute x8, waiting for transfers between devices, partner(): return lax.ppermute(x, 'con', [(i, i ^ k) for i in range(con_count)])  16.2 us
    ppermute x8, starting transfers between devices, partner(): return lax.ppermute(x, 'con', [(i, i ^ k) for i in range(con_count)])  10.4 us
  transfers between devices with their start and end apart: 10, of which 8 were waited for; matrix products, arithmetic and copies ran while one was open for 0% of the time, Pallas kernels for 0%

profile of v4, /device:TPU:1, one launch (start us, length us, event | category | flops | bytes accessed | tf_op | source)
XLA Modules:
  0.0 217.7 jit_solution(8134404765116629743)
XLA Ops:
  0.7 4.0 %open.1 = (f32[128,8,128]{2,1,0:T(8,128)S(1)}, s32[72]{0:T(128)S(1)}) custom-call(s32[1,72]{1,0:T(1,128)} %bitcast.28, s32[1,72]{1,0:T(1,128)} %bitcast.22, f32[8,4096]{1,0:T(8,128)} %refs_5_.5, f32[72,128,128]{2,1,0:T(8,128)} %bitcast.6, f32[8,4096]{1,0:T(8,128)} %refs_5_.4, f32[8,2048]{1,0:T(8,128)} %refs_11_.5, f32[8,2048]{1,0:T(8,128)} %refs_11_.4, ...), custom_call_target="tpu_custom_call" | custom-call | tf_op jit(solution)/shard_map/open/pallas_call | solution.py:452
  4.8 27.6 %all_to_all.40.refs_0_ = f32[128,8,128]{2,1,0:T(8,128)S(1)} all-to-all(f32[128,8,128]{2,1,0:T(8,128)S(1)} %get-tuple-element.27), channel_id=1, replica_groups=mesh['con'=8,'var'=32] {'var'}, dimensions={0} | all-to-all | bytes 1048576 | tf_op jit(solution)/shard_map/all_to_all | solution.py:512
  32.3 1.5 penalty_first.1
  33.8 19.0 %all_to_all.41.refs_0_ = f32[96,8,128]{2,1,0:T(8,128)S(1)} all-to-all(f32[96,8,128]{2,1,0:T(8,128)S(1)} %get-tuple-element.28), channel_id=1, replica_groups=mesh['con'=8,'var'=32] {'var'}, dimensions={0} | all-to-all | bytes 786432 | tf_op jit(solution)/shard_map/all_to_all | solution.py:512
  52.9 1.3 transpose.4
  54.2 2.8 %collective-permute-start.2 = (f32[8,4224]{1,0:T(8,128)S(1)}, f32[8,4224]{1,0:T(8,128)S(1)}, u32[]{:S(2)}, u32[]{:S(2)}) collective-permute-start(f32[8,4224]{1,0:T(8,128)S(1)} %transpose.4), channel_id=1, source_target_pairs={{0,192},{32,224},{64,128},{96,160},{128,64},{160,96},{192,0},{224,... | collective-permute-start | bytes 405512 | tf_op jit(solution)/shard_map/ppermute | solution.py:516
  57.7 2.9 %collective-permute-done.2 = f32[8,4224]{1,0:T(8,128)S(1)} collective-permute-done((f32[8,4224]{1,0:T(8,128)S(1)}, f32[8,4224]{1,0:T(8,128)S(1)}, u32[]{:S(2)}, u32[]{:S(2)}) %collective-permute-start.2) | collective-permute-done | bytes 135200 | tf_op jit(solution)/shard_map/ppermute | solution.py:516
  60.6 1.9 collective-permute-done.1
  62.5 2.5 %collective-permute-start.3 = (f32[8,4224]{1,0:T(8,128)S(1)}, f32[8,4224]{1,0:T(8,128)S(1)}, u32[]{:S(2)}, u32[]{:S(2)}) collective-permute-start(f32[8,4224]{1,0:T(8,128)S(1)} %add_add_fusion.own), channel_id=1, source_target_pairs={{0,32},{32,0},{64,96},{96,64},{128,160},{160,128},{192,224},{224,1... | collective-permute-start | bytes 405512 | tf_op jit(solution)/shard_map/ppermute | solution.py:516
  65.1 2.9 %collective-permute-done.3.other = f32[8,4224]{1,0:T(8,128)S(1)} collective-permute-done((f32[8,4224]{1,0:T(8,128)S(1)}, f32[8,4224]{1,0:T(8,128)S(1)}, u32[]{:S(2)}, u32[]{:S(2)}) %collective-permute-start.3) | collective-permute-done | bytes 135200 | tf_op jit(solution)/shard_map/ppermute | solution.py:516
  68.0 1.9 residual.2
  70.0 22.1 %all_to_all.42.got = f32[96,8,128]{2,1,0:T(8,128)S(1)} all-to-all(f32[96,8,128]{2,1,0:T(8,128)S(1)} %get-tuple-element.31), channel_id=1, replica_groups=mesh['con'=8,'var'=32] {'var'}, dimensions={0} | all-to-all | bytes 786432 | tf_op jit(solution)/shard_map/all_to_all | solution.py:512
  92.1 1.0 scalars.2
  93.1 2.1 collective-permute-start.4
  95.2 0.8 collective-permute-done.4
  96.1 19.6 %all_to_all.43.refs_0_ = f32[128,2,128]{2,1,0:T(2,128)S(1)} all-to-all(f32[128,2,128]{2,1,0:T(2,128)S(1)} %broadcast_in_dim.4), channel_id=1, replica_groups={{0,2,4,6,8,10,12,14,16,18,20,22,24,26,28,30,32,34,36,38,40,42,44,46,48,..., dimensions={0} | all-to-all | bytes 262144 | tf_op jit(solution)/shard_map/all_to_all | solution.py:607
  115.6 2.6 %update.2 = (f32[8,4096]{1,0:T(8,128)S(1)}, f32[8,2048]{1,0:T(8,128)S(1)}, f32[8,4096]{1,0:T(8,128)S(1)}, f32[8,2048]{1,0:T(8,128)S(1)}, f32[8,4096]{1,0:T(8,128...) custom-call(f32[128,2,128]{2,1,0:T(2,128)S(1)} %all_to_all.43.refs_0_, ...), custom_call_target="tpu_custom_call" | custom-call | tf_op jit(solution)/shard_map/update/pallas_call | solution.py:452
  118.3 18.5 %all_to_all.44.refs_0_ = f32[96,8,128]{2,1,0:T(8,128)S(1)} all-to-all(f32[96,8,128]{2,1,0:T(8,128)S(1)} %get-tuple-element.38), channel_id=1, replica_groups=mesh['con'=8,'var'=32] {'var'}, dimensions={0} | all-to-all | bytes 786432 | tf_op jit(solution)/shard_map/all_to_all | solution.py:512
  137.6 18.9 %all_to_all.45.refs_0_ = f32[96,8,128]{2,1,0:T(8,128)S(1)} all-to-all(f32[96,8,128]{2,1,0:T(8,128)S(1)} %get-tuple-element.40), channel_id=1, replica_groups=mesh['con'=8,'var'=32] {'var'}, dimensions={0} | all-to-all | bytes 786432 | tf_op jit(solution)/shard_map/all_to_all | solution.py:512
  156.5 1.3 transpose.5
  158.2 1.2 collective-permute-start.6
  159.4 1.7 collective-permute-start.5
  161.1 3.7 %collective-permute-done.7 = f32[8,4096]{1,0:T(8,128)S(1)} collective-permute-done((f32[8,4096]{1,0:T(8,128)S(1)}, f32[8,4096]{1,0:T(8,128)S(1)}, u32[]{:S(2)}, u32[]{:S(2)}) %collective-permute-start.7) | collective-permute-done | bytes 131104 | tf_op jit(solution)/shard_map/ppermute | solution.py:516
  165.3 1.0 collective-permute-start.8
  166.3 4.4 %collective-permute-done.8.other = f32[8,4096]{1,0:T(8,128)S(1)} collective-permute-done((f32[8,4096]{1,0:T(8,128)S(1)}, f32[8,4096]{1,0:T(8,128)S(1)}, u32[]{:S(2)}, u32[]{:S(2)}) %collective-permute-start.8) | collective-permute-done | bytes 131104 | tf_op jit(solution)/shard_map/ppermute | solution.py:516
  170.7 1.9 residual.3
  172.6 22.1 %all_to_all.46.got = f32[96,8,128]{2,1,0:T(8,128)S(1)} all-to-all(f32[96,8,128]{2,1,0:T(8,128)S(1)} %get-tuple-element.42), channel_id=1, replica_groups=mesh['con'=8,'var'=32] {'var'}, dimensions={0} | all-to-all | bytes 786432 | tf_op jit(solution)/shard_map/all_to_all | solution.py:512
  194.7 1.0 scalars.3
  195.7 2.1 collective-permute-start.9
  197.8 0.8 collective-permute-done.9
  198.6 17.2 %all_to_all.47.refs_0_ = f32[128,2,128]{2,1,0:T(2,128)S(1)} all-to-all(f32[128,2,128]{2,1,0:T(2,128)S(1)} %broadcast_in_dim.5), channel_id=1, replica_groups={{0,2,4,6,8,10,12,14,16,18,20,22,24,26,28,30,32,34,36,38,40,42,44,46,48,..., dimensions={0} | all-to-all | bytes 262144 | tf_op jit(solution)/shard_map/all_to_all | solution.py:607
  215.8 1.9 update.3
  (54 shorter events, 2.6 us)
Async XLA Ops:
  0.6 52.2 %slice-start = ((s8[4718592]{0:T(1024)(128)(4,1)}), s8[4194304]{0:T(1024)(128)(4,1)S(1)}, s32[]{:S(2)}) async-start(s8[4718592]{0:T(1024)(128)(4,1)} %bitcast.7), calls=%async_computation.8 | async-start | bytes 8388608
  0.6 31.7 %copy-start.6 = (f32[8,2048]{1,0:T(8,128)S(1)}, f32[8,2048]{1,0:T(8,128)}, u32[]{:S(2)}) copy-start(f32[8,2048]{1,0:T(8,128)} %refs_11_.5) | copy-start | bytes 196612
  0.7 31.7 %copy-start.7 = (f32[8,2048]{1,0:T(8,128)S(1)}, f32[8,2048]{1,0:T(8,128)}, u32[]{:S(2)}) copy-start(f32[8,2048]{1,0:T(8,128)} %refs_15_.3) | copy-start | bytes 196612
  0.7 31.7 %copy-start.8 = (f32[8,2048]{1,0:T(8,128)S(1)}, f32[8,2048]{1,0:T(8,128)}, u32[]{:S(2)}) copy-start(f32[8,2048]{1,0:T(8,128)} %refs_16_.3) | copy-start | bytes 196612
  0.7 31.6 %copy-start.14 = (s32[2048]{0:T(1024)S(1)}, s32[2048]{0:T(1024)}, u32[]{:S(2)}) copy-start(s32[2048]{0:T(1024)} %param.27) | copy-start | bytes 24580
  0.7 52.1 %slice-start.1 = ((s8[4718592]{0:T(1024)(128)(4,1)}), s8[524288]{0:T(1024)(128)(4,1)S(1)}, s32[]{:S(2)}) async-start(s8[4718592]{0:T(1024)(128)(4,1)} %bitcast.7), calls=%async_computation.9 | async-start | bytes 1048576
  0.7 52.1 %copy-start.15 = (s32[1,1,72]{2,1,0:T(1,128)S(1)}, s32[1,1,72]{2,1,0:T(1,128)}, u32[]{:S(2)}) copy-start(s32[1,1,72]{2,1,0:T(1,128)} %param.22) | copy-start | bytes 868
  4.7 63.3 %copy-start.3 = (f32[8,4096]{1,0:T(8,128)S(1)}, f32[8,4096]{1,0:T(8,128)}, u32[]{:S(2)}) copy-start(f32[8,4096]{1,0:T(8,128)} %refs_5_.5) | copy-start | bytes 393220
  4.7 63.2 %copy-start.12 = (f32[8,4096]{1,0:T(8,128)S(1)}, f32[8,4096]{1,0:T(8,128)}, u32[]{:S(2)}) copy-start(f32[8,4096]{1,0:T(8,128)} %linear.3) | copy-start | bytes 393220
  4.7 63.2 %copy-start.13 = (f32[4096]{0:T(1024)S(1)}, f32[4096]{0:T(1024)}, u32[]{:S(2)}) copy-start(f32[4096]{0:T(1024)} %param.23) | copy-start | bytes 49156
  52.8 39.2 %copy-start = (f32[8,8,4096]{2,1,0:T(8,128)S(1)}, f32[8,8,4096]{2,1,0:T(8,128)}, u32[]{:S(2)}) copy-start(f32[8,8,4096]{2,1,0:T(8,128)} %refs_9_.5) | copy-start | bytes 3145732
  52.8 39.2 %copy-start.1 = (f32[8,8,2048]{2,1,0:T(8,128)S(1)}, f32[8,8,2048]{2,1,0:T(8,128)}, u32[]{:S(2)}) copy-start(f32[8,8,2048]{2,1,0:T(8,128)} %refs_18_.3) | copy-start | bytes 1572868
  52.8 39.2 %copy-start.5 = (f32[8,4096]{1,0:T(8,128)S(1)}, f32[8,4096]{1,0:T(8,128)}, u32[]{:S(2)}) copy-start(f32[8,4096]{1,0:T(8,128)} %qgx.3) | copy-start | bytes 393220
  52.8 39.2 %copy-start.9 = (f32[8,2048]{1,0:T(8,128)S(1)}, f32[8,2048]{1,0:T(8,128)}, u32[]{:S(2)}) copy-start(f32[8,2048]{1,0:T(8,128)} %qgw.3) | copy-start | bytes 196612
  52.9 39.2 %copy-start.10 = (f32[8,4096]{1,0:T(8,128)S(1)}, f32[8,4096]{1,0:T(8,128)}, u32[]{:S(2)}) copy-start(f32[8,4096]{1,0:T(8,128)} %refs_5_.4) | copy-start | bytes 393220
  52.9 39.2 %copy-start.11 = (f32[8,2048]{1,0:T(8,128)S(1)}, f32[8,2048]{1,0:T(8,128)}, u32[]{:S(2)}) copy-start(f32[8,2048]{1,0:T(8,128)} %refs_11_.4) | copy-start | bytes 196612
  54.2 6.4 %collective-permute-start.2 = (f32[8,4224]{1,0:T(8,128)S(1)}, f32[8,4224]{1,0:T(8,128)S(1)}, u32[]{:S(2)}, u32[]{:S(2)}) collective-permute-start(f32[8,4224]{1,0:T(8,128)S(1)} %transpose.4), channel_id=1, source_target_pairs={{0,192},{32,224},{64,128},{96,160},{128,64},{160,96},{192,0},{224,... | collective-permute-start | bytes 405512 | tf_op jit(solution)/shard_map/ppermute | solution.py:516
  57.0 5.5 %collective-permute-start.1 = (f32[8,4224]{1,0:T(8,128)S(1)}, f32[8,4224]{1,0:T(8,128)S(1)}, u32[]{:S(2)}, u32[]{:S(2)}) collective-permute-start(f32[8,4224]{1,0:T(8,128)S(1)} %transpose.4), channel_id=1, source_target_pairs={{0,128},{32,160},{64,192},{96,224},{128,0},{160,32},{192,64},{224,... | collective-permute-start | bytes 405512 | tf_op jit(solution)/shard_map/ppermute | solution.py:516
  57.4 5.1 %collective-permute-start = (f32[8,4224]{1,0:T(8,128)S(1)}, f32[8,4224]{1,0:T(8,128)S(1)}, u32[]{:S(2)}, u32[]{:S(2)}) collective-permute-start(f32[8,4224]{1,0:T(8,128)S(1)} %transpose.4), channel_id=1, source_target_pairs={{0,64},{32,96},{64,0},{96,32},{128,192},{160,224},{192,128},{224,1... | collective-permute-start | bytes 405512 | tf_op jit(solution)/shard_map/ppermute | solution.py:516
  62.5 5.5 %collective-permute-start.3 = (f32[8,4224]{1,0:T(8,128)S(1)}, f32[8,4224]{1,0:T(8,128)S(1)}, u32[]{:S(2)}, u32[]{:S(2)}) collective-permute-start(f32[8,4224]{1,0:T(8,128)S(1)} %add_add_fusion.own), channel_id=1, source_target_pairs={{0,32},{32,0},{64,96},{96,64},{128,160},{160,128},{192,224},{224,1... | collective-permute-start | bytes 405512 | tf_op jit(solution)/shard_map/ppermute | solution.py:516
  68.0 47.6 %copy-start.2 = (f32[8,8,4096]{2,1,0:T(8,128)S(1)}, f32[8,8,4096]{2,1,0:T(8,128)}, u32[]{:S(2)}) copy-start(f32[8,8,4096]{2,1,0:T(8,128)} %refs_8_.5) | copy-start | bytes 3145732
  68.0 47.6 %copy-start.4 = (f32[8,8,2048]{2,1,0:T(8,128)S(1)}, f32[8,8,2048]{2,1,0:T(8,128)}, u32[]{:S(2)}) copy-start(f32[8,8,2048]{2,1,0:T(8,128)} %refs_17_.3) | copy-start | bytes 1572868
  68.0 47.6 %copy-start.16 = (s32[8]{0:T(128)S(1)}, s32[8]{0:T(128)}, u32[]{:S(2)}) copy-start(s32[8]{0:T(128)} %refs_2_.7) | copy-start | bytes 100
  68.0 47.6 %copy-start.17 = (s32[8]{0:T(128)S(1)}, s32[8]{0:T(128)}, u32[]{:S(2)}) copy-start(s32[8]{0:T(128)} %refs_3_.7) | copy-start | bytes 100
  93.1 2.9 %collective-permute-start.4 = (f32[2,128]{1,0:T(2,128)S(1)}, f32[2,128]{1,0:T(2,128)S(1)}, u32[]{:S(2)}, u32[]{:S(2)}) collective-permute-start(f32[2,128]{1,0:T(2,128)S(1)} %get-tuple-element.35), channel_id=1, source_target_pairs={{0,1},{1,0},{2,3},{3,2},{4,5},{5,4},{6,7},{7,6},{8,9},{9,8},{10,11... | collective-permute-start | bytes 3080 | tf_op jit(solution)/shard_map/ppermute | solution.py:605
  157.8 7.1 %collective-permute-start.7 = (f32[8,4096]{1,0:T(8,128)S(1)}, f32[8,4096]{1,0:T(8,128)S(1)}, u32[]{:S(2)}, u32[]{:S(2)}) collective-permute-start(f32[8,4096]{1,0:T(8,128)S(1)} %transpose.5), channel_id=1, source_target_pairs={{0,192},{32,224},{64,128},{96,160},{128,64},{160,96},{192,0},{224,... | collective-permute-start | bytes 393224 | tf_op jit(solution)/shard_map/ppermute | solution.py:516
  158.2 6.6 %collective-permute-start.6 = (f32[8,4096]{1,0:T(8,128)S(1)}, f32[8,4096]{1,0:T(8,128)S(1)}, u32[]{:S(2)}, u32[]{:S(2)}) collective-permute-start(f32[8,4096]{1,0:T(8,128)S(1)} %transpose.5), channel_id=1, source_target_pairs={{0,128},{32,160},{64,192},{96,224},{128,0},{160,32},{192,64},{224,... | collective-permute-start | bytes 393224 | tf_op jit(solution)/shard_map/ppermute | solution.py:516
  159.4 5.8 %collective-permute-start.5 = (f32[8,4096]{1,0:T(8,128)S(1)}, f32[8,4096]{1,0:T(8,128)S(1)}, u32[]{:S(2)}, u32[]{:S(2)}) collective-permute-start(f32[8,4096]{1,0:T(8,128)S(1)} %transpose.5), channel_id=1, source_target_pairs={{0,64},{32,96},{64,0},{96,32},{128,192},{160,224},{192,128},{224,1... | collective-permute-start | bytes 393224 | tf_op jit(solution)/shard_map/ppermute | solution.py:516
  165.3 5.4 %collective-permute-start.8 = (f32[8,4096]{1,0:T(8,128)S(1)}, f32[8,4096]{1,0:T(8,128)S(1)}, u32[]{:S(2)}, u32[]{:S(2)}) collective-permute-start(f32[8,4096]{1,0:T(8,128)S(1)} %add_add_fusion.1.own), channel_id=1, source_target_pairs={{0,32},{32,0},{64,96},{96,64},{128,160},{160,128},{192,224},{224,1... | collective-permute-start | bytes 393224 | tf_op jit(solution)/shard_map/ppermute | solution.py:516
  195.7 2.9 %collective-permute-start.9 = (f32[2,128]{1,0:T(2,128)S(1)}, f32[2,128]{1,0:T(2,128)S(1)}, u32[]{:S(2)}, u32[]{:S(2)}) collective-permute-start(f32[2,128]{1,0:T(2,128)S(1)} %get-tuple-element.47), channel_id=1, source_target_pairs={{0,1},{1,0},{2,3},{3,2},{4,5},{5,4},{6,7},{7,6},{8,9},{9,8},{10,11... | collective-permute-start | bytes 3080 | tf_op jit(solution)/shard_map/ppermute | solution.py:605

commit v5 on v4

--- a/solution.py
+++ b/solution.py
@@ -66,14 +66,14 @@
     return lax.broadcasted_iota(jnp.int32, shape, len(shape) - 1)
 
 
-def send_products(x_ref, cols, where, tiles, send, left, waits=(None,)):
+def send_products(x_ref, cols, where, tiles, send, left, waits=(None,), flipped=True):
     for block in range(x_ref.shape[1] // LANES):
         left[block] = stacked(x_ref[:, block * LANES : (block + 1) * LANES])
     send[...] = jnp.zeros_like(send)
 
     def one(t):
-        high, low = halves(tiles[t])
-        send[where(t)] = times(left[cols[t]], jnp.concatenate([high, low], axis=1), 1)
+        axis = 0 if flipped else 1
+        send[where(t)] = times(left[cols[t]], jnp.concatenate(halves(tiles[t]), axis=axis), axis)
 
     size = tiles.shape[0] // len(waits)
     for i, wait in enumerate(waits):
@@ -148,7 +148,7 @@
         return spot[t]
 
     copies[2].wait()
-    send_products(x, cols, where, tiles, send, left, [copy.wait for copy in copies[3 : 3 + parts]])
+    send_products(x, cols, where, tiles, send, left, [copy.wait for copy in copies[3 : 3 + parts]], flipped=False)
     for copy in copies[3 + parts :]:
         copy.wait()
 
@@ -251,6 +251,13 @@
         send[:, columns * LANES :] = early[...]
 
 
+def prepare_kernel(tiles, hsx, hgx, hsw, hgw, _, flipped, hx, hw):
+    tile_loop(tiles.shape[0], lambda t: flipped.__setitem__(t, tiles[t].T))
+    for m in range(hx.shape[0]):
+        hx[m] = hsx[m] + hgx[m]
+        hw[m] = hsw[m] + hgw[m]
+
+
 def residual_kernel(first, own, other, x, linear, diag, cols, slot, tiles, send, resid, *refs):
     columns = x.shape[1] // LANES
     if first:
@@ -315,9 +322,9 @@
 
 
 def update_kernel(last, steps_before, *refs):
-    (late, known, order, sigma_level, x, px, pgx, resid, hsx, hgx) = refs[:10]
-    (w, pw, pgw, start, image, center, width, hsw, hgw) = refs[10:19]
-    refs = refs[19:]
+    (late, known, order, sigma_level, x, px, pgx, resid, hx) = refs[:9]
+    (w, pw, pgw, start, image, center, width, hw) = refs[9:17]
+    refs = refs[17:]
     if steps_before:
         dx, dw = refs[:2]
         refs = refs[2:]
@@ -326,12 +333,12 @@
     else:
         cols, slot, tiles, x_out, w_out, gx_out, gw_out, dx_out, dw_out, known_out, send, left = refs
     problems = x.shape[0]
-    memory = hgx.shape[0]
+    memory = hx.shape[0]
     shape = (problems, LANES)
     lanes = lane_ids(shape)
     program = lax.broadcasted_iota(jnp.int32, shape, 0)
-    chains = [late[i] for i in range(8)]
-    for i in range(8, late.shape[0]):
+    chains = [late[i] for i in range(min(8, late.shape[0]))]
+    for i in range(len(chains), late.shape[0]):
         chains[i % 8] = chains[i % 8] + late[i]
     rows = functools.reduce(lambda p, q: p + q, chains)
 
@@ -423,22 +430,22 @@
     older = older if steps_before else None
     for b in range(x.shape[1] // LANES):
         g = scaled * block_of(resid, b)
-        advance(b, newest, left_over, older, x, px, g, pgx, hsx, hgx, dx if steps_before else None, x_out, None if last else gx_out, None if last else dx_out)
+        advance(b, newest, left_over, older, x, px, g, pgx, hx, dx if steps_before else None, x_out, None if last else gx_out, None if last else dx_out)
     for b in range(w.shape[1] // LANES):
         slack = slack_of(block_of(w, b), block_of(center, b), block_of(width, b))
         g = relax * (block_of(start, b) + step * block_of(image, b) - slack)
-        advance(b, newest, left_over, older, w, pw, g, pgw, hsw, hgw, dw if steps_before else None, w_out, None if last else gw_out, None if last else dw_out)
+        advance(b, newest, left_over, older, w, pw, g, pgw, hw, dw if steps_before else None, w_out, None if last else gw_out, None if last else dw_out)
     if not last:
         send_products(x_out, cols, lambda t: slot[t], tiles, send, left)
 
 
-def advance(b, newest, left_over, older, state, previous, g, previous_g, hs, hg, kept, out, g_out, d_out):
+def advance(b, newest, left_over, older, state, previous, g, previous_g, hist, kept, out, g_out, d_out):
     lo, hi = b * LANES, (b + 1) * LANES
     here = state[:, lo:hi]
     fresh = (here - previous[:, lo:hi]) + (g - previous_g[:, lo:hi])
     value = here + g - newest * fresh
     for m in range(len(left_over)):
-        value = value - left_over[m] * (hs[m, :, lo:hi] + hg[m, :, lo:hi])
+        value = value - left_over[m] * hist[m, :, lo:hi]
     if kept is not None:
         value = value - older * kept[:, lo:hi]
     out[:, lo:hi] = value
@@ -581,10 +588,17 @@
             [pltpu.VMEM((col_count, problems, tile_size), f32)],
         )
         own, other = over_con(sent)
+        if first:
+            flipped, hist_x, hist_w = call(
+                prepare_kernel,
+                "prepare",
+                vs(blocks, hist_sx, hist_gx, hist_sw, hist_gw, sent),
+                [(blocks.shape, f32, "v"), (hist_sx.shape, f32, "v"), (hist_sw.shape, f32, "v")],
+            )
         outs = call(
             functools.partial(residual_kernel, first),
             "residual",
-            vs(own, other, x, linear_cost, diag) + ss(cols_here, slot) + vs(blocks),
+            vs(own, other, x, linear_cost, diag) + ss(cols_here, slot) + vs(flipped),
             [panel, x_like] + ([one_tile] if first else []),
             [left],
         )
@@ -610,9 +624,9 @@
             "update",
             vs(late, known)
             + ss(slot_order, sigma_level)
-            + vs(x, px, pgx, resid, hist_sx, hist_gx, w, pw, pgw, start, image, bound_center, bound_width, hist_sw, hist_gw)
+            + vs(x, px, pgx, resid, hist_x, w, pw, pgw, start, image, bound_center, bound_width, hist_w)
             + vs(*kept)
-            + ([] if last else ss(cols_here, slot) + vs(blocks)),
+            + ([] if last else ss(cols_here, slot) + vs(flipped)),
             [x_like, w_like] + ([] if last else [x_like, w_like, x_like, w_like, one_tile, panel]),
             [] if last else [left],
         )

time: 218 us -> 216 us (level)
    pallas_call x11 -> x12, Pallas kernels: 19.2 us -> 18.6 us  [call(): pl.pallas_call(kernel, out_shape=[jax.ShapeDtypeStruct(shape, dtype) for...]
  transfers between devices with their start and end apart: 10 -> 10, of which waited for: 8 -> 8; matrix products, arithmetic and copies ran while one was open for 0% -> 0% of each run, Pallas kernels for 0% -> 1%
where the time goes in v5:
time: 216 us
  blocking collectives  165 us (76%)
  Pallas kernels  18.6 us (9%)
  waiting for transfers between devices  16.4 us (8%)
  starting transfers between devices  14.6 us (7%)
    all_to_all x6, blocking collectives, exchange(): return lax.all_to_all(x, 'var', 0, 0, tiled=True)  128 us
    all_to_all x2, blocking collectives, per_device(): lax.all_to_all(copies, ('con', 'var'), 0, 0, tiled=True, axis_index_group...  36.7 us
    pallas_call x12, Pallas kernels, call(): pl.pallas_call(kernel, out_shape=[jax.ShapeDtypeStruct(shape, dtype) for...  18.6 us
    ppermute x8, waiting for transfers between devices, partner(): return lax.ppermute(x, 'con', [(i, i ^ k) for i in range(con_count)])  14.8 us
    ppermute x8, starting transfers between devices, partner(): return lax.ppermute(x, 'con', [(i, i ^ k) for i in range(con_count)])  10.4 us
  transfers between devices with their start and end apart: 10, of which 8 were waited for; matrix products, arithmetic and copies ran while one was open for 0% of the time, Pallas kernels for 1%

profile of v5, /device:TPU:1, one launch (start us, length us, event | category | flops | bytes accessed | tf_op | source)
XLA Modules:
  0.0 215.8 jit_solution(5503740040797373851)
XLA Ops:
  0.7 4.0 %open.1 = (f32[128,8,128]{2,1,0:T(8,128)S(1)}, s32[72]{0:T(128)S(1)}) custom-call(s32[1,72]{1,0:T(1,128)} %bitcast.26, s32[1,72]{1,0:T(1,128)} %bitcast.20, f32[8,4096]{1,0:T(8,128)} %refs_5_.5, f32[72,128,128]{2,1,0:T(8,128)} %bitcast.6, f32[8,4096]{1,0:T(8,128)} %refs_5_.4, f32[8,2048]{1,0:T(8,128)} %refs_10_.5, f32[8,2048]{1,0:T(8,128)} %refs_10_.4, ...), custom_call_target="tpu_custom_call" | custom-call | tf_op jit(solution)/shard_map/open/pallas_call | solution.py:459
  4.8 27.7 %all_to_all.40.refs_0_ = f32[128,8,128]{2,1,0:T(8,128)S(1)} all-to-all(f32[128,8,128]{2,1,0:T(8,128)S(1)} %get-tuple-element.30), channel_id=1, replica_groups=mesh['con'=8,'var'=32] {'var'}, dimensions={0} | all-to-all | bytes 1048576 | tf_op jit(solution)/shard_map/all_to_all | solution.py:519
  32.5 1.5 penalty_first.1
  34.0 19.0 %all_to_all.41.refs_0_ = f32[96,8,128]{2,1,0:T(8,128)S(1)} all-to-all(f32[96,8,128]{2,1,0:T(8,128)S(1)} %get-tuple-element.31), channel_id=1, replica_groups=mesh['con'=8,'var'=32] {'var'}, dimensions={0} | all-to-all | bytes 786432 | tf_op jit(solution)/shard_map/all_to_all | solution.py:519
  53.0 1.3 transpose.4._
  54.3 2.8 %collective-permute-start.2 = (f32[8,4224]{1,0:T(8,128)S(1)}, f32[8,4224]{1,0:T(8,128)S(1)}, u32[]{:S(2)}, u32[]{:S(2)}) collective-permute-start(f32[8,4224]{1,0:T(8,128)S(1)} %transpose.4._), channel_id=1, source_target_pairs={{0,192},{32,224},{64,128},{96,160},{128,64},{160,96},{192,0},{224,... | collective-permute-start | bytes 405512 | tf_op jit(solution)/shard_map/ppermute | solution.py:523
  57.8 2.9 %collective-permute-done.2 = f32[8,4224]{1,0:T(8,128)S(1)} collective-permute-done((f32[8,4224]{1,0:T(8,128)S(1)}, f32[8,4224]{1,0:T(8,128)S(1)}, u32[]{:S(2)}, u32[]{:S(2)}) %collective-permute-start.2) | collective-permute-done | bytes 135200 | tf_op jit(solution)/shard_map/ppermute | solution.py:523
  60.7 1.9 collective-permute-done.1
  62.6 2.5 %collective-permute-start.3 = (f32[8,4224]{1,0:T(8,128)S(1)}, f32[8,4224]{1,0:T(8,128)S(1)}, u32[]{:S(2)}, u32[]{:S(2)}) collective-permute-start(f32[8,4224]{1,0:T(8,128)S(1)} %add_add_fusion.own), channel_id=1, source_target_pairs={{0,32},{32,0},{64,96},{96,64},{128,160},{160,128},{192,224},{224,1... | collective-permute-start | bytes 405512 | tf_op jit(solution)/shard_map/ppermute | solution.py:523
  65.2 1.4 prepare.1
  66.6 1.5 collective-permute-done.3.other
  68.1 1.4 residual.2
  69.5 22.1 %all_to_all.42.got = f32[96,8,128]{2,1,0:T(8,128)S(1)} all-to-all(f32[96,8,128]{2,1,0:T(8,128)S(1)} %get-tuple-element.35), channel_id=1, replica_groups=mesh['con'=8,'var'=32] {'var'}, dimensions={0} | all-to-all | bytes 786432 | tf_op jit(solution)/shard_map/all_to_all | solution.py:519
  91.6 1.0 scalars.2
  92.6 2.1 collective-permute-start.4
  95.5 19.5 %all_to_all.43.refs_0_ = f32[128,2,128]{2,1,0:T(2,128)S(1)} all-to-all(f32[128,2,128]{2,1,0:T(2,128)S(1)} %broadcast_in_dim.4), channel_id=1, replica_groups={{0,2,4,6,8,10,12,14,16,18,20,22,24,26,28,30,32,34,36,38,40,42,44,46,48,..., dimensions={0} | all-to-all | bytes 262144 | tf_op jit(solution)/shard_map/all_to_all | solution.py:621
  115.1 1.9 update.2
  117.0 18.5 %all_to_all.44.refs_0_ = f32[96,8,128]{2,1,0:T(8,128)S(1)} all-to-all(f32[96,8,128]{2,1,0:T(8,128)S(1)} %get-tuple-element.44), channel_id=1, replica_groups=mesh['con'=8,'var'=32] {'var'}, dimensions={0} | all-to-all | bytes 786432 | tf_op jit(solution)/shard_map/all_to_all | solution.py:519
  136.3 18.9 %all_to_all.45.refs_0_ = f32[96,8,128]{2,1,0:T(8,128)S(1)} all-to-all(f32[96,8,128]{2,1,0:T(8,128)S(1)} %get-tuple-element.46), channel_id=1, replica_groups=mesh['con'=8,'var'=32] {'var'}, dimensions={0} | all-to-all | bytes 786432 | tf_op jit(solution)/shard_map/all_to_all | solution.py:519
  155.2 1.3 transpose.5
  157.0 1.2 collective-permute-start.6
  158.1 1.7 collective-permute-start.5
  159.9 3.7 %collective-permute-done.7 = f32[8,4096]{1,0:T(8,128)S(1)} collective-permute-done((f32[8,4096]{1,0:T(8,128)S(1)}, f32[8,4096]{1,0:T(8,128)S(1)}, u32[]{:S(2)}, u32[]{:S(2)}) %collective-permute-start.7) | collective-permute-done | bytes 131104 | tf_op jit(solution)/shard_map/ppermute | solution.py:523
  164.0 1.0 collective-permute-start.8
  165.0 4.4 %collective-permute-done.8.other = f32[8,4096]{1,0:T(8,128)S(1)} collective-permute-done((f32[8,4096]{1,0:T(8,128)S(1)}, f32[8,4096]{1,0:T(8,128)S(1)}, u32[]{:S(2)}, u32[]{:S(2)}) %collective-permute-start.8) | collective-permute-done | bytes 131104 | tf_op jit(solution)/shard_map/ppermute | solution.py:523
  169.4 1.4 residual.3
  170.8 22.1 %all_to_all.46.got = f32[96,8,128]{2,1,0:T(8,128)S(1)} all-to-all(f32[96,8,128]{2,1,0:T(8,128)S(1)} %get-tuple-element.48), channel_id=1, replica_groups=mesh['con'=8,'var'=32] {'var'}, dimensions={0} | all-to-all | bytes 786432 | tf_op jit(solution)/shard_map/all_to_all | solution.py:519
  192.9 1.0 scalars.3
  193.8 2.1 collective-permute-start.9
  195.9 0.8 collective-permute-done.9
  196.8 17.2 %all_to_all.47.refs_0_ = f32[128,2,128]{2,1,0:T(2,128)S(1)} all-to-all(f32[128,2,128]{2,1,0:T(2,128)S(1)} %broadcast_in_dim.5), channel_id=1, replica_groups={{0,2,4,6,8,10,12,14,16,18,20,22,24,26,28,30,32,34,36,38,40,42,44,46,48,..., dimensions={0} | all-to-all | bytes 262144 | tf_op jit(solution)/shard_map/all_to_all | solution.py:621
  214.0 1.8 update.3
  (55 shorter events, 3.4 us)
Async XLA Ops:
  0.6 52.3 %slice-start = ((s8[4718592]{0:T(1024)(128)(4,1)}), s8[4194304]{0:T(1024)(128)(4,1)S(1)}, s32[]{:S(2)}) async-start(s8[4718592]{0:T(1024)(128)(4,1)} %bitcast.7), calls=%async_computation.8 | async-start | bytes 8388608
  0.6 31.8 %copy-start.5 = (f32[8,2048]{1,0:T(8,128)S(1)}, f32[8,2048]{1,0:T(8,128)}, u32[]{:S(2)}) copy-start(f32[8,2048]{1,0:T(8,128)} %refs_10_.5) | copy-start | bytes 196612
  0.7 31.8 %copy-start.6 = (f32[8,2048]{1,0:T(8,128)S(1)}, f32[8,2048]{1,0:T(8,128)}, u32[]{:S(2)}) copy-start(f32[8,2048]{1,0:T(8,128)} %refs_14_.3) | copy-start | bytes 196612
  0.7 31.8 %copy-start.7 = (f32[8,2048]{1,0:T(8,128)S(1)}, f32[8,2048]{1,0:T(8,128)}, u32[]{:S(2)}) copy-start(f32[8,2048]{1,0:T(8,128)} %refs_15_.3) | copy-start | bytes 196612
  0.7 31.8 %copy-start.14 = (s32[2048]{0:T(1024)S(1)}, s32[2048]{0:T(1024)}, u32[]{:S(2)}) copy-start(s32[2048]{0:T(1024)} %param.27) | copy-start | bytes 24580
  0.7 52.3 %slice-start.1 = ((s8[4718592]{0:T(1024)(128)(4,1)}), s8[524288]{0:T(1024)(128)(4,1)S(1)}, s32[]{:S(2)}) async-start(s8[4718592]{0:T(1024)(128)(4,1)} %bitcast.7), calls=%async_computation.9 | async-start | bytes 1048576
  0.7 52.3 %copy-start.15 = (s32[1,1,72]{2,1,0:T(1,128)S(1)}, s32[1,1,72]{2,1,0:T(1,128)}, u32[]{:S(2)}) copy-start(s32[1,1,72]{2,1,0:T(1,128)} %param.22) | copy-start | bytes 868
  4.7 60.4 %copy-start = (f32[8,8,4096]{2,1,0:T(8,128)S(1)}, f32[8,8,4096]{2,1,0:T(8,128)}, u32[]{:S(2)}) copy-start(f32[8,8,4096]{2,1,0:T(8,128)} %hgx.5) | copy-start | bytes 3145732
  4.7 60.4 %copy-start.1 = (f32[8,8,2048]{2,1,0:T(8,128)S(1)}, f32[8,8,2048]{2,1,0:T(8,128)}, u32[]{:S(2)}) copy-start(f32[8,8,2048]{2,1,0:T(8,128)} %hgw.5) | copy-start | bytes 1572868
  4.7 60.4 %copy-start.3 = (f32[8,8,4096]{2,1,0:T(8,128)S(1)}, f32[8,8,4096]{2,1,0:T(8,128)}, u32[]{:S(2)}) copy-start(f32[8,8,4096]{2,1,0:T(8,128)} %hsx.1) | copy-start | bytes 3145732
  4.8 60.4 %copy-start.8 = (f32[8,8,2048]{2,1,0:T(8,128)S(1)}, f32[8,8,2048]{2,1,0:T(8,128)}, u32[]{:S(2)}) copy-start(f32[8,8,2048]{2,1,0:T(8,128)} %hsw.1) | copy-start | bytes 1572868
  54.3 13.8 %copy-start.2 = (f32[8,4096]{1,0:T(8,128)S(1)}, f32[8,4096]{1,0:T(8,128)}, u32[]{:S(2)}) copy-start(f32[8,4096]{1,0:T(8,128)} %refs_5_.5) | copy-start | bytes 393220
  54.3 13.8 %copy-start.12 = (f32[8,4096]{1,0:T(8,128)S(1)}, f32[8,4096]{1,0:T(8,128)}, u32[]{:S(2)}) copy-start(f32[8,4096]{1,0:T(8,128)} %linear.3) | copy-start | bytes 393220
  54.3 13.8 %copy-start.13 = (f32[4096]{0:T(1024)S(1)}, f32[4096]{0:T(1024)}, u32[]{:S(2)}) copy-start(f32[4096]{0:T(1024)} %param.23) | copy-start | bytes 49156
  54.3 6.4 %collective-permute-start.2 = (f32[8,4224]{1,0:T(8,128)S(1)}, f32[8,4224]{1,0:T(8,128)S(1)}, u32[]{:S(2)}, u32[]{:S(2)}) collective-permute-start(f32[8,4224]{1,0:T(8,128)S(1)} %transpose.4._), channel_id=1, source_target_pairs={{0,192},{32,224},{64,128},{96,160},{128,64},{160,96},{192,0},{224,... | collective-permute-start | bytes 405512 | tf_op jit(solution)/shard_map/ppermute | solution.py:523
  57.1 5.5 %collective-permute-start.1 = (f32[8,4224]{1,0:T(8,128)S(1)}, f32[8,4224]{1,0:T(8,128)S(1)}, u32[]{:S(2)}, u32[]{:S(2)}) collective-permute-start(f32[8,4224]{1,0:T(8,128)S(1)} %transpose.4._), channel_id=1, source_target_pairs={{0,128},{32,160},{64,192},{96,224},{128,0},{160,32},{192,64},{224,... | collective-permute-start | bytes 405512 | tf_op jit(solution)/shard_map/ppermute | solution.py:523
  57.5 5.1 %collective-permute-start = (f32[8,4224]{1,0:T(8,128)S(1)}, f32[8,4224]{1,0:T(8,128)S(1)}, u32[]{:S(2)}, u32[]{:S(2)}) collective-permute-start(f32[8,4224]{1,0:T(8,128)S(1)} %transpose.4._), channel_id=1, source_target_pairs={{0,64},{32,96},{64,0},{96,32},{128,192},{160,224},{192,128},{224,1... | collective-permute-start | bytes 405512 | tf_op jit(solution)/shard_map/ppermute | solution.py:523
  62.6 5.5 %collective-permute-start.3 = (f32[8,4224]{1,0:T(8,128)S(1)}, f32[8,4224]{1,0:T(8,128)S(1)}, u32[]{:S(2)}, u32[]{:S(2)}) collective-permute-start(f32[8,4224]{1,0:T(8,128)S(1)} %add_add_fusion.own), channel_id=1, source_target_pairs={{0,32},{32,0},{64,96},{96,64},{128,160},{160,128},{192,224},{224,1... | collective-permute-start | bytes 405512 | tf_op jit(solution)/shard_map/ppermute | solution.py:523
  66.6 25.0 %copy-start.4 = (f32[8,4096]{1,0:T(8,128)S(1)}, f32[8,4096]{1,0:T(8,128)}, u32[]{:S(2)}) copy-start(f32[8,4096]{1,0:T(8,128)} %qgx.3) | copy-start | bytes 393220
  66.6 25.0 %copy-start.9 = (f32[8,2048]{1,0:T(8,128)S(1)}, f32[8,2048]{1,0:T(8,128)}, u32[]{:S(2)}) copy-start(f32[8,2048]{1,0:T(8,128)} %qgw.3) | copy-start | bytes 196612
  66.6 25.0 %copy-start.10 = (f32[8,4096]{1,0:T(8,128)S(1)}, f32[8,4096]{1,0:T(8,128)}, u32[]{:S(2)}) copy-start(f32[8,4096]{1,0:T(8,128)} %refs_5_.4) | copy-start | bytes 393220
  66.6 25.0 %copy-start.11 = (f32[8,2048]{1,0:T(8,128)S(1)}, f32[8,2048]{1,0:T(8,128)}, u32[]{:S(2)}) copy-start(f32[8,2048]{1,0:T(8,128)} %refs_10_.4) | copy-start | bytes 196612
  68.1 47.0 %copy-start.16 = (s32[8]{0:T(128)S(1)}, s32[8]{0:T(128)}, u32[]{:S(2)}) copy-start(s32[8]{0:T(128)} %refs_2_.7) | copy-start | bytes 100
  68.1 47.0 %copy-start.17 = (s32[8]{0:T(128)S(1)}, s32[8]{0:T(128)}, u32[]{:S(2)}) copy-start(s32[8]{0:T(128)} %refs_3_.7) | copy-start | bytes 100
  92.6 2.9 %collective-permute-start.4 = (f32[2,128]{1,0:T(2,128)S(1)}, f32[2,128]{1,0:T(2,128)S(1)}, u32[]{:S(2)}, u32[]{:S(2)}) collective-permute-start(f32[2,128]{1,0:T(2,128)S(1)} %get-tuple-element.39), channel_id=1, source_target_pairs={{0,1},{1,0},{2,3},{3,2},{4,5},{5,4},{6,7},{7,6},{8,9},{9,8},{10,11... | collective-permute-start | bytes 3080 | tf_op jit(solution)/shard_map/ppermute | solution.py:619
  156.5 7.1 %collective-permute-start.7 = (f32[8,4096]{1,0:T(8,128)S(1)}, f32[8,4096]{1,0:T(8,128)S(1)}, u32[]{:S(2)}, u32[]{:S(2)}) collective-permute-start(f32[8,4096]{1,0:T(8,128)S(1)} %transpose.5), channel_id=1, source_target_pairs={{0,192},{32,224},{64,128},{96,160},{128,64},{160,96},{192,0},{224,... | collective-permute-start | bytes 393224 | tf_op jit(solution)/shard_map/ppermute | solution.py:523
  157.0 6.6 %collective-permute-start.6 = (f32[8,4096]{1,0:T(8,128)S(1)}, f32[8,4096]{1,0:T(8,128)S(1)}, u32[]{:S(2)}, u32[]{:S(2)}) collective-permute-start(f32[8,4096]{1,0:T(8,128)S(1)} %transpose.5), channel_id=1, source_target_pairs={{0,128},{32,160},{64,192},{96,224},{128,0},{160,32},{192,64},{224,... | collective-permute-start | bytes 393224 | tf_op jit(solution)/shard_map/ppermute | solution.py:523
  158.1 5.8 %collective-permute-start.5 = (f32[8,4096]{1,0:T(8,128)S(1)}, f32[8,4096]{1,0:T(8,128)S(1)}, u32[]{:S(2)}, u32[]{:S(2)}) collective-permute-start(f32[8,4096]{1,0:T(8,128)S(1)} %transpose.5), channel_id=1, source_target_pairs={{0,64},{32,96},{64,0},{96,32},{128,192},{160,224},{192,128},{224,1... | collective-permute-start | bytes 393224 | tf_op jit(solution)/shard_map/ppermute | solution.py:523
  164.0 5.4 %collective-permute-start.8 = (f32[8,4096]{1,0:T(8,128)S(1)}, f32[8,4096]{1,0:T(8,128)S(1)}, u32[]{:S(2)}, u32[]{:S(2)}) collective-permute-start(f32[8,4096]{1,0:T(8,128)S(1)} %add_add_fusion.1.own), channel_id=1, source_target_pairs={{0,32},{32,0},{64,96},{96,64},{128,160},{160,128},{192,224},{224,1... | collective-permute-start | bytes 393224 | tf_op jit(solution)/shard_map/ppermute | solution.py:523
  193.8 2.9 %collective-permute-start.9 = (f32[2,128]{1,0:T(2,128)S(1)}, f32[2,128]{1,0:T(2,128)S(1)}, u32[]{:S(2)}, u32[]{:S(2)}) collective-permute-start(f32[2,128]{1,0:T(2,128)S(1)} %get-tuple-element.53), channel_id=1, source_target_pairs={{0,1},{1,0},{2,3},{3,2},{4,5},{5,4},{6,7},{7,6},{8,9},{9,8},{10,11... | collective-permute-start | bytes 3080 | tf_op jit(solution)/shard_map/ppermute | solution.py:619

commit v6 on v5

--- a/solution.py
+++ b/solution.py
@@ -18,6 +18,14 @@
 bf16 = jnp.bfloat16
 
 U_H, V_H, U_U, U_V, U_P, V_P, V_V, S_S, R_R, C_C, U_D, V_D, SCALARS = 0, 8, 16, 17, 18, 19, 20, 21, 22, 23, 24, 25, 26
+
+
+MEMORY = 8
+LANE_P, LANE_S, LANE_ENTRY = 36, 44, 52
+
+
+def pair_lane(m, n):
+    return m * MEMORY - m * (m - 1) // 2 + n - m
 
 
 def halves(value):
@@ -43,6 +51,8 @@
 
 
 def at(ref, block):
+    if isinstance(block, int):
+        return block_of(ref, block)
     return ref[:, pl.ds(pl.multiple_of(block * LANES, LANES), LANES)]
 
 
@@ -73,7 +83,12 @@
 
     def one(t):
         axis = 0 if flipped else 1
-        send[where(t)] = times(left[cols[t]], jnp.concatenate(halves(tiles[t]), axis=axis), axis)
+        value = times(left[cols[t]], jnp.concatenate(halves(tiles[t]), axis=axis), axis)
+        if flipped:
+            send[where(t)] = value
+        else:
+            send[where(t)] = value[: value.shape[0] // 2]
+            send[where(t) + 1] = value[value.shape[0] // 2 :]
 
     size = tiles.shape[0] // len(waits)
     for i, wait in enumerate(waits):
@@ -82,13 +97,13 @@
         tile_loop(size, lambda t, i=i: one(t + i * size))
 
 
-def add_rows(got, index, rows, runs, sums):
+def add_rows(received, rows, sums):
     for ref in sums:
         ref[...] = jnp.zeros_like(ref)
     for s in range(rows.shape[0]):
         ref = sums[s % len(sums)]
         row = rows[s]
-        ref[row] = ref[row] + got[index(s)]
+        ref[row] = ref[row] + received(s)
     return lambda b: functools.reduce(lambda p, q: p + q, [ref[b] for ref in sums])
 
 
@@ -109,12 +124,13 @@
 
 
 def open_kernel(per_run, run_length, share, parts, *refs):
-    (hbm_rows, hbm_cols, hbm_x, hbm_tiles, *far), (send, slot), refs = refs[:13], refs[13:15], refs[15:]
-    rows_buf, cols_buf, x, tiles, px, w, pw, pgx, pgw, hsx, hsw, hgx, hgw, left, count, asked, spot, sem = refs
+    (hbm_rows, hbm_cols, hbm_x, hbm_tiles, *far), (send, slot, tiles), refs = refs[:13], refs[13:16], refs[16:]
+    rows_buf, cols_buf, x, px, w, pw, pgx, pgw, hsx, hsw, hgx, hgw, left, count, asked, spot, sem = refs
     memory = hgx.shape[0]
     problems = x.shape[0]
-    runs = send.shape[0] // (per_run + 1)
-    wide = per_run + 1
+    half = problems // 2
+    wide = 2 * per_run + 1
+    runs = send.shape[0] // wide
     first = lax.axis_index("con") * share
     mine = pl.ds(pl.multiple_of(first * LANES, LANES), share * LANES)
     far_px, far_w, far_pw, far_pgx, far_pgw, far_hsx, far_hsw, far_hgx, far_hgw = far
@@ -141,7 +157,7 @@
         count[owner] = rank + 1
         place = owner * per_run + rank
         slot[t] = place
-        spot[t] = place + owner
+        spot[t] = owner * wide + rank * 2
         asked[place] = row & (run_length - 1)
 
     def where(t):
@@ -155,45 +171,43 @@
     lanes = lane_ids((problems, LANES))
     out = jnp.zeros((problems, LANES), f32)
 
-    def both(f):
-        acc = None
-        for b in range(w.shape[1] // LANES):
-            v = f(False, b)
-            acc = v if acc is None else acc + v
-        for b in range(share):
-            acc = acc + f(True, b)
-        return total(acc)
-
-    def hist(ref_x, ref_w, m, is_x, b):
-        return (ref_x if is_x else ref_w)[m, :, b * LANES : (b + 1) * LANES]
-
-    def plain(ref_x, ref_w, is_x, b):
-        return block_of(ref_x if is_x else ref_w, b)
-
-    for m in range(memory):
-        for n in range(m, memory):
-            value = both(lambda q, b: hist(hgx, hgw, m, q, b) * hist(hgx, hgw, n, q, b))
-            out = jnp.where((lanes == m * memory + n) | (lanes == n * memory + m), value, out)
-        value = both(lambda q, b: hist(hgx, hgw, m, q, b) * plain(pgx, pgw, q, b))
-        out = jnp.where(lanes == memory * memory + m, value, out)
-
-        def square(q, b):
-            h = hist(hsx, hsw, m, q, b)
-            return h * h
-
-        out = jnp.where(lanes == memory * (memory + 1) + m, both(square), out)
-    index = entry_ids(runs * per_run, problems) - lax.axis_index("var") * per_run
+    places = [(False, b) for b in range(w.shape[1] // LANES)] + [(True, b) for b in range(share)]
+
+    def read(ref_x, ref_w, place):
+        is_x, b = place
+        ref = ref_x if is_x else ref_w
+        return ref[..., b * LANES : (b + 1) * LANES]
+
+    acc = {}
+
+    def add(lane, value):
+        acc[lane] = acc[lane] + value if lane in acc else value
+
+    for place in places:
+        g = [read(hgx.at[m], hgw.at[m], place) for m in range(memory)]
+        for m in range(memory):
+            for n in range(m, memory):
+                add(pair_lane(m, n), g[m] * g[n])
+    for place in places:
+        p = read(pgx, pgw, place)
+        for m in range(memory):
+            add(LANE_P + m, read(hgx.at[m], hgw.at[m], place) * p)
+            h = read(hsx.at[m], hsw.at[m], place)
+            add(LANE_S + m, h * h)
+    for lane, value in acc.items():
+        out = jnp.where(lanes == lane, total(value), out)
+    index = entry_ids(problems) - lax.axis_index("var") * per_run
     for r in range(runs):
         mark = out
         for i in range(per_run):
             mark = jnp.where(index == i, asked[r * per_run + i].astype(f32), mark)
-        send[r * wide + per_run] = mark
-
-
-def entry_ids(entries, problems):
+        turned = pltpu.roll(mark, LANES // 2, 1)
+        send[r * wide + 2 * per_run] = jnp.where(lanes[:half] < LANES // 2, mark[:half], turned[half:])
+
+
+def entry_ids(problems):
     shape = (problems, LANES)
-    base = LANES - -(-entries // problems)
-    return (lane_ids(shape) - base) * problems + lax.broadcasted_iota(jnp.int32, shape, 0)
+    return (lane_ids(shape) - LANE_ENTRY) * problems + lax.broadcasted_iota(jnp.int32, shape, 0)
 
 
 def penalty_kernel(first, per_run, *refs):
@@ -204,20 +218,25 @@
     slots = send.shape[0]
     runs = slots // per_run
     if first:
-        wide = per_run + 1
-        early_sum = functools.reduce(lambda p, q: p + q, [got[r * wide + per_run] for r in range(runs)])
+        wide = 2 * per_run + 1
+        folded = functools.reduce(lambda p, q: p + q, [got[r * wide + 2 * per_run] for r in range(runs)])
+        early_sum = jnp.concatenate([folded, pltpu.roll(folded, LANES // 2, 1)], axis=0)
         early[...] = early_sum
         marks_int[...] = early_sum.astype(jnp.int32)
         copy = pltpu.make_async_copy(marks_int, marks, sem)
         copy.start()
         copy.wait()
         problems = w.shape[0]
-        base = LANES - -(-slots // problems)
         for s in range(slots):
-            rows[s] = marks[s % problems, base + s // problems]
-        result = add_rows(got, lambda s: s // per_run * wide + s % per_run, rows, runs, sums)
+            rows[s] = marks[s % problems, LANE_ENTRY + s // problems]
+
+        def received(s):
+            unit = s // per_run * wide + s % per_run * 2
+            return jnp.concatenate([got[unit], got[unit + 1]], axis=0)
+
+        result = add_rows(received, rows, sums)
     else:
-        result = add_rows(got, lambda s: s, rows, runs, sums)
+        result = add_rows(lambda s: got[s], rows, sums)
     blocks = w.shape[1] // LANES
     for b in range(blocks):
         start = result(b)
@@ -273,52 +292,69 @@
     send_products(resid, cols, lambda t: slot[t], tiles, send, left)
 
 
+class Sums:
+    def __init__(self, problems):
+        self.shape = (problems, LANES)
+        self.acc = {}
+
+    def add(self, i, value):
+        self.acc[i] = self.acc[i] + value if i in self.acc else value
+
+    def tiles(self, tiles):
+        turn = (LANES - 16 * lax.broadcasted_iota(jnp.int32, self.shape, 0)) & (LANES - 1)
+        lanes = lane_ids(self.shape)
+        tiles = list(tiles)
+        for i, value in self.acc.items():
+            tiles[i // 16] = jnp.where(lanes == turn + i % 16, total(value), tiles[i // 16])
+        return tiles
+
+
+def blocks_of(w, share):
+    first = lax.axis_index("con") * share
+    return [(False, b) for b in range(w.shape[1] // LANES)] + [(True, first + b) for b in range(share)]
+
+
+def before_kernel(share, start, w, center, width, pw, pgw, x, px, pgx, hgx, hgw, qgx, qgw, _, out):
+    sums = Sums(w.shape[0])
+    for is_x, b in blocks_of(w, share):
+        if is_x:
+            p = at(pgx, b)
+            u, s, d = -p, at(x, b) - at(px, b), p - at(qgx, b)
+        else:
+            p, here = block_of(pgw, b), block_of(w, b)
+            slack = slack_of(here, block_of(center, b), block_of(width, b))
+            u, s, d = relax * (block_of(start, b) - slack) - p, here - block_of(pw, b), p - block_of(qgw, b)
+        for m in range(MEMORY):
+            sums.add(U_H + m, u * at(hgx.at[m] if is_x else hgw.at[m], b))
+        for i, value in ((U_U, u * u), (U_P, u * p), (S_S, s * s), (U_D, u * d)):
+            sums.add(i, value)
+    zero = jnp.zeros(sums.shape, f32)
+    out[0], out[1] = sums.tiles([zero, zero])
+
+
 def scalar_kernel(
-    share, got, rows, start, w, center, width, level, pw, pgw, x, px, pgx, resid, diag, hgx, hgw, qgx, qgw, send, image, *sums
+    share, got, rows, start, w, center, width, level, pgw, pgx, resid, diag, hgx, hgw, qgx, qgw, before, send, image, *scratch
 ):
-    problems = w.shape[0]
-    result = add_rows(got, lambda s: s, rows, sums[0].shape[0], sums)
-    memory = hgx.shape[0]
-    acc = [None] * SCALARS
-
-    def add(i, value):
-        acc[i] = value if acc[i] is None else acc[i] + value
-
-    def terms(u, v, p, s, d, hist):
-        for m in range(memory):
-            h = hist(m)
-            add(U_H + m, u * h)
-            add(V_H + m, v * h)
-        for i, value in ((U_U, u * u), (U_V, u * v), (U_P, u * p), (V_P, v * p), (V_V, v * v), (S_S, s * s), (U_D, u * d), (V_D, v * d)):
-            add(i, value)
-
-    for b in range(w.shape[1] // LANES):
-        ar = result(b)
-        image[:, b * LANES : (b + 1) * LANES] = ar
-        here = block_of(w, b)
-        slack = slack_of(here, block_of(center, b), block_of(width, b))
-        p = block_of(pgw, b)
-        u = relax * (block_of(start, b) - slack) - p
-        add(C_C, rho_of(level, b) * ar * ar)
-        terms(u, relax * ar, p, here - block_of(pw, b), p - block_of(qgw, b), lambda m: hgw[m, :, b * LANES : (b + 1) * LANES])
-    for i in range(share):
-        b = lax.axis_index("con") * share + i
-        r = at(resid, b)
-        p = at(pgx, b)
-        add(R_R, r * r)
-        add(C_C, at(diag, b) * r * r)
-        terms(-p, relax * r, p, at(x, b) - at(px, b), p - at(qgx, b), lambda m: hgx[m, :, pl.ds(pl.multiple_of(b * LANES, LANES), LANES)])
-    lanes = lane_ids((problems, LANES))
-    lane_of = (LANES - 16 * lax.broadcasted_iota(jnp.int32, (problems, LANES), 0)) & (LANES - 1)
-    packed = []
-    for row in range(2):
-        tile = jnp.zeros((problems, LANES), f32)
-        for i in range(16):
-            if row * 16 + i < SCALARS:
-                tile = jnp.where(lanes == lane_of + i, total(acc[row * 16 + i]), tile)
-        packed.append(jnp.sum(tile, axis=0, keepdims=True))
-    both = jnp.concatenate(packed, axis=0)
-    send[...] = both
+    result = add_rows(lambda s: got[s], rows, scratch)
+    sums = Sums(w.shape[0])
+    for is_x, b in blocks_of(w, share):
+        if is_x:
+            r, p = at(resid, b), at(pgx, b)
+            u, v, d = -p, relax * r, p - at(qgx, b)
+            sums.add(R_R, r * r)
+            sums.add(C_C, at(diag, b) * r * r)
+        else:
+            ar, p = result(b), block_of(pgw, b)
+            image[:, b * LANES : (b + 1) * LANES] = ar
+            slack = slack_of(block_of(w, b), block_of(center, b), block_of(width, b))
+            u, v, d = relax * (block_of(start, b) - slack) - p, relax * ar, p - block_of(qgw, b)
+            sums.add(C_C, rho_of(level, b) * ar * ar)
+        for m in range(MEMORY):
+            sums.add(V_H + m, v * at(hgx.at[m] if is_x else hgw.at[m], b))
+        for i, value in ((U_V, u * v), (V_P, v * p), (V_V, v * v), (V_D, v * d)):
+            sums.add(i, value)
+    rows_out = [jnp.sum(tile, axis=0, keepdims=True) for tile in sums.tiles([before[0], before[1]])]
+    send[...] = jnp.concatenate(rows_out, axis=0)
 
 
 def update_kernel(last, steps_before, *refs):
@@ -372,28 +408,27 @@
     with_p = scalar(U_P) + step * scalar(V_P)
     gram = [[None] * memory for _ in range(memory)]
     for m in range(memory):
-        gram[m][m] = given(m * memory + m) * keep[m] + own * new[m]
+        gram[m][m] = given(pair_lane(m, m)) * keep[m] + own * new[m]
         for n in range(m + 1, memory):
-            value = given(m * memory + n) * (keep[m] * keep[n]) + dot[n] * new[m] + dot[m] * new[n]
+            value = given(pair_lane(m, n)) * (keep[m] * keep[n]) + dot[n] * new[m] + dot[m] * new[n]
             gram[m][n] = gram[n][m] = value
-    at_p, at_s = memory * memory, memory * (memory + 1)
     rhs = []
     for m in range(memory):
-        value = given(at_p + m) * keep[m] + with_p * new[m]
+        value = given(LANE_P + m) * keep[m] + with_p * new[m]
         for n in range(memory):
             value = value + gram[m][n] * new[n]
         rhs.append(value)
     s_s = scalar(S_S)
-    squares = [given(at_s + m) * keep[m] + s_s * new[m] for m in range(memory)]
+    squares = [given(LANE_S + m) * keep[m] + s_s * new[m] for m in range(memory)]
     frob = functools.reduce(lambda p, q: p + q, squares + [gram[m][m] for m in range(memory)])
     damp = ridge * frob
     if not last:
         out = jnp.zeros(shape, f32)
         for m in range(memory):
             for n in range(m, memory):
-                out = jnp.where((lanes == m * memory + n) | (lanes == n * memory + m), gram[m][n], out)
-            out = jnp.where(lanes == at_p + m, rhs[m], out)
-            out = jnp.where(lanes == at_s + m, squares[m], out)
+                out = jnp.where(lanes == pair_lane(m, n), gram[m][n], out)
+            out = jnp.where(lanes == LANE_P + m, rhs[m], out)
+            out = jnp.where(lanes == LANE_S + m, squares[m], out)
         known_out[...] = out
     low = [[None] * memory for _ in range(memory)]
     inverse = []
@@ -507,7 +542,7 @@
     x_like = ((problems, var_cols), f32, "v")
     w_like = ((problems, con_cols), f32, "v")
     panel = ((slots, problems, tile_size), f32, "v")
-    wide_panel = ((slots + var_count, problems, tile_size), f32, "v")
+    wide_panel = (((2 * per_run + 1) * var_count, problems // 2, tile_size), f32, "v")
     one_tile = ((problems, tile_size), f32, "v")
     left = pltpu.VMEM((col_count, 2 * problems, 2 * tile_size), bf16)
     sums = [pltpu.VMEM((run_length, problems, tile_size), f32)] * 4
@@ -536,16 +571,15 @@
     memory = hist_gx.shape[0]
     hx_mine = pltpu.VMEM((memory, problems, share * tile_size), f32)
     hw_mine = pltpu.VMEM((memory, problems, con_cols), f32)
-    sent, slot = call(
+    sent, slot, blocks = call(
         functools.partial(open_kernel, per_run, run_length, share, parts),
         "open",
         [(pltpu.with_memory_space_constraint(a, pltpu.HBM), "h") for a in [row_tile[0], col_tile[0]] + far],
-        [wide_panel, ((count,), jnp.int32, "s")],
+        [wide_panel, ((count,), jnp.int32, "s"), (blocks.shape, f32, "v")],
         [
             pltpu.SMEM((1, count), jnp.int32),
             pltpu.SMEM((1, count), jnp.int32),
             pltpu.VMEM((problems, var_cols), f32),
-            pltpu.VMEM(blocks.shape, f32),
             x_mine, w_mine, w_mine, x_mine, w_mine, hx_mine, hw_mine, hx_mine, hw_mine,
             left,
             pltpu.SMEM((var_count,), jnp.int32),
@@ -588,6 +622,12 @@
             [pltpu.VMEM((col_count, problems, tile_size), f32)],
         )
         own, other = over_con(sent)
+        (before,) = call(
+            functools.partial(before_kernel, share),
+            "before",
+            vs(start, w, bound_center, bound_width, pw, pgw, x, px, pgx, hist_gx, hist_gw, qgx, qgw, sent),
+            [((2, problems, tile_size), f32, "v")],
+        )
         if first:
             flipped, hist_x, hist_w = call(
                 prepare_kernel,
@@ -612,7 +652,7 @@
             "scalars",
             vs(got)
             + ss(rows)
-            + vs(start, w, bound_center, bound_width, level, pw, pgw, x, px, pgx, resid, diag, hist_gx, hist_gw, qgx, qgw),
+            + vs(start, w, bound_center, bound_width, level, pgw, pgx, resid, diag, hist_gx, hist_gw, qgx, qgw, before),
             [((2, LANES), f32, "v"), w_like],
             sums,
         )

time: 216 us -> 253 us (1.17)
  blocking collectives: 165 us -> 119 us
  local copies, waits for them, and re-layouts: 0.19 us -> 42 us
  waiting for transfers between devices: 16.4 us -> 37.9 us
  starting transfers between devices: 14.6 us -> 31.6 us
    all_to_all x6 -> x4, blocking collectives: 128 us -> 82.9 us  [exchange(): return lax.all_to_all(x, 'var', 0, 0, tiled=True)]
    unnamed x40 -> x166, local copies, waits for them, and re-layouts: 0.11 us -> 42 us
    all_to_all x0 -> x2, waiting for transfers between devices: none -> 21.5 us  [exchange(): return lax.all_to_all(x, 'var', 0, 0, tiled=True)]
    all_to_all x0 -> x2, starting transfers between devices: none -> 17 us  [exchange(): return lax.all_to_all(x, 'var', 0, 0, tiled=True)]
    pallas_call x12 -> x14, Pallas kernels: 18.6 us -> 19.4 us  [call(): pl.pallas_call(kernel, out_shape=[jax.ShapeDtypeStruct(shape, dtype) for...]
  transfers between devices with their start and end apart: 10 -> 12, of which waited for: 8 -> 10; matrix products, arithmetic and copies ran while one was open for 0% -> 0% of each run, Pallas kernels for 1% -> 1%
where the time goes in v6:
time: 253 us; the launch traced here: 252 us
  blocking collectives  119 us (47%)
  local copies, waits for them, and re-layouts  42 us (17%)
  waiting for transfers between devices  37.9 us (15%)
  starting transfers between devices  31.6 us (12%)
  Pallas kernels  19.4 us (8%)
    all_to_all x4, blocking collectives, exchange(): return lax.all_to_all(x, 'var', 0, 0, tiled=True)  82.9 us
    unnamed x166, local copies, waits for them, and re-layouts  42 us
    all_to_all x2, blocking collectives, per_device(): lax.all_to_all(copies, ('con', 'var'), 0, 0, tiled=True, axis_index_group...  36.4 us
    all_to_all x2, waiting for transfers between devices, exchange(): return lax.all_to_all(x, 'var', 0, 0, tiled=True)  21.5 us
    pallas_call x14, Pallas kernels, call(): pl.pallas_call(kernel, out_shape=[jax.ShapeDtypeStruct(shape, dtype) for...  19.4 us
    all_to_all x2, starting transfers between devices, exchange(): return lax.all_to_all(x, 'var', 0, 0, tiled=True)  17 us
    ppermute x8, waiting for transfers between devices, partner(): return lax.ppermute(x, 'con', [(i, i ^ k) for i in range(con_count)])  14.8 us
    ppermute x8, starting transfers between devices, partner(): return lax.ppermute(x, 'con', [(i, i ^ k) for i in range(con_count)])  10.3 us
  transfers between devices with their start and end apart: 12, of which 10 were waited for; matrix products, arithmetic and copies ran while one was open for 0% of the time, Pallas kernels for 1%

profile of v6, /device:TPU:1, one launch (start us, length us, event | category | flops | bytes accessed | tf_op | source)
XLA Modules:
  0.0 251.6 jit_solution(8151945870417229032)
XLA Ops:
  0.7 4.3 %open.1 = (f32[224,4,128]{2,1,0:T(4,128)S(1)}, s32[72]{0:T(128)S(1)}, f32[72,128,128]{2,1,0:T(8,128)S(1)}) custom-call(s32[1,72]{1,0:T(1,128)} %bitcast.25, s32[1,72]{1,0:T(1,128)} %bitcast.18, f32[8,4096]{1,0:T(8,128)} %refs_5_.5, f32[72,128,128]{2,1,0:T(8,128)} %bitcast.24, f32[8,4096]{1,0:T(8,128)} %refs_5_.4, f32[8,2048]{1,0:T(8,128)} %refs_10_.5, ...), custom_call_target="tpu_custom_call" | custom-call | tf_op jit(solution)/shard_map/open/pallas_call | solution.py:494
  5.0 26.5 %all_to_all.40.refs_0_ = f32[224,4,128]{2,1,0:T(4,128)S(1)} all-to-all(f32[224,4,128]{2,1,0:T(4,128)S(1)} %get-tuple-element.31), channel_id=1, replica_groups=mesh['con'=8,'var'=32] {'var'}, dimensions={0} | all-to-all | bytes 917504 | tf_op jit(solution)/shard_map/all_to_all | solution.py:554
  31.5 1.6 penalty_first.1
  33.1 18.9 %all_to_all.41.refs_0_ = f32[96,8,128]{2,1,0:T(8,128)S(1)} all-to-all(f32[96,8,128]{2,1,0:T(8,128)S(1)} %get-tuple-element.32), channel_id=1, replica_groups=mesh['con'=8,'var'=32] {'var'}, dimensions={0} | all-to-all | bytes 786432 | tf_op jit(solution)/shard_map/all_to_all | solution.py:554
  52.0 1.3 transpose.4._
  53.3 2.8 %collective-permute-start.2 = (f32[8,4224]{1,0:T(8,128)S(1)}, f32[8,4224]{1,0:T(8,128)S(1)}, u32[]{:S(2)}, u32[]{:S(2)}) collective-permute-start(f32[8,4224]{1,0:T(8,128)S(1)} %transpose.4._), channel_id=1, source_target_pairs={{0,192},{32,224},{64,128},{96,160},{128,64},{160,96},{192,0},{224,... | collective-permute-start | bytes 405512 | tf_op jit(solution)/shard_map/ppermute | solution.py:558
  56.9 2.9 %collective-permute-done.2 = f32[8,4224]{1,0:T(8,128)S(1)} collective-permute-done((f32[8,4224]{1,0:T(8,128)S(1)}, f32[8,4224]{1,0:T(8,128)S(1)}, u32[]{:S(2)}, u32[]{:S(2)}) %collective-permute-start.2) | collective-permute-done | bytes 135200 | tf_op jit(solution)/shard_map/ppermute | solution.py:558
  59.8 1.9 collective-permute-done.1
  61.7 2.5 %collective-permute-start.3 = (f32[8,4224]{1,0:T(8,128)S(1)}, f32[8,4224]{1,0:T(8,128)S(1)}, u32[]{:S(2)}, u32[]{:S(2)}) collective-permute-start(f32[8,4224]{1,0:T(8,128)S(1)} %add_add_fusion.own), channel_id=1, source_target_pairs={{0,32},{32,0},{64,96},{96,64},{128,160},{160,128},{192,224},{224,1... | collective-permute-start | bytes 405512 | tf_op jit(solution)/shard_map/ppermute | solution.py:558
  64.2 1.4 prepare.1
  65.7 1.5 collective-permute-done.3.other
  67.2 1.4 residual.2
  68.6 2.2 copy-done.1
  72.8 8.9 %all-to-all-start.2 = ((f32[96,8,128]{2,1,0:T(8,128)}), f32[96,8,128]{2,1,0:T(8,128)}, u32[]{:S(2)}, u32[]{:S(2)}) async-start(f32[96,8,128]{2,1,0:T(8,128)} %copy-done.48), calls=%async_computation.2 | async-start | bytes 786432 | tf_op jit(solution)/shard_map/all_to_all | solution.py:554
  82.4 13.5 %all-to-all-done.2.got = f32[96,8,128]{2,1,0:T(8,128)} async-done(((f32[96,8,128]{2,1,0:T(8,128)}), f32[96,8,128]{2,1,0:T(8,128)}, u32[]{:S(2)}, u32[]{:S(2)}) %all-to-all-start.2) | async-done | bytes 393248 | tf_op jit(solution)/shard_map/all_to_all | solution.py:554
  98.9 1.4 scalars.2
  100.3 2.1 collective-permute-start.4
  103.2 19.2 %all_to_all.42.refs_0_ = f32[128,2,128]{2,1,0:T(2,128)S(1)} all-to-all(f32[128,2,128]{2,1,0:T(2,128)S(1)} %broadcast_in_dim.4), channel_id=1, replica_groups={{0,2,4,6,8,10,12,14,16,18,20,22,24,26,28,30,32,34,36,38,40,42,44,46,48,..., dimensions={0} | all-to-all | bytes 262144 | tf_op jit(solution)/shard_map/all_to_all | solution.py:661
  122.5 2.5 copy-done.2
  129.7 1.9 update.2
  133.5 18.7 %all_to_all.43.refs_0_ = f32[96,8,128]{2,1,0:T(8,128)S(1)} all-to-all(f32[96,8,128]{2,1,0:T(8,128)S(1)} %get-tuple-element.46), channel_id=1, replica_groups=mesh['con'=8,'var'=32] {'var'}, dimensions={0} | all-to-all | bytes 786432 | tf_op jit(solution)/shard_map/all_to_all | solution.py:554
  153.6 18.9 %all_to_all.44.refs_0_ = f32[96,8,128]{2,1,0:T(8,128)S(1)} all-to-all(f32[96,8,128]{2,1,0:T(8,128)S(1)} %get-tuple-element.48), channel_id=1, replica_groups=mesh['con'=8,'var'=32] {'var'}, dimensions={0} | all-to-all | bytes 786432 | tf_op jit(solution)/shard_map/all_to_all | solution.py:554
  172.5 1.3 transpose.5._
  175.4 1.7 collective-permute-start.5
  177.2 3.7 %collective-permute-done.7 = f32[8,4096]{1,0:T(8,128)S(1)} collective-permute-done((f32[8,4096]{1,0:T(8,128)S(1)}, f32[8,4096]{1,0:T(8,128)S(1)}, u32[]{:S(2)}, u32[]{:S(2)}) %collective-permute-start.7) | collective-permute-done | bytes 131104 | tf_op jit(solution)/shard_map/ppermute | solution.py:558
  182.9 4.4 %collective-permute-done.8.other = f32[8,4096]{1,0:T(8,128)S(1)} collective-permute-done((f32[8,4096]{1,0:T(8,128)S(1)}, f32[8,4096]{1,0:T(8,128)S(1)}, u32[]{:S(2)}, u32[]{:S(2)}) %collective-permute-start.8) | collective-permute-done | bytes 131104 | tf_op jit(solution)/shard_map/ppermute | solution.py:558
  187.3 1.3 residual.3
  190.1 8.2 %all-to-all-start.6 = ((f32[96,8,128]{2,1,0:T(8,128)}), f32[96,8,128]{2,1,0:T(8,128)S(1)}, u32[]{:S(2)}, u32[]{:S(2)}) async-start(f32[96,8,128]{2,1,0:T(8,128)} %copy-done.47), calls=%async_computation.6 | async-start | bytes 786432 | tf_op jit(solution)/shard_map/all_to_all | solution.py:554
  204.3 8.1 %all-to-all-done.6.got = f32[96,8,128]{2,1,0:T(8,128)S(1)} async-done(((f32[96,8,128]{2,1,0:T(8,128)}), f32[96,8,128]{2,1,0:T(8,128)S(1)}, u32[]{:S(2)}, u32[]{:S(2)}) %all-to-all-start.6) | async-done | bytes 393248 | tf_op jit(solution)/shard_map/all_to_all | solution.py:554
  219.7 2.1 collective-permute-start.9
  222.6 17.2 %all_to_all.45.refs_0_ = f32[128,2,128]{2,1,0:T(2,128)S(1)} all-to-all(f32[128,2,128]{2,1,0:T(2,128)S(1)} %broadcast_in_dim.5), channel_id=1, replica_groups={{0,2,4,6,8,10,12,14,16,18,20,22,24,26,28,30,32,34,36,38,40,42,44,46,48,..., dimensions={0} | all-to-all | bytes 262144 | tf_op jit(solution)/shard_map/all_to_all | solution.py:661
  249.9 1.7 update.3
  (186 shorter events, 44.7 us)
Async XLA Ops:
  0.7 51.3 %copy-start.63 = (s32[1,1,72]{2,1,0:T(1,128)S(1)}, s32[1,1,72]{2,1,0:T(1,128)}, u32[]{:S(2)}) copy-start(s32[1,1,72]{2,1,0:T(1,128)} %param.22) | copy-start | bytes 868
  4.9 60.7 %copy-start = (f32[72,128,128]{2,1,0:T(8,128)}, f32[72,128,128]{2,1,0:T(8,128)S(1)}, u32[]{:S(2)}) copy-start(f32[72,128,128]{2,1,0:T(8,128)S(1)} %get-tuple-element.34.refs_3_.tiles) | copy-start | bytes 14155780
  5.0 62.2 %copy-start.65 = (s32[72]{0:T(128)}, s32[72]{0:T(128)S(1)}, u32[]{:S(2)}) copy-start(s32[72]{0:T(128)S(1)} %get-tuple-element.33.refs_1_.slot.refs_18_) | copy-start | bytes 868
  5.0 59.3 %copy-start.3 = (f32[8,8,4096]{2,1,0:T(8,128)S(1)}, f32[8,8,4096]{2,1,0:T(8,128)}, u32[]{:S(2)}) copy-start(f32[8,8,4096]{2,1,0:T(8,128)} %hgx.9) | copy-start | bytes 3145732
  5.0 59.3 %copy-start.4 = (f32[8,8,2048]{2,1,0:T(8,128)S(1)}, f32[8,8,2048]{2,1,0:T(8,128)}, u32[]{:S(2)}) copy-start(f32[8,8,2048]{2,1,0:T(8,128)} %hgw.9) | copy-start | bytes 1572868
  5.0 59.2 %copy-start.7 = (f32[8,8,4096]{2,1,0:T(8,128)S(1)}, f32[8,8,4096]{2,1,0:T(8,128)}, u32[]{:S(2)}) copy-start(f32[8,8,4096]{2,1,0:T(8,128)} %hsx.1) | copy-start | bytes 3145732
  5.0 59.2 %copy-start.12 = (f32[8,8,2048]{2,1,0:T(8,128)S(1)}, f32[8,8,2048]{2,1,0:T(8,128)}, u32[]{:S(2)}) copy-start(f32[8,8,2048]{2,1,0:T(8,128)} %hsw.1) | copy-start | bytes 1572868
  53.3 6.4 %collective-permute-start.2 = (f32[8,4224]{1,0:T(8,128)S(1)}, f32[8,4224]{1,0:T(8,128)S(1)}, u32[]{:S(2)}, u32[]{:S(2)}) collective-permute-start(f32[8,4224]{1,0:T(8,128)S(1)} %transpose.4._), channel_id=1, source_target_pairs={{0,192},{32,224},{64,128},{96,160},{128,64},{160,96},{192,0},{224,... | collective-permute-start | bytes 405512 | tf_op jit(solution)/shard_map/ppermute | solution.py:558
  56.2 5.5 %collective-permute-start.1 = (f32[8,4224]{1,0:T(8,128)S(1)}, f32[8,4224]{1,0:T(8,128)S(1)}, u32[]{:S(2)}, u32[]{:S(2)}) collective-permute-start(f32[8,4224]{1,0:T(8,128)S(1)} %transpose.4._), channel_id=1, source_target_pairs={{0,128},{32,160},{64,192},{96,224},{128,0},{160,32},{192,64},{224,... | collective-permute-start | bytes 405512 | tf_op jit(solution)/shard_map/ppermute | solution.py:558
  56.5 5.1 %collective-permute-start = (f32[8,4224]{1,0:T(8,128)S(1)}, f32[8,4224]{1,0:T(8,128)S(1)}, u32[]{:S(2)}, u32[]{:S(2)}) collective-permute-start(f32[8,4224]{1,0:T(8,128)S(1)} %transpose.4._), channel_id=1, source_target_pairs={{0,64},{32,96},{64,0},{96,32},{128,192},{160,224},{192,128},{224,1... | collective-permute-start | bytes 405512 | tf_op jit(solution)/shard_map/ppermute | solution.py:558
  61.7 5.5 %collective-permute-start.3 = (f32[8,4224]{1,0:T(8,128)S(1)}, f32[8,4224]{1,0:T(8,128)S(1)}, u32[]{:S(2)}, u32[]{:S(2)}) collective-permute-start(f32[8,4224]{1,0:T(8,128)S(1)} %add_add_fusion.own), channel_id=1, source_target_pairs={{0,32},{32,0},{64,96},{96,64},{128,160},{160,128},{192,224},{224,1... | collective-permute-start | bytes 405512 | tf_op jit(solution)/shard_map/ppermute | solution.py:558
  72.8 23.1 %all-to-all-start.2 = ((f32[96,8,128]{2,1,0:T(8,128)}), f32[96,8,128]{2,1,0:T(8,128)}, u32[]{:S(2)}, u32[]{:S(2)}) async-start(f32[96,8,128]{2,1,0:T(8,128)} %copy-done.48), calls=%async_computation.2 | async-start | bytes 786432 | tf_op jit(solution)/shard_map/all_to_all | solution.py:554
  100.2 52.0 %copy-start.53 = (s32[2048]{0:T(1024)S(1)}, s32[2048]{0:T(1024)}, u32[]{:S(2)}) copy-start(s32[2048]{0:T(1024)} %param.27) | copy-start | bytes 24580
  100.3 51.9 %copy-start.69 = (s32[96]{0:T(128)S(1)}, s32[96]{0:T(128)}, u32[]{:S(2)}) copy-start(s32[96]{0:T(128)} %copy-done.67) | copy-start | bytes 1156
  100.3 2.9 %collective-permute-start.4 = (f32[2,128]{1,0:T(2,128)S(1)}, f32[2,128]{1,0:T(2,128)S(1)}, u32[]{:S(2)}, u32[]{:S(2)}) collective-permute-start(f32[2,128]{1,0:T(2,128)S(1)} %get-tuple-element.41), channel_id=1, source_target_pairs={{0,1},{1,0},{2,3},{3,2},{4,5},{5,4},{6,7},{7,6},{8,9},{9,8},{10,11... | collective-permute-start | bytes 3080 | tf_op jit(solution)/shard_map/ppermute | solution.py:659
  122.4 50.0 %slice-start = ((s8[4718592]{0:T(1024)(128)(4,1)}), s8[4194304]{0:T(1024)(128)(4,1)S(1)}, s32[]{:S(2)}) async-start(s8[4718592]{0:T(1024)(128)(4,1)} %bitcast.6), calls=%async_computation.8 | async-start | bytes 8388608
  129.7 42.8 %slice-start.1 = ((s8[4718592]{0:T(1024)(128)(4,1)}), s8[524288]{0:T(1024)(128)(4,1)S(1)}, s32[]{:S(2)}) async-start(s8[4718592]{0:T(1024)(128)(4,1)} %bitcast.6), calls=%async_computation.9 | async-start | bytes 1048576
  129.7 42.8 %copy-start.64 = (s32[1,1,72]{2,1,0:T(1,128)S(1)}, s32[1,1,72]{2,1,0:T(1,128)}, u32[]{:S(2)}) copy-start(s32[1,1,72]{2,1,0:T(1,128)} %param.22) | copy-start | bytes 868
  129.7 57.6 %slice-start.2 = ((s8[4718592]{0:T(1024)(128)(4,1)}), s8[4194304]{0:T(1024)(128)(4,1)S(1)}, s32[]{:S(2)}) async-start(s8[4718592]{0:T(1024)(128)(4,1)} %bitcast.8), calls=%async_computation.10 | async-start | bytes 8388608
  133.5 55.2 %copy-start.19 = (f32[8,4096]{1,0:T(8,128)}, f32[8,4096]{1,0:T(8,128)S(1)}, u32[]{:S(2)}) copy-start(f32[8,4096]{1,0:T(8,128)S(1)} %get-tuple-element.49.x.refs_4_) | copy-start | bytes 393220
  133.5 55.2 %copy-start.26 = (f32[8,2048]{1,0:T(8,128)}, f32[8,2048]{1,0:T(8,128)S(1)}, u32[]{:S(2)}) copy-start(f32[8,2048]{1,0:T(8,128)S(1)} %get-tuple-element.47.refs_2_.w.refs_9_) | copy-start | bytes 196612
  133.5 55.2 %copy-start.57 = (f32[8,2048]{1,0:T(8,128)}, f32[8,2048]{1,0:T(8,128)S(1)}, u32[]{:S(2)}) copy-start(f32[8,2048]{1,0:T(8,128)S(1)} %get-tuple-element.59.refs_18_) | copy-start | bytes 196612
  133.5 55.2 %copy-start.71 = (f32[8,128]{1,0:T(8,128)}, f32[8,128]{1,0:T(8,128)S(1)}, u32[]{:S(2)}) copy-start(f32[8,128]{1,0:T(8,128)S(1)} %get-tuple-element.56.refs_1_) | copy-start | bytes 12292
  133.5 53.8 %copy-start.43 = (f32[8,4096]{1,0:T(8,128)S(1)}, f32[8,4096]{1,0:T(8,128)}, u32[]{:S(2)}) copy-start(f32[8,4096]{1,0:T(8,128)} %linear.3) | copy-start | bytes 393220
  133.5 53.8 %copy-start.51 = (f32[4096]{0:T(1024)S(1)}, f32[4096]{0:T(1024)}, u32[]{:S(2)}) copy-start(f32[4096]{0:T(1024)} %param.23) | copy-start | bytes 49156
  133.5 53.8 %slice-start.3 = ((s8[4718592]{0:T(1024)(128)(4,1)}), s8[524288]{0:T(1024)(128)(4,1)S(1)}, s32[]{:S(2)}) async-start(s8[4718592]{0:T(1024)(128)(4,1)} %bitcast.8), calls=%async_computation.11 | async-start | bytes 1048576
  173.8 7.1 %collective-permute-start.7 = (f32[8,4096]{1,0:T(8,128)S(1)}, f32[8,4096]{1,0:T(8,128)S(1)}, u32[]{:S(2)}, u32[]{:S(2)}) collective-permute-start(f32[8,4096]{1,0:T(8,128)S(1)} %transpose.5._), channel_id=1, source_target_pairs={{0,192},{32,224},{64,128},{96,160},{128,64},{160,96},{192,0},{224,... | collective-permute-start | bytes 393224 | tf_op jit(solution)/shard_map/ppermute | solution.py:558
  174.3 6.6 %collective-permute-start.6 = (f32[8,4096]{1,0:T(8,128)S(1)}, f32[8,4096]{1,0:T(8,128)S(1)}, u32[]{:S(2)}, u32[]{:S(2)}) collective-permute-start(f32[8,4096]{1,0:T(8,128)S(1)} %transpose.5._), channel_id=1, source_target_pairs={{0,128},{32,160},{64,192},{96,224},{128,0},{160,32},{192,64},{224,... | collective-permute-start | bytes 393224 | tf_op jit(solution)/shard_map/ppermute | solution.py:558
  175.4 5.8 %collective-permute-start.5 = (f32[8,4096]{1,0:T(8,128)S(1)}, f32[8,4096]{1,0:T(8,128)S(1)}, u32[]{:S(2)}, u32[]{:S(2)}) collective-permute-start(f32[8,4096]{1,0:T(8,128)S(1)} %transpose.5._), channel_id=1, source_target_pairs={{0,64},{32,96},{64,0},{96,32},{128,192},{160,224},{192,128},{224,1... | collective-permute-start | bytes 393224 | tf_op jit(solution)/shard_map/ppermute | solution.py:558
  181.9 5.3 %collective-permute-start.8 = (f32[8,4096]{1,0:T(8,128)S(1)}, f32[8,4096]{1,0:T(8,128)S(1)}, u32[]{:S(2)}, u32[]{:S(2)}) collective-permute-start(f32[8,4096]{1,0:T(8,128)S(1)} %add_add_fusion.1.own), channel_id=1, source_target_pairs={{0,32},{32,0},{64,96},{96,64},{128,160},{160,128},{192,224},{224,1... | collective-permute-start | bytes 393224 | tf_op jit(solution)/shard_map/ppermute | solution.py:558
  190.1 22.3 %all-to-all-start.6 = ((f32[96,8,128]{2,1,0:T(8,128)}), f32[96,8,128]{2,1,0:T(8,128)S(1)}, u32[]{:S(2)}, u32[]{:S(2)}) async-start(f32[96,8,128]{2,1,0:T(8,128)} %copy-done.47), calls=%async_computation.6 | async-start | bytes 786432 | tf_op jit(solution)/shard_map/all_to_all | solution.py:554
  219.7 2.9 %collective-permute-start.9 = (f32[2,128]{1,0:T(2,128)S(1)}, f32[2,128]{1,0:T(2,128)S(1)}, u32[]{:S(2)}, u32[]{:S(2)}) collective-permute-start(f32[2,128]{1,0:T(2,128)S(1)} %get-tuple-element.55), channel_id=1, source_target_pairs={{0,1},{1,0},{2,3},{3,2},{4,5},{5,4},{6,7},{7,6},{8,9},{9,8},{10,11... | collective-permute-start | bytes 3080 | tf_op jit(solution)/shard_map/ppermute | solution.py:659
  (63 other events, 302.2 us)

commit v7 on v6

--- a/solution.py
+++ b/solution.py
@@ -124,8 +124,8 @@
 
 
 def open_kernel(per_run, run_length, share, parts, *refs):
-    (hbm_rows, hbm_cols, hbm_x, hbm_tiles, *far), (send, slot, tiles), refs = refs[:13], refs[13:16], refs[16:]
-    rows_buf, cols_buf, x, px, w, pw, pgx, pgw, hsx, hsw, hgx, hgw, left, count, asked, spot, sem = refs
+    (hbm_rows, hbm_cols, hbm_x, hbm_tiles, *far), (send, slot, tiles), refs = refs[:10], refs[10:13], refs[13:]
+    rows_buf, cols_buf, x, pgx, pgw, hsx, hsw, hgx, hgw, left, count, asked, spot, sem = refs
     memory = hgx.shape[0]
     problems = x.shape[0]
     half = problems // 2
@@ -133,12 +133,12 @@
     runs = send.shape[0] // wide
     first = lax.axis_index("con") * share
     mine = pl.ds(pl.multiple_of(first * LANES, LANES), share * LANES)
-    far_px, far_w, far_pw, far_pgx, far_pgw, far_hsx, far_hsw, far_hgx, far_hgw = far
+    far_pgx, far_pgw, far_hsx, far_hsw, far_hgx, far_hgw = far
     size = tiles.shape[0] // parts
     moves = [(hbm_rows, rows_buf), (hbm_cols, cols_buf), (hbm_x, x)]
     moves += [(hbm_tiles.at[pl.ds(i * size, size)], tiles.at[pl.ds(i * size, size)]) for i in range(parts)]
-    moves += [(far_w, w), (far_pw, pw), (far_pgw, pgw), (far_hsw, hsw), (far_hgw, hgw)]
-    moves += [(far_px.at[:, mine], px), (far_pgx.at[:, mine], pgx), (far_hsx.at[:, :, mine], hsx), (far_hgx.at[:, :, mine], hgx)]
+    moves += [(far_pgw, pgw), (far_hsw, hsw), (far_hgw, hgw)]
+    moves += [(far_pgx.at[:, mine], pgx), (far_hsx.at[:, :, mine], hsx), (far_hgx.at[:, :, mine], hgx)]
     copies = [pltpu.make_async_copy(a, b, sem.at[i]) for i, (a, b) in enumerate(moves)]
     for copy in copies:
         copy.start()
@@ -164,14 +164,7 @@
         return spot[t]
 
     copies[2].wait()
-    send_products(x, cols, where, tiles, send, left, [copy.wait for copy in copies[3 : 3 + parts]], flipped=False)
-    for copy in copies[3 + parts :]:
-        copy.wait()
-
-    lanes = lane_ids((problems, LANES))
-    out = jnp.zeros((problems, LANES), f32)
-
-    places = [(False, b) for b in range(w.shape[1] // LANES)] + [(True, b) for b in range(share)]
+    places = [(False, b) for b in range(pgw.shape[1] // LANES)] + [(True, b) for b in range(share)]
 
     def read(ref_x, ref_w, place):
         is_x, b = place
@@ -183,17 +176,25 @@
     def add(lane, value):
         acc[lane] = acc[lane] + value if lane in acc else value
 
-    for place in places:
-        g = [read(hgx.at[m], hgw.at[m], place) for m in range(memory)]
-        for m in range(memory):
-            for n in range(m, memory):
-                add(pair_lane(m, n), g[m] * g[n])
-    for place in places:
-        p = read(pgx, pgw, place)
-        for m in range(memory):
-            add(LANE_P + m, read(hgx.at[m], hgw.at[m], place) * p)
-            h = read(hsx.at[m], hsw.at[m], place)
-            add(LANE_S + m, h * h)
+    def early_sums():
+        for copy in copies[2 + parts :]:
+            copy.wait()
+        for place in places:
+            g = [read(hgx.at[m], hgw.at[m], place) for m in range(memory)]
+            for m in range(memory):
+                for n in range(m, memory):
+                    add(pair_lane(m, n), g[m] * g[n])
+        for place in places:
+            p = read(pgx, pgw, place)
+            for m in range(memory):
+                add(LANE_P + m, read(hgx.at[m], hgw.at[m], place) * p)
+                h = read(hsx.at[m], hsw.at[m], place)
+                add(LANE_S + m, h * h)
+
+    send_products(x, cols, where, tiles, send, left, [copy.wait for copy in copies[3 : 2 + parts]] + [early_sums], flipped=False)
+
+    lanes = lane_ids((problems, LANES))
+    out = jnp.zeros((problems, LANES), f32)
     for lane, value in acc.items():
         out = jnp.where(lanes == lane, total(value), out)
     index = entry_ids(problems) - lax.axis_index("var") * per_run
@@ -314,46 +315,32 @@
     return [(False, b) for b in range(w.shape[1] // LANES)] + [(True, first + b) for b in range(share)]
 
 
-def before_kernel(share, start, w, center, width, pw, pgw, x, px, pgx, hgx, hgw, qgx, qgw, _, out):
-    sums = Sums(w.shape[0])
-    for is_x, b in blocks_of(w, share):
-        if is_x:
-            p = at(pgx, b)
-            u, s, d = -p, at(x, b) - at(px, b), p - at(qgx, b)
-        else:
-            p, here = block_of(pgw, b), block_of(w, b)
-            slack = slack_of(here, block_of(center, b), block_of(width, b))
-            u, s, d = relax * (block_of(start, b) - slack) - p, here - block_of(pw, b), p - block_of(qgw, b)
-        for m in range(MEMORY):
-            sums.add(U_H + m, u * at(hgx.at[m] if is_x else hgw.at[m], b))
-        for i, value in ((U_U, u * u), (U_P, u * p), (S_S, s * s), (U_D, u * d)):
-            sums.add(i, value)
-    zero = jnp.zeros(sums.shape, f32)
-    out[0], out[1] = sums.tiles([zero, zero])
-
-
 def scalar_kernel(
-    share, got, rows, start, w, center, width, level, pgw, pgx, resid, diag, hgx, hgw, qgx, qgw, before, send, image, *scratch
+    share, got, rows, start, w, center, width, level, pw, pgw, x, px, pgx, resid, diag, hgx, hgw, qgx, qgw, send, image, *scratch
 ):
     result = add_rows(lambda s: got[s], rows, scratch)
     sums = Sums(w.shape[0])
     for is_x, b in blocks_of(w, share):
         if is_x:
             r, p = at(resid, b), at(pgx, b)
-            u, v, d = -p, relax * r, p - at(qgx, b)
+            u, v, s, d = -p, relax * r, at(x, b) - at(px, b), p - at(qgx, b)
             sums.add(R_R, r * r)
             sums.add(C_C, at(diag, b) * r * r)
         else:
             ar, p = result(b), block_of(pgw, b)
             image[:, b * LANES : (b + 1) * LANES] = ar
-            slack = slack_of(block_of(w, b), block_of(center, b), block_of(width, b))
-            u, v, d = relax * (block_of(start, b) - slack) - p, relax * ar, p - block_of(qgw, b)
+            here = block_of(w, b)
+            slack = slack_of(here, block_of(center, b), block_of(width, b))
+            u, v, s, d = relax * (block_of(start, b) - slack) - p, relax * ar, here - block_of(pw, b), p - block_of(qgw, b)
             sums.add(C_C, rho_of(level, b) * ar * ar)
         for m in range(MEMORY):
-            sums.add(V_H + m, v * at(hgx.at[m] if is_x else hgw.at[m], b))
-        for i, value in ((U_V, u * v), (V_P, v * p), (V_V, v * v), (V_D, v * d)):
+            h = at(hgx.at[m] if is_x else hgw.at[m], b)
+            sums.add(U_H + m, u * h)
+            sums.add(V_H + m, v * h)
+        for i, value in ((U_U, u * u), (U_V, u * v), (U_P, u * p), (V_P, v * p), (V_V, v * v), (S_S, s * s), (U_D, u * d), (V_D, v * d)):
             sums.add(i, value)
-    rows_out = [jnp.sum(tile, axis=0, keepdims=True) for tile in sums.tiles([before[0], before[1]])]
+    zero = jnp.zeros(sums.shape, f32)
+    rows_out = [jnp.sum(tile, axis=0, keepdims=True) for tile in sums.tiles([zero, zero])]
     send[...] = jnp.concatenate(rows_out, axis=0)
 
 
@@ -566,7 +553,7 @@
     one_core = [list(range(k, con_count * var_count, 2)) for k in range(2)]
     share = col_count // con_count
     parts = max(d for d in range(1, 4) if count % d == 0)
-    far = [state_x, blocks, prev_x, state_w, prev_w, prev_gx, prev_gw, hist_sx, hist_sw, hist_gx, hist_gw]
+    far = [state_x, blocks, prev_gx, prev_gw, hist_sx, hist_sw, hist_gx, hist_gw]
     x_mine, w_mine = pltpu.VMEM((problems, share * tile_size), f32), pltpu.VMEM((problems, con_cols), f32)
     memory = hist_gx.shape[0]
     hx_mine = pltpu.VMEM((memory, problems, share * tile_size), f32)
@@ -580,12 +567,12 @@
             pltpu.SMEM((1, count), jnp.int32),
             pltpu.SMEM((1, count), jnp.int32),
             pltpu.VMEM((problems, var_cols), f32),
-            x_mine, w_mine, w_mine, x_mine, w_mine, hx_mine, hw_mine, hx_mine, hw_mine,
+            x_mine, w_mine, hx_mine, hw_mine, hx_mine, hw_mine,
             left,
             pltpu.SMEM((var_count,), jnp.int32),
             pltpu.SMEM((slots,), jnp.int32),
             pltpu.SMEM((count,), jnp.int32),
-            pltpu.SemaphoreType.DMA((3 + parts + 9,)),
+            pltpu.SemaphoreType.DMA((3 + parts + 6,)),
         ],
     )
     got = exchange(sent)
@@ -622,12 +609,6 @@
             [pltpu.VMEM((col_count, problems, tile_size), f32)],
         )
         own, other = over_con(sent)
-        (before,) = call(
-            functools.partial(before_kernel, share),
-            "before",
-            vs(start, w, bound_center, bound_width, pw, pgw, x, px, pgx, hist_gx, hist_gw, qgx, qgw, sent),
-            [((2, problems, tile_size), f32, "v")],
-        )
         if first:
             flipped, hist_x, hist_w = call(
                 prepare_kernel,
@@ -652,7 +633,7 @@
             "scalars",
             vs(got)
             + ss(rows)
-            + vs(start, w, bound_center, bound_width, level, pgw, pgx, resid, diag, hist_gx, hist_gw, qgx, qgw, before),
+            + vs(start, w, bound_center, bound_width, level, pw, pgw, x, px, pgx, resid, diag, hist_gx, hist_gw, qgx, qgw),
             [((2, LANES), f32, "v"), w_like],
             sums,
         )

time: 253 us -> 215 us (0.85)
  blocking collectives: 119 us -> 164 us
  local copies, waits for them, and re-layouts: 42 us -> 0.18 us
  waiting for transfers between devices: 37.9 us -> 16.4 us
  starting transfers between devices: 31.6 us -> 14.6 us
    all_to_all x4 -> x6, blocking collectives: 82.9 us -> 127 us  [exchange(): return lax.all_to_all(x, 'var', 0, 0, tiled=True)]
    unnamed x166 -> x36, local copies, waits for them, and re-layouts: 42 us -> 0.1 us
    all_to_all x2 -> x0, waiting for transfers between devices: 21.5 us -> none  [exchange(): return lax.all_to_all(x, 'var', 0, 0, tiled=True)]
    all_to_all x2 -> x0, starting transfers between devices: 17 us -> none  [exchange(): return lax.all_to_all(x, 'var', 0, 0, tiled=True)]
    pallas_call x14 -> x12, Pallas kernels: 19.4 us -> 18.8 us  [call(): pl.pallas_call(kernel, out_shape=[jax.ShapeDtypeStruct(shape, dtype) for...]
  transfers between devices with their start and end apart: 12 -> 10, of which waited for: 10 -> 8; matrix products, arithmetic and copies ran while one was open for 0% -> 0% of each run, Pallas kernels for 1% -> 1%
where the time goes in v7:
time: 215 us
  blocking collectives  164 us (76%)
  Pallas kernels  18.8 us (9%)
  waiting for transfers between devices  16.4 us (8%)
  starting transfers between devices  14.6 us (7%)
    all_to_all x6, blocking collectives, exchange(): return lax.all_to_all(x, 'var', 0, 0, tiled=True)  127 us
    all_to_all x2, blocking collectives, per_device(): lax.all_to_all(copies, ('con', 'var'), 0, 0, tiled=True, axis_index_group...  36.7 us
    pallas_call x12, Pallas kernels, call(): pl.pallas_call(kernel, out_shape=[jax.ShapeDtypeStruct(shape, dtype) for...  18.8 us
    ppermute x8, waiting for transfers between devices, partner(): return lax.ppermute(x, 'con', [(i, i ^ k) for i in range(con_count)])  14.8 us
    ppermute x8, starting transfers between devices, partner(): return lax.ppermute(x, 'con', [(i, i ^ k) for i in range(con_count)])  10.4 us
  transfers between devices with their start and end apart: 10, of which 8 were waited for; matrix products, arithmetic and copies ran while one was open for 0% of the time, Pallas kernels for 1%

profile of v7, /device:TPU:1, one launch (start us, length us, event | category | flops | bytes accessed | tf_op | source)
XLA Modules:
  0.0 214.7 jit_solution(6171298668474593704)
XLA Ops:
  0.7 4.1 %open.1 = (f32[224,4,128]{2,1,0:T(4,128)S(1)}, s32[72]{0:T(128)S(1)}, f32[72,128,128]{2,1,0:T(8,128)S(1)}) custom-call(s32[1,72]{1,0:T(1,128)} %bitcast.21, s32[1,72]{1,0:T(1,128)} %bitcast.14, f32[8,4096]{1,0:T(8,128)} %refs_5_.5, f32[72,128,128]{2,1,0:T(8,128)} %bitcast.20, f32[8,4096]{1,0:T(8,128)} %qgx.3, f32[8,2048]{1,0:T(8,128)} %qgw.3, ...), custom_call_target="tpu_custom_call" | custom-call | tf_op jit(solution)/shard_map/open/pallas_call | solution.py:481
  4.8 26.5 %all_to_all.40.refs_0_ = f32[224,4,128]{2,1,0:T(4,128)S(1)} all-to-all(f32[224,4,128]{2,1,0:T(4,128)S(1)} %get-tuple-element.31), channel_id=1, replica_groups=mesh['con'=8,'var'=32] {'var'}, dimensions={0} | all-to-all | bytes 917504 | tf_op jit(solution)/shard_map/all_to_all | solution.py:541
  31.3 1.6 penalty_first.1
  32.9 18.9 %all_to_all.41.refs_0_ = f32[96,8,128]{2,1,0:T(8,128)S(1)} all-to-all(f32[96,8,128]{2,1,0:T(8,128)S(1)} %get-tuple-element.32), channel_id=1, replica_groups=mesh['con'=8,'var'=32] {'var'}, dimensions={0} | all-to-all | bytes 786432 | tf_op jit(solution)/shard_map/all_to_all | solution.py:541
  51.8 1.3 transpose.4._
  53.2 2.8 %collective-permute-start.2 = (f32[8,4224]{1,0:T(8,128)S(1)}, f32[8,4224]{1,0:T(8,128)S(1)}, u32[]{:S(2)}, u32[]{:S(2)}) collective-permute-start(f32[8,4224]{1,0:T(8,128)S(1)} %transpose.4._), channel_id=1, source_target_pairs={{0,192},{32,224},{64,128},{96,160},{128,64},{160,96},{192,0},{224,... | collective-permute-start | bytes 405512 | tf_op jit(solution)/shard_map/ppermute | solution.py:545
  56.6 2.9 %collective-permute-done.2 = f32[8,4224]{1,0:T(8,128)S(1)} collective-permute-done((f32[8,4224]{1,0:T(8,128)S(1)}, f32[8,4224]{1,0:T(8,128)S(1)}, u32[]{:S(2)}, u32[]{:S(2)}) %collective-permute-start.2) | collective-permute-done | bytes 135200 | tf_op jit(solution)/shard_map/ppermute | solution.py:545
  59.6 1.9 collective-permute-done.1
  61.5 2.6 %collective-permute-start.3 = (f32[8,4224]{1,0:T(8,128)S(1)}, f32[8,4224]{1,0:T(8,128)S(1)}, u32[]{:S(2)}, u32[]{:S(2)}) collective-permute-start(f32[8,4224]{1,0:T(8,128)S(1)} %add_add_fusion.own), channel_id=1, source_target_pairs={{0,32},{32,0},{64,96},{96,64},{128,160},{160,128},{192,224},{224,1... | collective-permute-start | bytes 405512 | tf_op jit(solution)/shard_map/ppermute | solution.py:545
  64.0 1.4 prepare.1
  65.5 1.5 collective-permute-done.3.other
  67.0 1.4 residual.2
  68.4 22.1 %all_to_all.42.got = f32[96,8,128]{2,1,0:T(8,128)S(1)} all-to-all(f32[96,8,128]{2,1,0:T(8,128)S(1)} %get-tuple-element.37), channel_id=1, replica_groups=mesh['con'=8,'var'=32] {'var'}, dimensions={0} | all-to-all | bytes 786432 | tf_op jit(solution)/shard_map/all_to_all | solution.py:541
  90.4 1.0 scalars.2
  91.4 2.1 collective-permute-start.4
  93.6 0.8 collective-permute-done.4
  94.4 19.5 %all_to_all.43.refs_0_ = f32[128,2,128]{2,1,0:T(2,128)S(1)} all-to-all(f32[128,2,128]{2,1,0:T(2,128)S(1)} %broadcast_in_dim.4), channel_id=1, replica_groups={{0,2,4,6,8,10,12,14,16,18,20,22,24,26,28,30,32,34,36,38,40,42,44,46,48,..., dimensions={0} | all-to-all | bytes 262144 | tf_op jit(solution)/shard_map/all_to_all | solution.py:642
  114.0 1.9 update.2
  115.9 18.5 %all_to_all.44.refs_0_ = f32[96,8,128]{2,1,0:T(8,128)S(1)} all-to-all(f32[96,8,128]{2,1,0:T(8,128)S(1)} %get-tuple-element.46), channel_id=1, replica_groups=mesh['con'=8,'var'=32] {'var'}, dimensions={0} | all-to-all | bytes 786432 | tf_op jit(solution)/shard_map/all_to_all | solution.py:541
  135.2 18.9 %all_to_all.45.refs_0_ = f32[96,8,128]{2,1,0:T(8,128)S(1)} all-to-all(f32[96,8,128]{2,1,0:T(8,128)S(1)} %get-tuple-element.48), channel_id=1, replica_groups=mesh['con'=8,'var'=32] {'var'}, dimensions={0} | all-to-all | bytes 786432 | tf_op jit(solution)/shard_map/all_to_all | solution.py:541
  154.1 1.3 transpose.5
  155.8 1.2 collective-permute-start.6
  157.0 1.7 collective-permute-start.5
  158.7 3.7 %collective-permute-done.7 = f32[8,4096]{1,0:T(8,128)S(1)} collective-permute-done((f32[8,4096]{1,0:T(8,128)S(1)}, f32[8,4096]{1,0:T(8,128)S(1)}, u32[]{:S(2)}, u32[]{:S(2)}) %collective-permute-start.7) | collective-permute-done | bytes 131104 | tf_op jit(solution)/shard_map/ppermute | solution.py:545
  162.9 1.0 collective-permute-start.8
  163.9 4.4 %collective-permute-done.8.other = f32[8,4096]{1,0:T(8,128)S(1)} collective-permute-done((f32[8,4096]{1,0:T(8,128)S(1)}, f32[8,4096]{1,0:T(8,128)S(1)}, u32[]{:S(2)}, u32[]{:S(2)}) %collective-permute-start.8) | collective-permute-done | bytes 131104 | tf_op jit(solution)/shard_map/ppermute | solution.py:545
  168.3 1.4 residual.3
  169.7 22.1 %all_to_all.46.got = f32[96,8,128]{2,1,0:T(8,128)S(1)} all-to-all(f32[96,8,128]{2,1,0:T(8,128)S(1)} %get-tuple-element.50), channel_id=1, replica_groups=mesh['con'=8,'var'=32] {'var'}, dimensions={0} | all-to-all | bytes 786432 | tf_op jit(solution)/shard_map/all_to_all | solution.py:541
  191.8 1.0 scalars.3
  192.7 2.1 collective-permute-start.9
  195.7 17.2 %all_to_all.47.refs_0_ = f32[128,2,128]{2,1,0:T(2,128)S(1)} all-to-all(f32[128,2,128]{2,1,0:T(2,128)S(1)} %broadcast_in_dim.5), channel_id=1, replica_groups={{0,2,4,6,8,10,12,14,16,18,20,22,24,26,28,30,32,34,36,38,40,42,44,46,48,..., dimensions={0} | all-to-all | bytes 262144 | tf_op jit(solution)/shard_map/all_to_all | solution.py:642
  212.9 1.8 update.3
  (50 shorter events, 3.4 us)
Async XLA Ops:
  0.6 30.7 %copy-start.6 = (f32[8,2048]{1,0:T(8,128)S(1)}, f32[8,2048]{1,0:T(8,128)}, u32[]{:S(2)}) copy-start(f32[8,2048]{1,0:T(8,128)} %refs_15_.3) | copy-start | bytes 196612
  0.6 30.7 %copy-start.5 = (f32[8,2048]{1,0:T(8,128)S(1)}, f32[8,2048]{1,0:T(8,128)}, u32[]{:S(2)}) copy-start(f32[8,2048]{1,0:T(8,128)} %refs_14_.3) | copy-start | bytes 196612
  0.7 30.6 %copy-start.9 = (f32[8,2048]{1,0:T(8,128)S(1)}, f32[8,2048]{1,0:T(8,128)}, u32[]{:S(2)}) copy-start(f32[8,2048]{1,0:T(8,128)} %refs_10_.3) | copy-start | bytes 196612
  0.7 30.6 %copy-start.14 = (s32[2048]{0:T(1024)S(1)}, s32[2048]{0:T(1024)}, u32[]{:S(2)}) copy-start(s32[2048]{0:T(1024)} %param.27) | copy-start | bytes 24580
  0.7 51.1 %copy-start.15 = (s32[1,1,72]{2,1,0:T(1,128)S(1)}, s32[1,1,72]{2,1,0:T(1,128)}, u32[]{:S(2)}) copy-start(s32[1,1,72]{2,1,0:T(1,128)} %param.22) | copy-start | bytes 868
  4.8 59.3 %copy-start = (f32[8,8,4096]{2,1,0:T(8,128)S(1)}, f32[8,8,4096]{2,1,0:T(8,128)}, u32[]{:S(2)}) copy-start(f32[8,8,4096]{2,1,0:T(8,128)} %hgx.5) | copy-start | bytes 3145732
  4.8 59.2 %copy-start.1 = (f32[8,8,2048]{2,1,0:T(8,128)S(1)}, f32[8,8,2048]{2,1,0:T(8,128)}, u32[]{:S(2)}) copy-start(f32[8,8,2048]{2,1,0:T(8,128)} %hgw.5) | copy-start | bytes 1572868
  4.8 59.2 %copy-start.3 = (f32[8,8,4096]{2,1,0:T(8,128)S(1)}, f32[8,8,4096]{2,1,0:T(8,128)}, u32[]{:S(2)}) copy-start(f32[8,8,4096]{2,1,0:T(8,128)} %hsx.1) | copy-start | bytes 3145732
  4.8 59.2 %copy-start.7 = (f32[8,8,2048]{2,1,0:T(8,128)S(1)}, f32[8,8,2048]{2,1,0:T(8,128)}, u32[]{:S(2)}) copy-start(f32[8,8,2048]{2,1,0:T(8,128)} %hsw.1) | copy-start | bytes 1572868
  53.1 13.8 %copy-start.2 = (f32[8,4096]{1,0:T(8,128)S(1)}, f32[8,4096]{1,0:T(8,128)}, u32[]{:S(2)}) copy-start(f32[8,4096]{1,0:T(8,128)} %refs_5_.5) | copy-start | bytes 393220
  53.1 13.8 %copy-start.11 = (f32[8,4096]{1,0:T(8,128)S(1)}, f32[8,4096]{1,0:T(8,128)}, u32[]{:S(2)}) copy-start(f32[8,4096]{1,0:T(8,128)} %linear.3) | copy-start | bytes 393220
  53.1 13.8 %copy-start.12 = (f32[4096]{0:T(1024)S(1)}, f32[4096]{0:T(1024)}, u32[]{:S(2)}) copy-start(f32[4096]{0:T(1024)} %param.23) | copy-start | bytes 49156
  53.2 6.4 %collective-permute-start.2 = (f32[8,4224]{1,0:T(8,128)S(1)}, f32[8,4224]{1,0:T(8,128)S(1)}, u32[]{:S(2)}, u32[]{:S(2)}) collective-permute-start(f32[8,4224]{1,0:T(8,128)S(1)} %transpose.4._), channel_id=1, source_target_pairs={{0,192},{32,224},{64,128},{96,160},{128,64},{160,96},{192,0},{224,... | collective-permute-start | bytes 405512 | tf_op jit(solution)/shard_map/ppermute | solution.py:545
  56.0 5.5 %collective-permute-start.1 = (f32[8,4224]{1,0:T(8,128)S(1)}, f32[8,4224]{1,0:T(8,128)S(1)}, u32[]{:S(2)}, u32[]{:S(2)}) collective-permute-start(f32[8,4224]{1,0:T(8,128)S(1)} %transpose.4._), channel_id=1, source_target_pairs={{0,128},{32,160},{64,192},{96,224},{128,0},{160,32},{192,64},{224,... | collective-permute-start | bytes 405512 | tf_op jit(solution)/shard_map/ppermute | solution.py:545
  56.3 5.1 %collective-permute-start = (f32[8,4224]{1,0:T(8,128)S(1)}, f32[8,4224]{1,0:T(8,128)S(1)}, u32[]{:S(2)}, u32[]{:S(2)}) collective-permute-start(f32[8,4224]{1,0:T(8,128)S(1)} %transpose.4._), channel_id=1, source_target_pairs={{0,64},{32,96},{64,0},{96,32},{128,192},{160,224},{192,128},{224,1... | collective-permute-start | bytes 405512 | tf_op jit(solution)/shard_map/ppermute | solution.py:545
  61.5 5.5 %collective-permute-start.3 = (f32[8,4224]{1,0:T(8,128)S(1)}, f32[8,4224]{1,0:T(8,128)S(1)}, u32[]{:S(2)}, u32[]{:S(2)}) collective-permute-start(f32[8,4224]{1,0:T(8,128)S(1)} %add_add_fusion.own), channel_id=1, source_target_pairs={{0,32},{32,0},{64,96},{96,64},{128,160},{160,128},{192,224},{224,1... | collective-permute-start | bytes 405512 | tf_op jit(solution)/shard_map/ppermute | solution.py:545
  65.4 25.0 %copy-start.4 = (f32[8,4096]{1,0:T(8,128)S(1)}, f32[8,4096]{1,0:T(8,128)}, u32[]{:S(2)}) copy-start(f32[8,4096]{1,0:T(8,128)} %qgx.3) | copy-start | bytes 393220
  65.4 25.0 %copy-start.8 = (f32[8,2048]{1,0:T(8,128)S(1)}, f32[8,2048]{1,0:T(8,128)}, u32[]{:S(2)}) copy-start(f32[8,2048]{1,0:T(8,128)} %qgw.3) | copy-start | bytes 196612
  65.4 25.0 %copy-start.10 = (f32[8,4096]{1,0:T(8,128)S(1)}, f32[8,4096]{1,0:T(8,128)}, u32[]{:S(2)}) copy-start(f32[8,4096]{1,0:T(8,128)} %refs_5_.4) | copy-start | bytes 393220
  65.5 25.0 %copy-start.13 = (f32[8,2048]{1,0:T(8,128)S(1)}, f32[8,2048]{1,0:T(8,128)}, u32[]{:S(2)}) copy-start(f32[8,2048]{1,0:T(8,128)} %refs_10_.2) | copy-start | bytes 196612
  66.9 47.0 %copy-start.16 = (s32[8]{0:T(128)S(1)}, s32[8]{0:T(128)}, u32[]{:S(2)}) copy-start(s32[8]{0:T(128)} %refs_2_.7) | copy-start | bytes 100
  67.0 47.0 %copy-start.17 = (s32[8]{0:T(128)S(1)}, s32[8]{0:T(128)}, u32[]{:S(2)}) copy-start(s32[8]{0:T(128)} %refs_3_.7) | copy-start | bytes 100
  91.4 2.9 %collective-permute-start.4 = (f32[2,128]{1,0:T(2,128)S(1)}, f32[2,128]{1,0:T(2,128)S(1)}, u32[]{:S(2)}, u32[]{:S(2)}) collective-permute-start(f32[2,128]{1,0:T(2,128)S(1)} %get-tuple-element.41), channel_id=1, source_target_pairs={{0,1},{1,0},{2,3},{3,2},{4,5},{5,4},{6,7},{7,6},{8,9},{9,8},{10,11... | collective-permute-start | bytes 3080 | tf_op jit(solution)/shard_map/ppermute | solution.py:640
  155.4 7.1 %collective-permute-start.7 = (f32[8,4096]{1,0:T(8,128)S(1)}, f32[8,4096]{1,0:T(8,128)S(1)}, u32[]{:S(2)}, u32[]{:S(2)}) collective-permute-start(f32[8,4096]{1,0:T(8,128)S(1)} %transpose.5), channel_id=1, source_target_pairs={{0,192},{32,224},{64,128},{96,160},{128,64},{160,96},{192,0},{224,... | collective-permute-start | bytes 393224 | tf_op jit(solution)/shard_map/ppermute | solution.py:545
  155.8 6.6 %collective-permute-start.6 = (f32[8,4096]{1,0:T(8,128)S(1)}, f32[8,4096]{1,0:T(8,128)S(1)}, u32[]{:S(2)}, u32[]{:S(2)}) collective-permute-start(f32[8,4096]{1,0:T(8,128)S(1)} %transpose.5), channel_id=1, source_target_pairs={{0,128},{32,160},{64,192},{96,224},{128,0},{160,32},{192,64},{224,... | collective-permute-start | bytes 393224 | tf_op jit(solution)/shard_map/ppermute | solution.py:545
  157.0 5.8 %collective-permute-start.5 = (f32[8,4096]{1,0:T(8,128)S(1)}, f32[8,4096]{1,0:T(8,128)S(1)}, u32[]{:S(2)}, u32[]{:S(2)}) collective-permute-start(f32[8,4096]{1,0:T(8,128)S(1)} %transpose.5), channel_id=1, source_target_pairs={{0,64},{32,96},{64,0},{96,32},{128,192},{160,224},{192,128},{224,1... | collective-permute-start | bytes 393224 | tf_op jit(solution)/shard_map/ppermute | solution.py:545
  162.9 5.4 %collective-permute-start.8 = (f32[8,4096]{1,0:T(8,128)S(1)}, f32[8,4096]{1,0:T(8,128)S(1)}, u32[]{:S(2)}, u32[]{:S(2)}) collective-permute-start(f32[8,4096]{1,0:T(8,128)S(1)} %add_add_fusion.1.own), channel_id=1, source_target_pairs={{0,32},{32,0},{64,96},{96,64},{128,160},{160,128},{192,224},{224,1... | collective-permute-start | bytes 393224 | tf_op jit(solution)/shard_map/ppermute | solution.py:545
  192.7 2.9 %collective-permute-start.9 = (f32[2,128]{1,0:T(2,128)S(1)}, f32[2,128]{1,0:T(2,128)S(1)}, u32[]{:S(2)}, u32[]{:S(2)}) collective-permute-start(f32[2,128]{1,0:T(2,128)S(1)} %get-tuple-element.55), channel_id=1, source_target_pairs={{0,1},{1,0},{2,3},{3,2},{4,5},{5,4},{6,7},{7,6},{8,9},{9,8},{10,11... | collective-permute-start | bytes 3080 | tf_op jit(solution)/shard_map/ppermute | solution.py:640

commit v8 on v7

--- a/solution.py
+++ b/solution.py
@@ -84,11 +84,12 @@
     def one(t):
         axis = 0 if flipped else 1
         value = times(left[cols[t]], jnp.concatenate(halves(tiles[t]), axis=axis), axis)
+        spot = where(t)
         if flipped:
-            send[where(t)] = value
+            send[spot] = value
         else:
-            send[where(t)] = value[: value.shape[0] // 2]
-            send[where(t) + 1] = value[value.shape[0] // 2 :]
+            send[spot] = value[: value.shape[0] // 2]
+            send[spot + 1] = value[value.shape[0] // 2 :]
 
     size = tiles.shape[0] // len(waits)
     for i, wait in enumerate(waits):
@@ -97,12 +98,10 @@
         tile_loop(size, lambda t, i=i: one(t + i * size))
 
 
-def add_rows(received, rows, sums):
-    for ref in sums:
-        ref[...] = jnp.zeros_like(ref)
-    for s in range(rows.shape[0]):
+def add_rows(received, row_of, slots, sums):
+    for s in range(slots):
         ref = sums[s % len(sums)]
-        row = rows[s]
+        row = row_of(s)
         ref[row] = ref[row] + received(s)
     return lambda b: functools.reduce(lambda p, q: p + q, [ref[b] for ref in sums])
 
@@ -125,7 +124,7 @@
 
 def open_kernel(per_run, run_length, share, parts, *refs):
     (hbm_rows, hbm_cols, hbm_x, hbm_tiles, *far), (send, slot, tiles), refs = refs[:10], refs[10:13], refs[13:]
-    rows_buf, cols_buf, x, pgx, pgw, hsx, hsw, hgx, hgw, left, count, asked, spot, sem = refs
+    rows_buf, cols_buf, x, pgx, pgw, hsx, hsw, hgx, hgw, left, count, asked, sem = refs
     memory = hgx.shape[0]
     problems = x.shape[0]
     half = problems // 2
@@ -148,22 +147,18 @@
         count[i] = 0
     for i in range(runs * per_run):
         asked[i] = 0
-    copies[0].wait()
-    copies[1].wait()
-    for t in range(tiles.shape[0]):
+    def where(t):
         row = rows[t]
         owner = row >> (run_length.bit_length() - 1)
         rank = count[owner]
         count[owner] = rank + 1
         place = owner * per_run + rank
         slot[t] = place
-        spot[t] = owner * wide + rank * 2
         asked[place] = row & (run_length - 1)
-
-    def where(t):
-        return spot[t]
-
-    copies[2].wait()
+        return owner * wide + rank * 2
+
+    for copy in copies[:3]:
+        copy.wait()
     places = [(False, b) for b in range(pgw.shape[1] // LANES)] + [(True, b) for b in range(share)]
 
     def read(ref_x, ref_w, place):
@@ -226,18 +221,25 @@
         marks_int[...] = early_sum.astype(jnp.int32)
         copy = pltpu.make_async_copy(marks_int, marks, sem)
         copy.start()
+        for ref in sums:
+            ref[...] = jnp.zeros_like(ref)
+        problems = w.shape[0]
         copy.wait()
-        problems = w.shape[0]
-        for s in range(slots):
-            rows[s] = marks[s % problems, LANE_ENTRY + s // problems]
+
+        def row_of(s):
+            row = marks[s % problems, LANE_ENTRY + s // problems]
+            rows[s] = row
+            return row
 
         def received(s):
             unit = s // per_run * wide + s % per_run * 2
             return jnp.concatenate([got[unit], got[unit + 1]], axis=0)
 
-        result = add_rows(received, rows, sums)
+        result = add_rows(received, row_of, slots, sums)
     else:
-        result = add_rows(lambda s: got[s], rows, sums)
+        for ref in sums:
+            ref[...] = jnp.zeros_like(ref)
+        result = add_rows(lambda s: got[s], lambda s: rows[s], slots, sums)
     blocks = w.shape[1] // LANES
     for b in range(blocks):
         start = result(b)
@@ -318,7 +320,9 @@
 def scalar_kernel(
     share, got, rows, start, w, center, width, level, pw, pgw, x, px, pgx, resid, diag, hgx, hgw, qgx, qgw, send, image, *scratch
 ):
-    result = add_rows(lambda s: got[s], rows, scratch)
+    for ref in scratch:
+        ref[...] = jnp.zeros_like(ref)
+    result = add_rows(lambda s: got[s], lambda s: rows[s], rows.shape[0], scratch)
     sums = Sums(w.shape[0])
     for is_x, b in blocks_of(w, share):
         if is_x:
@@ -571,7 +575,6 @@
             left,
             pltpu.SMEM((var_count,), jnp.int32),
             pltpu.SMEM((slots,), jnp.int32),
-            pltpu.SMEM((count,), jnp.int32),
             pltpu.SemaphoreType.DMA((3 + parts + 6,)),
         ],
     )

time: 215 us -> 215 us (level)
  no operation moved by 1% of the time
where the time goes in v8:
time: 215 us
  blocking collectives  164 us (76%)
  Pallas kernels  18.9 us (9%)
  waiting for transfers between devices  16.4 us (8%)
  starting transfers between devices  14.6 us (7%)
    all_to_all x6, blocking collectives, exchange(): return lax.all_to_all(x, 'var', 0, 0, tiled=True)  127 us
    all_to_all x2, blocking collectives, per_device(): lax.all_to_all(copies, ('con', 'var'), 0, 0, tiled=True, axis_index_group...  36.7 us
    pallas_call x12, Pallas kernels, call(): pl.pallas_call(kernel, out_shape=[jax.ShapeDtypeStruct(shape, dtype) for...  18.9 us
    ppermute x8, waiting for transfers between devices, partner(): return lax.ppermute(x, 'con', [(i, i ^ k) for i in range(con_count)])  14.8 us
    ppermute x8, starting transfers between devices, partner(): return lax.ppermute(x, 'con', [(i, i ^ k) for i in range(con_count)])  10.4 us
  transfers between devices with their start and end apart: 10, of which 8 were waited for; matrix products, arithmetic and copies ran while one was open for 0% of the time, Pallas kernels for 1%

profile of v8, /device:TPU:1, one launch (start us, length us, event | category | flops | bytes accessed | tf_op | source)
XLA Modules:
  0.0 214.7 jit_solution(10639134384562543704)
XLA Ops:
  0.7 4.2 %open.1 = (f32[224,4,128]{2,1,0:T(4,128)S(1)}, s32[72]{0:T(128)S(1)}, f32[72,128,128]{2,1,0:T(8,128)S(1)}) custom-call(s32[1,72]{1,0:T(1,128)} %bitcast.21, s32[1,72]{1,0:T(1,128)} %bitcast.14, f32[8,4096]{1,0:T(8,128)} %refs_5_.5, f32[72,128,128]{2,1,0:T(8,128)} %bitcast.20, f32[8,4096]{1,0:T(8,128)} %qgx.3, f32[8,2048]{1,0:T(8,128)} %qgw.3, ...), custom_call_target="tpu_custom_call" | custom-call | tf_op jit(solution)/shard_map/open/pallas_call | solution.py:485
  4.9 26.5 %all_to_all.40.refs_0_ = f32[224,4,128]{2,1,0:T(4,128)S(1)} all-to-all(f32[224,4,128]{2,1,0:T(4,128)S(1)} %get-tuple-element.31), channel_id=1, replica_groups=mesh['con'=8,'var'=32] {'var'}, dimensions={0} | all-to-all | bytes 917504 | tf_op jit(solution)/shard_map/all_to_all | solution.py:545
  31.4 1.5 penalty_first.1
  32.9 18.9 %all_to_all.41.refs_0_ = f32[96,8,128]{2,1,0:T(8,128)S(1)} all-to-all(f32[96,8,128]{2,1,0:T(8,128)S(1)} %get-tuple-element.32), channel_id=1, replica_groups=mesh['con'=8,'var'=32] {'var'}, dimensions={0} | all-to-all | bytes 786432 | tf_op jit(solution)/shard_map/all_to_all | solution.py:545
  51.9 1.3 transpose.4._
  53.2 2.8 %collective-permute-start.2 = (f32[8,4224]{1,0:T(8,128)S(1)}, f32[8,4224]{1,0:T(8,128)S(1)}, u32[]{:S(2)}, u32[]{:S(2)}) collective-permute-start(f32[8,4224]{1,0:T(8,128)S(1)} %transpose.4._), channel_id=1, source_target_pairs={{0,192},{32,224},{64,128},{96,160},{128,64},{160,96},{192,0},{224,... | collective-permute-start | bytes 405512 | tf_op jit(solution)/shard_map/ppermute | solution.py:549
  56.7 2.9 %collective-permute-done.2 = f32[8,4224]{1,0:T(8,128)S(1)} collective-permute-done((f32[8,4224]{1,0:T(8,128)S(1)}, f32[8,4224]{1,0:T(8,128)S(1)}, u32[]{:S(2)}, u32[]{:S(2)}) %collective-permute-start.2) | collective-permute-done | bytes 135200 | tf_op jit(solution)/shard_map/ppermute | solution.py:549
  59.6 1.9 collective-permute-done.1
  61.5 2.5 %collective-permute-start.3 = (f32[8,4224]{1,0:T(8,128)S(1)}, f32[8,4224]{1,0:T(8,128)S(1)}, u32[]{:S(2)}, u32[]{:S(2)}) collective-permute-start(f32[8,4224]{1,0:T(8,128)S(1)} %add_add_fusion.own), channel_id=1, source_target_pairs={{0,32},{32,0},{64,96},{96,64},{128,160},{160,128},{192,224},{224,1... | collective-permute-start | bytes 405512 | tf_op jit(solution)/shard_map/ppermute | solution.py:549
  64.1 1.4 prepare.1
  65.5 1.5 collective-permute-done.3.other
  67.0 1.4 residual.2
  68.4 22.1 %all_to_all.42.got = f32[96,8,128]{2,1,0:T(8,128)S(1)} all-to-all(f32[96,8,128]{2,1,0:T(8,128)S(1)} %get-tuple-element.37), channel_id=1, replica_groups=mesh['con'=8,'var'=32] {'var'}, dimensions={0} | all-to-all | bytes 786432 | tf_op jit(solution)/shard_map/all_to_all | solution.py:545
  90.5 1.0 scalars.2
  91.5 2.1 collective-permute-start.4
  93.6 0.8 collective-permute-done.4
  94.5 19.5 %all_to_all.43.refs_0_ = f32[128,2,128]{2,1,0:T(2,128)S(1)} all-to-all(f32[128,2,128]{2,1,0:T(2,128)S(1)} %broadcast_in_dim.4), channel_id=1, replica_groups={{0,2,4,6,8,10,12,14,16,18,20,22,24,26,28,30,32,34,36,38,40,42,44,46,48,..., dimensions={0} | all-to-all | bytes 262144 | tf_op jit(solution)/shard_map/all_to_all | solution.py:645
  114.0 1.9 update.2
  115.9 18.5 %all_to_all.44.refs_0_ = f32[96,8,128]{2,1,0:T(8,128)S(1)} all-to-all(f32[96,8,128]{2,1,0:T(8,128)S(1)} %get-tuple-element.46), channel_id=1, replica_groups=mesh['con'=8,'var'=32] {'var'}, dimensions={0} | all-to-all | bytes 786432 | tf_op jit(solution)/shard_map/all_to_all | solution.py:545
  135.3 18.9 %all_to_all.45.refs_0_ = f32[96,8,128]{2,1,0:T(8,128)S(1)} all-to-all(f32[96,8,128]{2,1,0:T(8,128)S(1)} %get-tuple-element.48), channel_id=1, replica_groups=mesh['con'=8,'var'=32] {'var'}, dimensions={0} | all-to-all | bytes 786432 | tf_op jit(solution)/shard_map/all_to_all | solution.py:545
  154.1 1.3 transpose.5
  155.9 1.2 collective-permute-start.6
  157.1 1.7 collective-permute-start.5
  158.8 3.7 %collective-permute-done.7 = f32[8,4096]{1,0:T(8,128)S(1)} collective-permute-done((f32[8,4096]{1,0:T(8,128)S(1)}, f32[8,4096]{1,0:T(8,128)S(1)}, u32[]{:S(2)}, u32[]{:S(2)}) %collective-permute-start.7) | collective-permute-done | bytes 131104 | tf_op jit(solution)/shard_map/ppermute | solution.py:549
  162.9 1.0 collective-permute-start.8
  164.0 4.4 %collective-permute-done.8.other = f32[8,4096]{1,0:T(8,128)S(1)} collective-permute-done((f32[8,4096]{1,0:T(8,128)S(1)}, f32[8,4096]{1,0:T(8,128)S(1)}, u32[]{:S(2)}, u32[]{:S(2)}) %collective-permute-start.8) | collective-permute-done | bytes 131104 | tf_op jit(solution)/shard_map/ppermute | solution.py:549
  168.4 1.4 residual.3
  169.7 22.1 %all_to_all.46.got = f32[96,8,128]{2,1,0:T(8,128)S(1)} all-to-all(f32[96,8,128]{2,1,0:T(8,128)S(1)} %get-tuple-element.50), channel_id=1, replica_groups=mesh['con'=8,'var'=32] {'var'}, dimensions={0} | all-to-all | bytes 786432 | tf_op jit(solution)/shard_map/all_to_all | solution.py:545
  191.8 1.0 scalars.3
  192.8 2.1 collective-permute-start.9
  195.8 17.2 %all_to_all.47.refs_0_ = f32[128,2,128]{2,1,0:T(2,128)S(1)} all-to-all(f32[128,2,128]{2,1,0:T(2,128)S(1)} %broadcast_in_dim.5), channel_id=1, replica_groups={{0,2,4,6,8,10,12,14,16,18,20,22,24,26,28,30,32,34,36,38,40,42,44,46,48,..., dimensions={0} | all-to-all | bytes 262144 | tf_op jit(solution)/shard_map/all_to_all | solution.py:645
  213.0 1.8 update.3
  (50 shorter events, 3.4 us)
Async XLA Ops:
  0.6 30.7 %copy-start.6 = (f32[8,2048]{1,0:T(8,128)S(1)}, f32[8,2048]{1,0:T(8,128)}, u32[]{:S(2)}) copy-start(f32[8,2048]{1,0:T(8,128)} %refs_15_.3) | copy-start | bytes 196612
  0.6 30.7 %copy-start.5 = (f32[8,2048]{1,0:T(8,128)S(1)}, f32[8,2048]{1,0:T(8,128)}, u32[]{:S(2)}) copy-start(f32[8,2048]{1,0:T(8,128)} %refs_14_.3) | copy-start | bytes 196612
  0.7 30.7 %copy-start.9 = (f32[8,2048]{1,0:T(8,128)S(1)}, f32[8,2048]{1,0:T(8,128)}, u32[]{:S(2)}) copy-start(f32[8,2048]{1,0:T(8,128)} %refs_10_.3) | copy-start | bytes 196612
  0.7 30.7 %copy-start.14 = (s32[2048]{0:T(1024)S(1)}, s32[2048]{0:T(1024)}, u32[]{:S(2)}) copy-start(s32[2048]{0:T(1024)} %param.27) | copy-start | bytes 24580
  0.7 51.2 %copy-start.15 = (s32[1,1,72]{2,1,0:T(1,128)S(1)}, s32[1,1,72]{2,1,0:T(1,128)}, u32[]{:S(2)}) copy-start(s32[1,1,72]{2,1,0:T(1,128)} %param.22) | copy-start | bytes 868
  4.9 59.2 %copy-start = (f32[8,8,4096]{2,1,0:T(8,128)S(1)}, f32[8,8,4096]{2,1,0:T(8,128)}, u32[]{:S(2)}) copy-start(f32[8,8,4096]{2,1,0:T(8,128)} %hgx.5) | copy-start | bytes 3145732
  4.9 59.2 %copy-start.1 = (f32[8,8,2048]{2,1,0:T(8,128)S(1)}, f32[8,8,2048]{2,1,0:T(8,128)}, u32[]{:S(2)}) copy-start(f32[8,8,2048]{2,1,0:T(8,128)} %hgw.5) | copy-start | bytes 1572868
  4.9 59.2 %copy-start.3 = (f32[8,8,4096]{2,1,0:T(8,128)S(1)}, f32[8,8,4096]{2,1,0:T(8,128)}, u32[]{:S(2)}) copy-start(f32[8,8,4096]{2,1,0:T(8,128)} %hsx.1) | copy-start | bytes 3145732
  4.9 59.2 %copy-start.7 = (f32[8,8,2048]{2,1,0:T(8,128)S(1)}, f32[8,8,2048]{2,1,0:T(8,128)}, u32[]{:S(2)}) copy-start(f32[8,8,2048]{2,1,0:T(8,128)} %hsw.1) | copy-start | bytes 1572868
  53.2 13.8 %copy-start.2 = (f32[8,4096]{1,0:T(8,128)S(1)}, f32[8,4096]{1,0:T(8,128)}, u32[]{:S(2)}) copy-start(f32[8,4096]{1,0:T(8,128)} %refs_5_.5) | copy-start | bytes 393220
  53.2 13.8 %copy-start.11 = (f32[8,4096]{1,0:T(8,128)S(1)}, f32[8,4096]{1,0:T(8,128)}, u32[]{:S(2)}) copy-start(f32[8,4096]{1,0:T(8,128)} %linear.3) | copy-start | bytes 393220
  53.2 13.8 %copy-start.12 = (f32[4096]{0:T(1024)S(1)}, f32[4096]{0:T(1024)}, u32[]{:S(2)}) copy-start(f32[4096]{0:T(1024)} %param.23) | copy-start | bytes 49156
  53.2 6.4 %collective-permute-start.2 = (f32[8,4224]{1,0:T(8,128)S(1)}, f32[8,4224]{1,0:T(8,128)S(1)}, u32[]{:S(2)}, u32[]{:S(2)}) collective-permute-start(f32[8,4224]{1,0:T(8,128)S(1)} %transpose.4._), channel_id=1, source_target_pairs={{0,192},{32,224},{64,128},{96,160},{128,64},{160,96},{192,0},{224,... | collective-permute-start | bytes 405512 | tf_op jit(solution)/shard_map/ppermute | solution.py:549
  56.0 5.5 %collective-permute-start.1 = (f32[8,4224]{1,0:T(8,128)S(1)}, f32[8,4224]{1,0:T(8,128)S(1)}, u32[]{:S(2)}, u32[]{:S(2)}) collective-permute-start(f32[8,4224]{1,0:T(8,128)S(1)} %transpose.4._), channel_id=1, source_target_pairs={{0,128},{32,160},{64,192},{96,224},{128,0},{160,32},{192,64},{224,... | collective-permute-start | bytes 405512 | tf_op jit(solution)/shard_map/ppermute | solution.py:549
  56.4 5.1 %collective-permute-start = (f32[8,4224]{1,0:T(8,128)S(1)}, f32[8,4224]{1,0:T(8,128)S(1)}, u32[]{:S(2)}, u32[]{:S(2)}) collective-permute-start(f32[8,4224]{1,0:T(8,128)S(1)} %transpose.4._), channel_id=1, source_target_pairs={{0,64},{32,96},{64,0},{96,32},{128,192},{160,224},{192,128},{224,1... | collective-permute-start | bytes 405512 | tf_op jit(solution)/shard_map/ppermute | solution.py:549
  61.5 5.5 %collective-permute-start.3 = (f32[8,4224]{1,0:T(8,128)S(1)}, f32[8,4224]{1,0:T(8,128)S(1)}, u32[]{:S(2)}, u32[]{:S(2)}) collective-permute-start(f32[8,4224]{1,0:T(8,128)S(1)} %add_add_fusion.own), channel_id=1, source_target_pairs={{0,32},{32,0},{64,96},{96,64},{128,160},{160,128},{192,224},{224,1... | collective-permute-start | bytes 405512 | tf_op jit(solution)/shard_map/ppermute | solution.py:549
  65.5 25.0 %copy-start.4 = (f32[8,4096]{1,0:T(8,128)S(1)}, f32[8,4096]{1,0:T(8,128)}, u32[]{:S(2)}) copy-start(f32[8,4096]{1,0:T(8,128)} %qgx.3) | copy-start | bytes 393220
  65.5 25.0 %copy-start.8 = (f32[8,2048]{1,0:T(8,128)S(1)}, f32[8,2048]{1,0:T(8,128)}, u32[]{:S(2)}) copy-start(f32[8,2048]{1,0:T(8,128)} %qgw.3) | copy-start | bytes 196612
  65.5 25.0 %copy-start.10 = (f32[8,4096]{1,0:T(8,128)S(1)}, f32[8,4096]{1,0:T(8,128)}, u32[]{:S(2)}) copy-start(f32[8,4096]{1,0:T(8,128)} %refs_5_.4) | copy-start | bytes 393220
  65.5 25.0 %copy-start.13 = (f32[8,2048]{1,0:T(8,128)S(1)}, f32[8,2048]{1,0:T(8,128)}, u32[]{:S(2)}) copy-start(f32[8,2048]{1,0:T(8,128)} %refs_10_.2) | copy-start | bytes 196612
  67.0 47.0 %copy-start.16 = (s32[8]{0:T(128)S(1)}, s32[8]{0:T(128)}, u32[]{:S(2)}) copy-start(s32[8]{0:T(128)} %refs_2_.7) | copy-start | bytes 100
  67.0 47.0 %copy-start.17 = (s32[8]{0:T(128)S(1)}, s32[8]{0:T(128)}, u32[]{:S(2)}) copy-start(s32[8]{0:T(128)} %refs_3_.7) | copy-start | bytes 100
  91.5 2.9 %collective-permute-start.4 = (f32[2,128]{1,0:T(2,128)S(1)}, f32[2,128]{1,0:T(2,128)S(1)}, u32[]{:S(2)}, u32[]{:S(2)}) collective-permute-start(f32[2,128]{1,0:T(2,128)S(1)} %get-tuple-element.41), channel_id=1, source_target_pairs={{0,1},{1,0},{2,3},{3,2},{4,5},{5,4},{6,7},{7,6},{8,9},{9,8},{10,11... | collective-permute-start | bytes 3080 | tf_op jit(solution)/shard_map/ppermute | solution.py:643
  155.4 7.1 %collective-permute-start.7 = (f32[8,4096]{1,0:T(8,128)S(1)}, f32[8,4096]{1,0:T(8,128)S(1)}, u32[]{:S(2)}, u32[]{:S(2)}) collective-permute-start(f32[8,4096]{1,0:T(8,128)S(1)} %transpose.5), channel_id=1, source_target_pairs={{0,192},{32,224},{64,128},{96,160},{128,64},{160,96},{192,0},{224,... | collective-permute-start | bytes 393224 | tf_op jit(solution)/shard_map/ppermute | solution.py:549
  155.9 6.6 %collective-permute-start.6 = (f32[8,4096]{1,0:T(8,128)S(1)}, f32[8,4096]{1,0:T(8,128)S(1)}, u32[]{:S(2)}, u32[]{:S(2)}) collective-permute-start(f32[8,4096]{1,0:T(8,128)S(1)} %transpose.5), channel_id=1, source_target_pairs={{0,128},{32,160},{64,192},{96,224},{128,0},{160,32},{192,64},{224,... | collective-permute-start | bytes 393224 | tf_op jit(solution)/shard_map/ppermute | solution.py:549
  157.1 5.8 %collective-permute-start.5 = (f32[8,4096]{1,0:T(8,128)S(1)}, f32[8,4096]{1,0:T(8,128)S(1)}, u32[]{:S(2)}, u32[]{:S(2)}) collective-permute-start(f32[8,4096]{1,0:T(8,128)S(1)} %transpose.5), channel_id=1, source_target_pairs={{0,64},{32,96},{64,0},{96,32},{128,192},{160,224},{192,128},{224,1... | collective-permute-start | bytes 393224 | tf_op jit(solution)/shard_map/ppermute | solution.py:549
  162.9 5.4 %collective-permute-start.8 = (f32[8,4096]{1,0:T(8,128)S(1)}, f32[8,4096]{1,0:T(8,128)S(1)}, u32[]{:S(2)}, u32[]{:S(2)}) collective-permute-start(f32[8,4096]{1,0:T(8,128)S(1)} %add_add_fusion.1.own), channel_id=1, source_target_pairs={{0,32},{32,0},{64,96},{96,64},{128,160},{160,128},{192,224},{224,1... | collective-permute-start | bytes 393224 | tf_op jit(solution)/shard_map/ppermute | solution.py:549
  192.8 2.9 %collective-permute-start.9 = (f32[2,128]{1,0:T(2,128)S(1)}, f32[2,128]{1,0:T(2,128)S(1)}, u32[]{:S(2)}, u32[]{:S(2)}) collective-permute-start(f32[2,128]{1,0:T(2,128)S(1)} %get-tuple-element.55), channel_id=1, source_target_pairs={{0,1},{1,0},{2,3},{3,2},{4,5},{5,4},{6,7},{7,6},{8,9},{9,8},{10,11... | collective-permute-start | bytes 3080 | tf_op jit(solution)/shard_map/ppermute | solution.py:643

commit v9 on v7

--- a/solution.py
+++ b/solution.py
@@ -136,9 +136,9 @@
     far_pgx, far_pgw, far_hsx, far_hsw, far_hgx, far_hgw = far
     size = tiles.shape[0] // parts
     moves = [(hbm_rows, rows_buf), (hbm_cols, cols_buf), (hbm_x, x)]
-    moves += [(hbm_tiles.at[pl.ds(i * size, size)], tiles.at[pl.ds(i * size, size)]) for i in range(parts)]
     moves += [(far_pgw, pgw), (far_hsw, hsw), (far_hgw, hgw)]
     moves += [(far_pgx.at[:, mine], pgx), (far_hsx.at[:, :, mine], hsx), (far_hgx.at[:, :, mine], hgx)]
+    moves += [(hbm_tiles.at[pl.ds(i * size, size)], tiles.at[pl.ds(i * size, size)]) for i in range(parts)]
     copies = [pltpu.make_async_copy(a, b, sem.at[i]) for i, (a, b) in enumerate(moves)]
     for copy in copies:
         copy.start()
@@ -176,8 +176,8 @@
     def add(lane, value):
         acc[lane] = acc[lane] + value if lane in acc else value
 
-    def early_sums():
-        for copy in copies[2 + parts :]:
+    def while_tiles_come():
+        for copy in copies[3:9]:
             copy.wait()
         for place in places:
             g = [read(hgx.at[m], hgw.at[m], place) for m in range(memory)]
@@ -190,20 +190,21 @@
                 add(LANE_P + m, read(hgx.at[m], hgw.at[m], place) * p)
                 h = read(hsx.at[m], hsw.at[m], place)
                 add(LANE_S + m, h * h)
-
-    send_products(x, cols, where, tiles, send, left, [copy.wait for copy in copies[3 : 2 + parts]] + [early_sums], flipped=False)
-
-    lanes = lane_ids((problems, LANES))
-    out = jnp.zeros((problems, LANES), f32)
-    for lane, value in acc.items():
-        out = jnp.where(lanes == lane, total(value), out)
-    index = entry_ids(problems) - lax.axis_index("var") * per_run
-    for r in range(runs):
-        mark = out
-        for i in range(per_run):
-            mark = jnp.where(index == i, asked[r * per_run + i].astype(f32), mark)
-        turned = pltpu.roll(mark, LANES // 2, 1)
-        send[r * wide + 2 * per_run] = jnp.where(lanes[:half] < LANES // 2, mark[:half], turned[half:])
+        lanes = lane_ids((problems, LANES))
+        out = jnp.zeros((problems, LANES), f32)
+        for lane, value in acc.items():
+            out = jnp.where(lanes == lane, total(value), out)
+        index = entry_ids(problems) - lax.axis_index("var") * per_run
+        for r in range(runs):
+            mark = out
+            for i in range(per_run):
+                mark = jnp.where(index == i, asked[r * per_run + i].astype(f32), mark)
+            turned = pltpu.roll(mark, LANES // 2, 1)
+            send[r * wide + 2 * per_run] = jnp.where(lanes[:half] < LANES // 2, mark[:half], turned[half:])
+        copies[9].wait()
+
+    waits = [while_tiles_come] + [copy.wait for copy in copies[10:]]
+    send_products(x, cols, where, tiles, send, left, waits, flipped=False)
 
 
 def entry_ids(problems):
@@ -552,7 +553,7 @@
 
     one_core = [list(range(k, con_count * var_count, 2)) for k in range(2)]
     share = col_count // con_count
-    parts = max(d for d in range(1, 4) if count % d == 0)
+    parts = max(d for d in range(1, 7) if count % d == 0)
     far = [state_x, blocks, prev_gx, prev_gw, hist_sx, hist_sw, hist_gx, hist_gw]
     x_mine, w_mine = pltpu.VMEM((problems, share * tile_size), f32), pltpu.VMEM((problems, con_cols), f32)
     memory = hist_gx.shape[0]

time: 215 us -> 215 us (level)
  no operation moved by 1% of the time
where the time goes in v9:
time: 215 us
  blocking collectives  164 us (76%)
  Pallas kernels  19.1 us (9%)
  waiting for transfers between devices  16.4 us (8%)
  starting transfers between devices  14.6 us (7%)
    all_to_all x6, blocking collectives, exchange(): return lax.all_to_all(x, 'var', 0, 0, tiled=True)  127 us
    all_to_all x2, blocking collectives, per_device(): lax.all_to_all(copies, ('con', 'var'), 0, 0, tiled=True, axis_index_group...  36.7 us
    pallas_call x12, Pallas kernels, call(): pl.pallas_call(kernel, out_shape=[jax.ShapeDtypeStruct(shape, dtype) for...  19.1 us
    ppermute x8, waiting for transfers between devices, partner(): return lax.ppermute(x, 'con', [(i, i ^ k) for i in range(con_count)])  14.8 us
    ppermute x8, starting transfers between devices, partner(): return lax.ppermute(x, 'con', [(i, i ^ k) for i in range(con_count)])  10.4 us
  transfers between devices with their start and end apart: 10, of which 8 were waited for; matrix products, arithmetic and copies ran while one was open for 0% of the time, Pallas kernels for 1%

profile of v9, /device:TPU:1, one launch (start us, length us, event | category | flops | bytes accessed | tf_op | source)
XLA Modules:
  0.0 215.0 jit_solution(2507710912791365678)
XLA Ops:
  0.7 4.4 %open.1 = (f32[224,4,128]{2,1,0:T(4,128)S(1)}, s32[72]{0:T(128)S(1)}, f32[72,128,128]{2,1,0:T(8,128)S(1)}) custom-call(s32[1,72]{1,0:T(1,128)} %bitcast.21, s32[1,72]{1,0:T(1,128)} %bitcast.14, f32[8,4096]{1,0:T(8,128)} %refs_5_.5, f32[72,128,128]{2,1,0:T(8,128)} %bitcast.20, f32[8,4096]{1,0:T(8,128)} %qgx.3, f32[8,2048]{1,0:T(8,128)} %qgw.3, ...), custom_call_target="tpu_custom_call" | custom-call | tf_op jit(solution)/shard_map/open/pallas_call | solution.py:482
  5.1 26.5 %all_to_all.40.refs_0_ = f32[224,4,128]{2,1,0:T(4,128)S(1)} all-to-all(f32[224,4,128]{2,1,0:T(4,128)S(1)} %get-tuple-element.31), channel_id=1, replica_groups=mesh['con'=8,'var'=32] {'var'}, dimensions={0} | all-to-all | bytes 917504 | tf_op jit(solution)/shard_map/all_to_all | solution.py:542
  31.6 1.6 penalty_first.1
  33.2 18.9 %all_to_all.41.refs_0_ = f32[96,8,128]{2,1,0:T(8,128)S(1)} all-to-all(f32[96,8,128]{2,1,0:T(8,128)S(1)} %get-tuple-element.32), channel_id=1, replica_groups=mesh['con'=8,'var'=32] {'var'}, dimensions={0} | all-to-all | bytes 786432 | tf_op jit(solution)/shard_map/all_to_all | solution.py:542
  52.1 1.3 transpose.4._
  53.4 2.8 %collective-permute-start.2 = (f32[8,4224]{1,0:T(8,128)S(1)}, f32[8,4224]{1,0:T(8,128)S(1)}, u32[]{:S(2)}, u32[]{:S(2)}) collective-permute-start(f32[8,4224]{1,0:T(8,128)S(1)} %transpose.4._), channel_id=1, source_target_pairs={{0,192},{32,224},{64,128},{96,160},{128,64},{160,96},{192,0},{224,... | collective-permute-start | bytes 405512 | tf_op jit(solution)/shard_map/ppermute | solution.py:546
  56.9 2.9 %collective-permute-done.2 = f32[8,4224]{1,0:T(8,128)S(1)} collective-permute-done((f32[8,4224]{1,0:T(8,128)S(1)}, f32[8,4224]{1,0:T(8,128)S(1)}, u32[]{:S(2)}, u32[]{:S(2)}) %collective-permute-start.2) | collective-permute-done | bytes 135200 | tf_op jit(solution)/shard_map/ppermute | solution.py:546
  59.9 1.9 collective-permute-done.1
  61.8 2.5 %collective-permute-start.3 = (f32[8,4224]{1,0:T(8,128)S(1)}, f32[8,4224]{1,0:T(8,128)S(1)}, u32[]{:S(2)}, u32[]{:S(2)}) collective-permute-start(f32[8,4224]{1,0:T(8,128)S(1)} %add_add_fusion.own), channel_id=1, source_target_pairs={{0,32},{32,0},{64,96},{96,64},{128,160},{160,128},{192,224},{224,1... | collective-permute-start | bytes 405512 | tf_op jit(solution)/shard_map/ppermute | solution.py:546
  64.3 1.4 prepare.1
  65.7 1.5 collective-permute-done.3.other
  67.3 1.4 residual.2
  68.6 22.1 %all_to_all.42.got = f32[96,8,128]{2,1,0:T(8,128)S(1)} all-to-all(f32[96,8,128]{2,1,0:T(8,128)S(1)} %get-tuple-element.37), channel_id=1, replica_groups=mesh['con'=8,'var'=32] {'var'}, dimensions={0} | all-to-all | bytes 786432 | tf_op jit(solution)/shard_map/all_to_all | solution.py:542
  90.7 1.0 scalars.2
  91.7 2.1 collective-permute-start.4
  93.8 0.8 collective-permute-done.4
  94.7 19.5 %all_to_all.43.refs_0_ = f32[128,2,128]{2,1,0:T(2,128)S(1)} all-to-all(f32[128,2,128]{2,1,0:T(2,128)S(1)} %broadcast_in_dim.4), channel_id=1, replica_groups={{0,2,4,6,8,10,12,14,16,18,20,22,24,26,28,30,32,34,36,38,40,42,44,46,48,..., dimensions={0} | all-to-all | bytes 262144 | tf_op jit(solution)/shard_map/all_to_all | solution.py:643
  114.3 1.9 update.2
  116.2 18.5 %all_to_all.44.refs_0_ = f32[96,8,128]{2,1,0:T(8,128)S(1)} all-to-all(f32[96,8,128]{2,1,0:T(8,128)S(1)} %get-tuple-element.46), channel_id=1, replica_groups=mesh['con'=8,'var'=32] {'var'}, dimensions={0} | all-to-all | bytes 786432 | tf_op jit(solution)/shard_map/all_to_all | solution.py:542
  135.5 18.9 %all_to_all.45.refs_0_ = f32[96,8,128]{2,1,0:T(8,128)S(1)} all-to-all(f32[96,8,128]{2,1,0:T(8,128)S(1)} %get-tuple-element.48), channel_id=1, replica_groups=mesh['con'=8,'var'=32] {'var'}, dimensions={0} | all-to-all | bytes 786432 | tf_op jit(solution)/shard_map/all_to_all | solution.py:542
  154.4 1.3 transpose.5
  156.1 1.2 collective-permute-start.6
  157.3 1.7 collective-permute-start.5
  159.0 3.7 %collective-permute-done.7 = f32[8,4096]{1,0:T(8,128)S(1)} collective-permute-done((f32[8,4096]{1,0:T(8,128)S(1)}, f32[8,4096]{1,0:T(8,128)S(1)}, u32[]{:S(2)}, u32[]{:S(2)}) %collective-permute-start.7) | collective-permute-done | bytes 131104 | tf_op jit(solution)/shard_map/ppermute | solution.py:546
  163.2 1.0 collective-permute-start.8
  164.2 4.4 %collective-permute-done.8.other = f32[8,4096]{1,0:T(8,128)S(1)} collective-permute-done((f32[8,4096]{1,0:T(8,128)S(1)}, f32[8,4096]{1,0:T(8,128)S(1)}, u32[]{:S(2)}, u32[]{:S(2)}) %collective-permute-start.8) | collective-permute-done | bytes 131104 | tf_op jit(solution)/shard_map/ppermute | solution.py:546
  168.6 1.4 residual.3
  170.0 22.1 %all_to_all.46.got = f32[96,8,128]{2,1,0:T(8,128)S(1)} all-to-all(f32[96,8,128]{2,1,0:T(8,128)S(1)} %get-tuple-element.50), channel_id=1, replica_groups=mesh['con'=8,'var'=32] {'var'}, dimensions={0} | all-to-all | bytes 786432 | tf_op jit(solution)/shard_map/all_to_all | solution.py:542
  192.0 1.0 scalars.3
  193.0 2.1 collective-permute-start.9
  196.0 17.2 %all_to_all.47.refs_0_ = f32[128,2,128]{2,1,0:T(2,128)S(1)} all-to-all(f32[128,2,128]{2,1,0:T(2,128)S(1)} %broadcast_in_dim.5), channel_id=1, replica_groups={{0,2,4,6,8,10,12,14,16,18,20,22,24,26,28,30,32,34,36,38,40,42,44,46,48,..., dimensions={0} | all-to-all | bytes 262144 | tf_op jit(solution)/shard_map/all_to_all | solution.py:643
  213.2 1.8 update.3
  (50 shorter events, 3.4 us)
Async XLA Ops:
  0.6 30.9 %copy-start.6 = (f32[8,2048]{1,0:T(8,128)S(1)}, f32[8,2048]{1,0:T(8,128)}, u32[]{:S(2)}) copy-start(f32[8,2048]{1,0:T(8,128)} %refs_15_.3) | copy-start | bytes 196612
  0.6 30.9 %copy-start.5 = (f32[8,2048]{1,0:T(8,128)S(1)}, f32[8,2048]{1,0:T(8,128)}, u32[]{:S(2)}) copy-start(f32[8,2048]{1,0:T(8,128)} %refs_14_.3) | copy-start | bytes 196612
  0.7 30.9 %copy-start.9 = (f32[8,2048]{1,0:T(8,128)S(1)}, f32[8,2048]{1,0:T(8,128)}, u32[]{:S(2)}) copy-start(f32[8,2048]{1,0:T(8,128)} %refs_10_.3) | copy-start | bytes 196612
  0.7 30.9 %copy-start.14 = (s32[2048]{0:T(1024)S(1)}, s32[2048]{0:T(1024)}, u32[]{:S(2)}) copy-start(s32[2048]{0:T(1024)} %param.27) | copy-start | bytes 24580
  0.7 51.4 %copy-start.15 = (s32[1,1,72]{2,1,0:T(1,128)S(1)}, s32[1,1,72]{2,1,0:T(1,128)}, u32[]{:S(2)}) copy-start(s32[1,1,72]{2,1,0:T(1,128)} %param.22) | copy-start | bytes 868
  5.1 59.2 %copy-start = (f32[8,8,4096]{2,1,0:T(8,128)S(1)}, f32[8,8,4096]{2,1,0:T(8,128)}, u32[]{:S(2)}) copy-start(f32[8,8,4096]{2,1,0:T(8,128)} %hgx.5) | copy-start | bytes 3145732
  5.1 59.2 %copy-start.1 = (f32[8,8,2048]{2,1,0:T(8,128)S(1)}, f32[8,8,2048]{2,1,0:T(8,128)}, u32[]{:S(2)}) copy-start(f32[8,8,2048]{2,1,0:T(8,128)} %hgw.5) | copy-start | bytes 1572868
  5.1 59.2 %copy-start.3 = (f32[8,8,4096]{2,1,0:T(8,128)S(1)}, f32[8,8,4096]{2,1,0:T(8,128)}, u32[]{:S(2)}) copy-start(f32[8,8,4096]{2,1,0:T(8,128)} %hsx.1) | copy-start | bytes 3145732
  5.1 59.2 %copy-start.7 = (f32[8,8,2048]{2,1,0:T(8,128)S(1)}, f32[8,8,2048]{2,1,0:T(8,128)}, u32[]{:S(2)}) copy-start(f32[8,8,2048]{2,1,0:T(8,128)} %hsw.1) | copy-start | bytes 1572868
  53.4 13.8 %copy-start.2 = (f32[8,4096]{1,0:T(8,128)S(1)}, f32[8,4096]{1,0:T(8,128)}, u32[]{:S(2)}) copy-start(f32[8,4096]{1,0:T(8,128)} %refs_5_.5) | copy-start | bytes 393220
  53.4 13.8 %copy-start.11 = (f32[8,4096]{1,0:T(8,128)S(1)}, f32[8,4096]{1,0:T(8,128)}, u32[]{:S(2)}) copy-start(f32[8,4096]{1,0:T(8,128)} %linear.3) | copy-start | bytes 393220
  53.4 13.8 %copy-start.12 = (f32[4096]{0:T(1024)S(1)}, f32[4096]{0:T(1024)}, u32[]{:S(2)}) copy-start(f32[4096]{0:T(1024)} %param.23) | copy-start | bytes 49156
  53.4 6.4 %collective-permute-start.2 = (f32[8,4224]{1,0:T(8,128)S(1)}, f32[8,4224]{1,0:T(8,128)S(1)}, u32[]{:S(2)}, u32[]{:S(2)}) collective-permute-start(f32[8,4224]{1,0:T(8,128)S(1)} %transpose.4._), channel_id=1, source_target_pairs={{0,192},{32,224},{64,128},{96,160},{128,64},{160,96},{192,0},{224,... | collective-permute-start | bytes 405512 | tf_op jit(solution)/shard_map/ppermute | solution.py:546
  56.3 5.5 %collective-permute-start.1 = (f32[8,4224]{1,0:T(8,128)S(1)}, f32[8,4224]{1,0:T(8,128)S(1)}, u32[]{:S(2)}, u32[]{:S(2)}) collective-permute-start(f32[8,4224]{1,0:T(8,128)S(1)} %transpose.4._), channel_id=1, source_target_pairs={{0,128},{32,160},{64,192},{96,224},{128,0},{160,32},{192,64},{224,... | collective-permute-start | bytes 405512 | tf_op jit(solution)/shard_map/ppermute | solution.py:546
  56.6 5.1 %collective-permute-start = (f32[8,4224]{1,0:T(8,128)S(1)}, f32[8,4224]{1,0:T(8,128)S(1)}, u32[]{:S(2)}, u32[]{:S(2)}) collective-permute-start(f32[8,4224]{1,0:T(8,128)S(1)} %transpose.4._), channel_id=1, source_target_pairs={{0,64},{32,96},{64,0},{96,32},{128,192},{160,224},{192,128},{224,1... | collective-permute-start | bytes 405512 | tf_op jit(solution)/shard_map/ppermute | solution.py:546
  61.8 5.5 %collective-permute-start.3 = (f32[8,4224]{1,0:T(8,128)S(1)}, f32[8,4224]{1,0:T(8,128)S(1)}, u32[]{:S(2)}, u32[]{:S(2)}) collective-permute-start(f32[8,4224]{1,0:T(8,128)S(1)} %add_add_fusion.own), channel_id=1, source_target_pairs={{0,32},{32,0},{64,96},{96,64},{128,160},{160,128},{192,224},{224,1... | collective-permute-start | bytes 405512 | tf_op jit(solution)/shard_map/ppermute | solution.py:546
  65.7 25.0 %copy-start.4 = (f32[8,4096]{1,0:T(8,128)S(1)}, f32[8,4096]{1,0:T(8,128)}, u32[]{:S(2)}) copy-start(f32[8,4096]{1,0:T(8,128)} %qgx.3) | copy-start | bytes 393220
  65.7 25.0 %copy-start.8 = (f32[8,2048]{1,0:T(8,128)S(1)}, f32[8,2048]{1,0:T(8,128)}, u32[]{:S(2)}) copy-start(f32[8,2048]{1,0:T(8,128)} %qgw.3) | copy-start | bytes 196612
  65.7 25.0 %copy-start.10 = (f32[8,4096]{1,0:T(8,128)S(1)}, f32[8,4096]{1,0:T(8,128)}, u32[]{:S(2)}) copy-start(f32[8,4096]{1,0:T(8,128)} %refs_5_.4) | copy-start | bytes 393220
  65.7 25.0 %copy-start.13 = (f32[8,2048]{1,0:T(8,128)S(1)}, f32[8,2048]{1,0:T(8,128)}, u32[]{:S(2)}) copy-start(f32[8,2048]{1,0:T(8,128)} %refs_10_.2) | copy-start | bytes 196612
  67.2 47.0 %copy-start.16 = (s32[8]{0:T(128)S(1)}, s32[8]{0:T(128)}, u32[]{:S(2)}) copy-start(s32[8]{0:T(128)} %refs_2_.7) | copy-start | bytes 100
  67.2 47.0 %copy-start.17 = (s32[8]{0:T(128)S(1)}, s32[8]{0:T(128)}, u32[]{:S(2)}) copy-start(s32[8]{0:T(128)} %refs_3_.7) | copy-start | bytes 100
  91.7 2.9 %collective-permute-start.4 = (f32[2,128]{1,0:T(2,128)S(1)}, f32[2,128]{1,0:T(2,128)S(1)}, u32[]{:S(2)}, u32[]{:S(2)}) collective-permute-start(f32[2,128]{1,0:T(2,128)S(1)} %get-tuple-element.41), channel_id=1, source_target_pairs={{0,1},{1,0},{2,3},{3,2},{4,5},{5,4},{6,7},{7,6},{8,9},{9,8},{10,11... | collective-permute-start | bytes 3080 | tf_op jit(solution)/shard_map/ppermute | solution.py:641
  155.7 7.1 %collective-permute-start.7 = (f32[8,4096]{1,0:T(8,128)S(1)}, f32[8,4096]{1,0:T(8,128)S(1)}, u32[]{:S(2)}, u32[]{:S(2)}) collective-permute-start(f32[8,4096]{1,0:T(8,128)S(1)} %transpose.5), channel_id=1, source_target_pairs={{0,192},{32,224},{64,128},{96,160},{128,64},{160,96},{192,0},{224,... | collective-permute-start | bytes 393224 | tf_op jit(solution)/shard_map/ppermute | solution.py:546
  156.1 6.6 %collective-permute-start.6 = (f32[8,4096]{1,0:T(8,128)S(1)}, f32[8,4096]{1,0:T(8,128)S(1)}, u32[]{:S(2)}, u32[]{:S(2)}) collective-permute-start(f32[8,4096]{1,0:T(8,128)S(1)} %transpose.5), channel_id=1, source_target_pairs={{0,128},{32,160},{64,192},{96,224},{128,0},{160,32},{192,64},{224,... | collective-permute-start | bytes 393224 | tf_op jit(solution)/shard_map/ppermute | solution.py:546
  157.3 5.8 %collective-permute-start.5 = (f32[8,4096]{1,0:T(8,128)S(1)}, f32[8,4096]{1,0:T(8,128)S(1)}, u32[]{:S(2)}, u32[]{:S(2)}) collective-permute-start(f32[8,4096]{1,0:T(8,128)S(1)} %transpose.5), channel_id=1, source_target_pairs={{0,64},{32,96},{64,0},{96,32},{128,192},{160,224},{192,128},{224,1... | collective-permute-start | bytes 393224 | tf_op jit(solution)/shard_map/ppermute | solution.py:546
  163.2 5.4 %collective-permute-start.8 = (f32[8,4096]{1,0:T(8,128)S(1)}, f32[8,4096]{1,0:T(8,128)S(1)}, u32[]{:S(2)}, u32[]{:S(2)}) collective-permute-start(f32[8,4096]{1,0:T(8,128)S(1)} %add_add_fusion.1.own), channel_id=1, source_target_pairs={{0,32},{32,0},{64,96},{96,64},{128,160},{160,128},{192,224},{224,1... | collective-permute-start | bytes 393224 | tf_op jit(solution)/shard_map/ppermute | solution.py:546
  193.0 2.9 %collective-permute-start.9 = (f32[2,128]{1,0:T(2,128)S(1)}, f32[2,128]{1,0:T(2,128)S(1)}, u32[]{:S(2)}, u32[]{:S(2)}) collective-permute-start(f32[2,128]{1,0:T(2,128)S(1)} %get-tuple-element.55), channel_id=1, source_target_pairs={{0,1},{1,0},{2,3},{3,2},{4,5},{5,4},{6,7},{7,6},{8,9},{9,8},{10,11... | collective-permute-start | bytes 3080 | tf_op jit(solution)/shard_map/ppermute | solution.py:641

commit v10 on v7

--- a/solution.py
+++ b/solution.py
@@ -544,11 +544,11 @@
         def partner(x, k):
             return lax.ppermute(x, "con", [(i, i ^ k) for i in range(con_count)])
 
-        others = [partner(x, k) for k in range(2, con_count, 2)]
-        terms = [x] + others
-        while len(terms) > 1:
+        pair = x + partner(x, 1)
+        terms = [pair] + [partner(pair, k) for k in range(2, con_count, 2)]
+        while len(terms) > 2:
             terms = [a + b for a, b in zip(terms[::2], terms[1::2])]
-        return terms[0], partner(terms[0], 1)
+        return terms
 
     one_core = [list(range(k, con_count * var_count, 2)) for k in range(2)]
     share = col_count // con_count

time: 215 us -> 214 us (level)
  transfers between devices with their start and end apart: 10 -> 10, of which waited for: 8 -> 9; matrix products, arithmetic and copies ran while one was open for 0% -> 0% of each run, Pallas kernels for 1% -> 1%
where the time goes in v10:
time: 214 us
  blocking collectives  163 us (76%)
  Pallas kernels  18.8 us (9%)
  waiting for transfers between devices  15.5 us (7%)
  starting transfers between devices  15.2 us (7%)
    all_to_all x6, blocking collectives, exchange(): return lax.all_to_all(x, 'var', 0, 0, tiled=True)  127 us
    all_to_all x2, blocking collectives, per_device(): lax.all_to_all(copies, ('con', 'var'), 0, 0, tiled=True, axis_index_group...  36.3 us
    pallas_call x12, Pallas kernels, call(): pl.pallas_call(kernel, out_shape=[jax.ShapeDtypeStruct(shape, dtype) for...  18.8 us
    ppermute x8, waiting for transfers between devices, partner(): return lax.ppermute(x, 'con', [(i, i ^ k) for i in range(con_count)])  13.8 us
    ppermute x8, starting transfers between devices, partner(): return lax.ppermute(x, 'con', [(i, i ^ k) for i in range(con_count)])  11 us
  transfers between devices with their start and end apart: 10, of which 9 were waited for; matrix products, arithmetic and copies ran while one was open for 0% of the time, Pallas kernels for 1%

profile of v10, /device:TPU:1, one launch (start us, length us, event | category | flops | bytes accessed | tf_op | source)
XLA Modules:
  0.0 214.0 jit_solution(12941985226274386851)
XLA Ops:
  0.7 4.1 %open.1 = (f32[224,4,128]{2,1,0:T(4,128)S(1)}, s32[72]{0:T(128)S(1)}, f32[72,128,128]{2,1,0:T(8,128)S(1)}) custom-call(s32[1,72]{1,0:T(1,128)} %bitcast.21, s32[1,72]{1,0:T(1,128)} %bitcast.14, f32[8,4096]{1,0:T(8,128)} %refs_5_.5, f32[72,128,128]{2,1,0:T(8,128)} %bitcast.20, f32[8,4096]{1,0:T(8,128)} %qgx.3, f32[8,2048]{1,0:T(8,128)} %qgw.3, ...), custom_call_target="tpu_custom_call" | custom-call | tf_op jit(solution)/shard_map/open/pallas_call | solution.py:481
  4.8 26.5 %all_to_all.40.refs_0_ = f32[224,4,128]{2,1,0:T(4,128)S(1)} all-to-all(f32[224,4,128]{2,1,0:T(4,128)S(1)} %get-tuple-element.31), channel_id=1, replica_groups=mesh['con'=8,'var'=32] {'var'}, dimensions={0} | all-to-all | bytes 917504 | tf_op jit(solution)/shard_map/all_to_all | solution.py:541
  31.3 1.6 penalty_first.1
  32.9 18.9 %all_to_all.41.refs_0_ = f32[96,8,128]{2,1,0:T(8,128)S(1)} all-to-all(f32[96,8,128]{2,1,0:T(8,128)S(1)} %get-tuple-element.32), channel_id=1, replica_groups=mesh['con'=8,'var'=32] {'var'}, dimensions={0} | all-to-all | bytes 786432 | tf_op jit(solution)/shard_map/all_to_all | solution.py:541
  51.8 1.3 transpose.4._
  53.2 2.5 %collective-permute-start = (f32[8,4224]{1,0:T(8,128)S(1)}, f32[8,4224]{1,0:T(8,128)S(1)}, u32[]{:S(2)}, u32[]{:S(2)}) collective-permute-start(f32[8,4224]{1,0:T(8,128)S(1)} %transpose.4._), channel_id=1, source_target_pairs={{0,32},{32,0},{64,96},{96,64},{128,160},{160,128},{192,224},{224,1... | collective-permute-start | bytes 405512 | tf_op jit(solution)/shard_map/ppermute | solution.py:545
  55.7 2.9 %collective-permute-done = f32[8,4224]{1,0:T(8,128)S(1)} collective-permute-done((f32[8,4224]{1,0:T(8,128)S(1)}, f32[8,4224]{1,0:T(8,128)S(1)}, u32[]{:S(2)}, u32[]{:S(2)}) %collective-permute-start) | collective-permute-done | bytes 135200 | tf_op jit(solution)/shard_map/ppermute | solution.py:545
  58.6 1.4 collective-permute-start.1
  60.0 1.9 collective-permute-start.3
  62.6 1.4 prepare.1
  64.1 1.0 collective-permute-done.3
  65.1 2.2 %collective-permute-done.2 = f32[8,4224]{1,0:T(8,128)S(1)} collective-permute-done((f32[8,4224]{1,0:T(8,128)S(1)}, f32[8,4224]{1,0:T(8,128)S(1)}, u32[]{:S(2)}, u32[]{:S(2)}) %collective-permute-start.2) | collective-permute-done | bytes 135200 | tf_op jit(solution)/shard_map/ppermute | solution.py:545
  67.4 1.4 residual.2
  68.7 22.0 %all_to_all.42.got = f32[96,8,128]{2,1,0:T(8,128)S(1)} all-to-all(f32[96,8,128]{2,1,0:T(8,128)S(1)} %get-tuple-element.37), channel_id=1, replica_groups=mesh['con'=8,'var'=32] {'var'}, dimensions={0} | all-to-all | bytes 786432 | tf_op jit(solution)/shard_map/all_to_all | solution.py:541
  90.8 1.0 scalars.2
  91.8 2.1 collective-permute-start.4
  94.8 18.9 %all_to_all.43.refs_0_ = f32[128,2,128]{2,1,0:T(2,128)S(1)} all-to-all(f32[128,2,128]{2,1,0:T(2,128)S(1)} %broadcast_in_dim.4), channel_id=1, replica_groups={{0,2,4,6,8,10,12,14,16,18,20,22,24,26,28,30,32,34,36,38,40,42,44,46,48,..., dimensions={0} | all-to-all | bytes 262144 | tf_op jit(solution)/shard_map/all_to_all | solution.py:642
  113.7 1.9 update.2
  115.6 18.5 %all_to_all.44.refs_0_ = f32[96,8,128]{2,1,0:T(8,128)S(1)} all-to-all(f32[96,8,128]{2,1,0:T(8,128)S(1)} %get-tuple-element.46), channel_id=1, replica_groups=mesh['con'=8,'var'=32] {'var'}, dimensions={0} | all-to-all | bytes 786432 | tf_op jit(solution)/shard_map/all_to_all | solution.py:541
  134.9 18.9 %all_to_all.45.refs_0_ = f32[96,8,128]{2,1,0:T(8,128)S(1)} all-to-all(f32[96,8,128]{2,1,0:T(8,128)S(1)} %get-tuple-element.48), channel_id=1, replica_groups=mesh['con'=8,'var'=32] {'var'}, dimensions={0} | all-to-all | bytes 786432 | tf_op jit(solution)/shard_map/all_to_all | solution.py:541
  153.8 1.3 transpose.5
  155.1 1.1 collective-permute-start.5
  156.2 4.3 %collective-permute-done.5 = f32[8,4096]{1,0:T(8,128)S(1)} collective-permute-done((f32[8,4096]{1,0:T(8,128)S(1)}, f32[8,4096]{1,0:T(8,128)S(1)}, u32[]{:S(2)}, u32[]{:S(2)}) %collective-permute-start.5) | collective-permute-done | bytes 131104 | tf_op jit(solution)/shard_map/ppermute | solution.py:545
  160.6 1.0 collective-permute-start.8
  161.6 2.2 %collective-permute-start.7 = (f32[8,4096]{1,0:T(8,128)S(1)}, f32[8,4096]{1,0:T(8,128)S(1)}, u32[]{:S(2)}, u32[]{:S(2)}) collective-permute-start(f32[8,4096]{1,0:T(8,128)S(1)} %add.28), channel_id=1, source_target_pairs={{0,128},{32,160},{64,192},{96,224},{128,0},{160,32},{192,64},{224,... | collective-permute-start | bytes 393224 | tf_op jit(solution)/shard_map/ppermute | solution.py:545
  164.4 2.5 %collective-permute-done.8 = f32[8,4096]{1,0:T(8,128)S(1)} collective-permute-done((f32[8,4096]{1,0:T(8,128)S(1)}, f32[8,4096]{1,0:T(8,128)S(1)}, u32[]{:S(2)}, u32[]{:S(2)}) %collective-permute-start.8) | collective-permute-done | bytes 131104 | tf_op jit(solution)/shard_map/ppermute | solution.py:545
  167.3 1.4 residual.3
  168.7 22.2 %all_to_all.46.got = f32[96,8,128]{2,1,0:T(8,128)S(1)} all-to-all(f32[96,8,128]{2,1,0:T(8,128)S(1)} %get-tuple-element.50), channel_id=1, replica_groups=mesh['con'=8,'var'=32] {'var'}, dimensions={0} | all-to-all | bytes 786432 | tf_op jit(solution)/shard_map/all_to_all | solution.py:541
  190.9 1.0 scalars.3
  191.8 2.1 collective-permute-start.9
  194.8 17.4 %all_to_all.47.refs_0_ = f32[128,2,128]{2,1,0:T(2,128)S(1)} all-to-all(f32[128,2,128]{2,1,0:T(2,128)S(1)} %broadcast_in_dim.5), channel_id=1, replica_groups={{0,2,4,6,8,10,12,14,16,18,20,22,24,26,28,30,32,34,36,38,40,42,44,46,48,..., dimensions={0} | all-to-all | bytes 262144 | tf_op jit(solution)/shard_map/all_to_all | solution.py:642
  212.3 1.8 update.3
  (54 shorter events, 4.4 us)
Async XLA Ops:
  0.6 30.7 %copy-start.6 = (f32[8,2048]{1,0:T(8,128)S(1)}, f32[8,2048]{1,0:T(8,128)}, u32[]{:S(2)}) copy-start(f32[8,2048]{1,0:T(8,128)} %refs_15_.3) | copy-start | bytes 196612
  0.6 30.7 %copy-start.5 = (f32[8,2048]{1,0:T(8,128)S(1)}, f32[8,2048]{1,0:T(8,128)}, u32[]{:S(2)}) copy-start(f32[8,2048]{1,0:T(8,128)} %refs_14_.3) | copy-start | bytes 196612
  0.7 30.6 %copy-start.9 = (f32[8,2048]{1,0:T(8,128)S(1)}, f32[8,2048]{1,0:T(8,128)}, u32[]{:S(2)}) copy-start(f32[8,2048]{1,0:T(8,128)} %refs_10_.3) | copy-start | bytes 196612
  0.7 30.6 %copy-start.14 = (s32[2048]{0:T(1024)S(1)}, s32[2048]{0:T(1024)}, u32[]{:S(2)}) copy-start(s32[2048]{0:T(1024)} %param.27) | copy-start | bytes 24580
  0.7 51.1 %copy-start.15 = (s32[1,1,72]{2,1,0:T(1,128)S(1)}, s32[1,1,72]{2,1,0:T(1,128)}, u32[]{:S(2)}) copy-start(s32[1,1,72]{2,1,0:T(1,128)} %param.22) | copy-start | bytes 868
  4.8 57.9 %copy-start = (f32[8,8,4096]{2,1,0:T(8,128)S(1)}, f32[8,8,4096]{2,1,0:T(8,128)}, u32[]{:S(2)}) copy-start(f32[8,8,4096]{2,1,0:T(8,128)} %hgx.5) | copy-start | bytes 3145732
  4.8 57.8 %copy-start.1 = (f32[8,8,2048]{2,1,0:T(8,128)S(1)}, f32[8,8,2048]{2,1,0:T(8,128)}, u32[]{:S(2)}) copy-start(f32[8,8,2048]{2,1,0:T(8,128)} %hgw.5) | copy-start | bytes 1572868
  4.8 57.8 %copy-start.3 = (f32[8,8,4096]{2,1,0:T(8,128)S(1)}, f32[8,8,4096]{2,1,0:T(8,128)}, u32[]{:S(2)}) copy-start(f32[8,8,4096]{2,1,0:T(8,128)} %hsx.1) | copy-start | bytes 3145732
  4.8 57.8 %copy-start.7 = (f32[8,8,2048]{2,1,0:T(8,128)S(1)}, f32[8,8,2048]{2,1,0:T(8,128)}, u32[]{:S(2)}) copy-start(f32[8,8,2048]{2,1,0:T(8,128)} %hsw.1) | copy-start | bytes 1572868
  53.1 14.2 %copy-start.2 = (f32[8,4096]{1,0:T(8,128)S(1)}, f32[8,4096]{1,0:T(8,128)}, u32[]{:S(2)}) copy-start(f32[8,4096]{1,0:T(8,128)} %refs_5_.5) | copy-start | bytes 393220
  53.1 14.2 %copy-start.11 = (f32[8,4096]{1,0:T(8,128)S(1)}, f32[8,4096]{1,0:T(8,128)}, u32[]{:S(2)}) copy-start(f32[8,4096]{1,0:T(8,128)} %linear.3) | copy-start | bytes 393220
  53.1 14.2 %copy-start.12 = (f32[4096]{0:T(1024)S(1)}, f32[4096]{0:T(1024)}, u32[]{:S(2)}) copy-start(f32[4096]{0:T(1024)} %param.23) | copy-start | bytes 49156
  53.2 5.5 %collective-permute-start = (f32[8,4224]{1,0:T(8,128)S(1)}, f32[8,4224]{1,0:T(8,128)S(1)}, u32[]{:S(2)}, u32[]{:S(2)}) collective-permute-start(f32[8,4224]{1,0:T(8,128)S(1)} %transpose.4._), channel_id=1, source_target_pairs={{0,32},{32,0},{64,96},{96,64},{128,160},{160,128},{192,224},{224,1... | collective-permute-start | bytes 405512 | tf_op jit(solution)/shard_map/ppermute | solution.py:545
  58.6 5.4 %collective-permute-start.1 = (f32[8,4224]{1,0:T(8,128)S(1)}, f32[8,4224]{1,0:T(8,128)S(1)}, u32[]{:S(2)}, u32[]{:S(2)}) collective-permute-start(f32[8,4224]{1,0:T(8,128)S(1)} %add.24), channel_id=1, source_target_pairs={{0,64},{32,96},{64,0},{96,32},{128,192},{160,224},{192,128},{224,1... | collective-permute-start | bytes 405512 | tf_op jit(solution)/shard_map/ppermute | solution.py:545
  60.0 5.1 %collective-permute-start.3 = (f32[8,4224]{1,0:T(8,128)S(1)}, f32[8,4224]{1,0:T(8,128)S(1)}, u32[]{:S(2)}, u32[]{:S(2)}) collective-permute-start(f32[8,4224]{1,0:T(8,128)S(1)} %add.24), channel_id=1, source_target_pairs={{0,192},{32,224},{64,128},{96,160},{128,64},{160,96},{192,0},{224,... | collective-permute-start | bytes 405512 | tf_op jit(solution)/shard_map/ppermute | solution.py:545
  61.9 5.4 %collective-permute-start.2 = (f32[8,4224]{1,0:T(8,128)S(1)}, f32[8,4224]{1,0:T(8,128)S(1)}, u32[]{:S(2)}, u32[]{:S(2)}) collective-permute-start(f32[8,4224]{1,0:T(8,128)S(1)} %add.24), channel_id=1, source_target_pairs={{0,128},{32,160},{64,192},{96,224},{128,0},{160,32},{192,64},{224,... | collective-permute-start | bytes 405512 | tf_op jit(solution)/shard_map/ppermute | solution.py:545
  64.0 26.7 %copy-start.4 = (f32[8,4096]{1,0:T(8,128)S(1)}, f32[8,4096]{1,0:T(8,128)}, u32[]{:S(2)}) copy-start(f32[8,4096]{1,0:T(8,128)} %qgx.3) | copy-start | bytes 393220
  64.0 26.7 %copy-start.8 = (f32[8,2048]{1,0:T(8,128)S(1)}, f32[8,2048]{1,0:T(8,128)}, u32[]{:S(2)}) copy-start(f32[8,2048]{1,0:T(8,128)} %qgw.3) | copy-start | bytes 196612
  64.1 26.7 %copy-start.10 = (f32[8,4096]{1,0:T(8,128)S(1)}, f32[8,4096]{1,0:T(8,128)}, u32[]{:S(2)}) copy-start(f32[8,4096]{1,0:T(8,128)} %refs_5_.4) | copy-start | bytes 393220
  64.1 26.7 %copy-start.13 = (f32[8,2048]{1,0:T(8,128)S(1)}, f32[8,2048]{1,0:T(8,128)}, u32[]{:S(2)}) copy-start(f32[8,2048]{1,0:T(8,128)} %refs_10_.2) | copy-start | bytes 196612
  67.3 46.3 %copy-start.16 = (s32[8]{0:T(128)S(1)}, s32[8]{0:T(128)}, u32[]{:S(2)}) copy-start(s32[8]{0:T(128)} %refs_2_.7) | copy-start | bytes 100
  67.3 46.3 %copy-start.17 = (s32[8]{0:T(128)S(1)}, s32[8]{0:T(128)}, u32[]{:S(2)}) copy-start(s32[8]{0:T(128)} %refs_3_.7) | copy-start | bytes 100
  91.8 2.9 %collective-permute-start.4 = (f32[2,128]{1,0:T(2,128)S(1)}, f32[2,128]{1,0:T(2,128)S(1)}, u32[]{:S(2)}, u32[]{:S(2)}) collective-permute-start(f32[2,128]{1,0:T(2,128)S(1)} %get-tuple-element.41), channel_id=1, source_target_pairs={{0,1},{1,0},{2,3},{3,2},{4,5},{5,4},{6,7},{7,6},{8,9},{9,8},{10,11... | collective-permute-start | bytes 3080 | tf_op jit(solution)/shard_map/ppermute | solution.py:640
  155.1 5.4 %collective-permute-start.5 = (f32[8,4096]{1,0:T(8,128)S(1)}, f32[8,4096]{1,0:T(8,128)S(1)}, u32[]{:S(2)}, u32[]{:S(2)}) collective-permute-start(f32[8,4096]{1,0:T(8,128)S(1)} %transpose.5), channel_id=1, source_target_pairs={{0,32},{32,0},{64,96},{96,64},{128,160},{160,128},{192,224},{224,1... | collective-permute-start | bytes 393224 | tf_op jit(solution)/shard_map/ppermute | solution.py:545
  160.5 3.9 %collective-permute-start.6 = (f32[8,4096]{1,0:T(8,128)S(1)}, f32[8,4096]{1,0:T(8,128)S(1)}, u32[]{:S(2)}, u32[]{:S(2)}) collective-permute-start(f32[8,4096]{1,0:T(8,128)S(1)} %add.28), channel_id=1, source_target_pairs={{0,64},{32,96},{64,0},{96,32},{128,192},{160,224},{192,128},{224,1... | collective-permute-start | bytes 393224 | tf_op jit(solution)/shard_map/ppermute | solution.py:545
  160.6 6.3 %collective-permute-start.8 = (f32[8,4096]{1,0:T(8,128)S(1)}, f32[8,4096]{1,0:T(8,128)S(1)}, u32[]{:S(2)}, u32[]{:S(2)}) collective-permute-start(f32[8,4096]{1,0:T(8,128)S(1)} %add.28), channel_id=1, source_target_pairs={{0,192},{32,224},{64,128},{96,160},{128,64},{160,96},{192,0},{224,... | collective-permute-start | bytes 393224 | tf_op jit(solution)/shard_map/ppermute | solution.py:545
  161.6 5.6 %collective-permute-start.7 = (f32[8,4096]{1,0:T(8,128)S(1)}, f32[8,4096]{1,0:T(8,128)S(1)}, u32[]{:S(2)}, u32[]{:S(2)}) collective-permute-start(f32[8,4096]{1,0:T(8,128)S(1)} %add.28), channel_id=1, source_target_pairs={{0,128},{32,160},{64,192},{96,224},{128,0},{160,32},{192,64},{224,... | collective-permute-start | bytes 393224 | tf_op jit(solution)/shard_map/ppermute | solution.py:545
  191.8 2.9 %collective-permute-start.9 = (f32[2,128]{1,0:T(2,128)S(1)}, f32[2,128]{1,0:T(2,128)S(1)}, u32[]{:S(2)}, u32[]{:S(2)}) collective-permute-start(f32[2,128]{1,0:T(2,128)S(1)} %get-tuple-element.55), channel_id=1, source_target_pairs={{0,1},{1,0},{2,3},{3,2},{4,5},{5,4},{6,7},{7,6},{8,9},{9,8},{10,11... | collective-permute-start | bytes 3080 | tf_op jit(solution)/shard_map/ppermute | solution.py:640
